TPU v7x, 32 devices: a whole 2x2x4 slice. The times are simulated.
32 devices in a mesh: groups: 2 (over y), ctx: 4 (over z), head: 2 (over x), sub: 2 (over core).
Axes of the slice: x: 2, y: 2, z: 4, core: 2. Of those that a mesh axis runs over, the one named last changes fastest.
Arguments:
- queries: bfloat16 [2048, 64, 128], P(('groups', 'ctx', 'sub'), 'head'), parts along dimension 0, may hold values from -6 to 6
- keys: bfloat16 [2048, 4, 128], P(('groups', 'ctx', 'sub'), 'head'), parts along dimension 0, may hold values from -6 to 6
- values: bfloat16 [2048, 4, 128], P(('groups', 'ctx', 'sub'), 'head'), parts along dimension 0, may hold values from -6 to 6
- grad_out: bfloat16 [2048, 64, 128], P(('groups', 'ctx', 'sub'), 'head'), parts along dimension 0, may hold values from -9 to 9
- row_lse: float32 [2048, 64], P(('groups', 'ctx', 'sub'), 'head'), parts along dimension 0, may hold values from 5.5 to 6.5
- row_delta: float32 [2048, 64], P(('groups', 'ctx', 'sub'), 'head'), parts along dimension 0, may hold values from -24 to 24
- doc_ids: int32 [2048], P(('groups', 'ctx', 'sub')), parts along dimension 0, may hold values from 0 to 3, never falling along the last dimension, each value on 1 to 512 neighbouring positions
- pairs: int32 [16, 2], P('groups'), parts along dimension 0, may hold values from 0 to 7, as said below
Outputs:
- grad_queries: float32 [2048, 64, 128], P(('groups', 'ctx', 'sub'), 'head'), parts along dimension 0
- grad_keys: float32 [2048, 4, 128], P(('groups', 'ctx', 'sub'), 'head'), parts along dimension 0
- grad_values: float32 [2048, 4, 128], P(('groups', 'ctx', 'sub'), 'head'), parts along dimension 0
There are 2 independent parts, one for each index of `groups`. A program takes and returns all parts, laid end to end along the dimension named above; each array names one. Nothing has to cross between parts.
Inputs may be any that keep to these rules, and one draw needn't show every extreme that they name: `pairs`: row c holds two different span indices, neither equal to c. `doc_ids`: never falls along the tokens; every document appears.
All inputs are finite; a program needn't handle non-finite values.
Results may differ from a plain program's by a relative error of at most 0.0046.
Values may be sent and summed in bfloat16 or wider, within the bound.
No kernel may reach another device: no remote copies, remote signals or barrier semaphores. Data moves between devices by JAX's collectives and lax.ppermute only.
A program may use at most 64 MiB of HBM per device.

v0:
```python
import functools

import jax
import jax.numpy as jnp
from jax import lax
from jax.experimental import pallas as pl
from jax.experimental.pallas import tpu as pltpu
from jax.sharding import PartitionSpec as P

QH = 64
KVH = 4
LOG2E = 1.4426950408889634
ROWS = 512
PARTS = 1
VMEM_LIMIT = 24 * 1024 * 1024

VMEM_SPEC = pl.BlockSpec(memory_space=pltpu.VMEM)
ANY_SPEC = pl.BlockSpec(memory_space=pl.ANY)
HBM_SPEC = pl.BlockSpec(memory_space=pltpu.HBM)


def rows_dot(left, right):
    return lax.dot_general(left, right, (((1,), (1,)), ((), ())), preferred_element_type=jnp.float32)


def tile_terms(key_blk, value_blk, query_blk, upstream, log_norm, row_terms, allowed, factor):
    scores = rows_dot(key_blk, query_blk)
    probs = jnp.exp2(scores * (factor * LOG2E) - log_norm)
    if allowed is not None:
        probs = jnp.where(allowed, probs, 0.0)
    grad_probs = rows_dot(value_blk, upstream)
    grad_scores = probs * (grad_probs - row_terms)
    return probs.astype(jnp.bfloat16), grad_scores.astype(jnp.bfloat16)


def chunks(tokens, grouped, rows):
    step = rows // grouped
    return [(i, slice(i * step, (i + 1) * step), slice(i * rows, (i + 1) * rows)) for i in range(tokens // step)]


def start_all(sources, targets, sems):
    copies = [pltpu.make_async_copy(source, target, sems.at[i]) for i, (source, target) in enumerate(zip(sources, targets))]
    for copy in copies:
        copy.start()
    return copies


class Rows:
    def __init__(self, query_ref, up_ref, held_ref, sems, first, rows):
        _, self.count, tokens, self.grouped, self.head_dim = held_ref.shape
        self.held, self.rows = held_ref, rows
        self.steps = chunks(tokens, self.grouped, rows)
        self.copies = {}
        for head in range(self.count):
            heads = slice((first + head) * self.grouped, (first + head + 1) * self.grouped)
            for i, toks, _ in self.steps:
                for kind, ref in enumerate((query_ref, up_ref)):
                    copy = pltpu.make_async_copy(
                        ref.at[toks, heads], held_ref.at[kind, head, toks], sems.at[head, i, kind]
                    )
                    copy.start()
                    self.copies[head, i, kind] = copy

    def blocks(self, head):
        for i, toks, cols in self.steps:
            pair = []
            for kind in range(2):
                self.copies[head, i, kind].wait()
                pair.append(self.held[kind, head, toks].reshape(self.rows, self.head_dim))
            yield toks, cols, *pair


def pack_kernel(key_ref, value_ref, *refs):
    *kv_refs, held_ref, sems = refs
    each = kv_refs[0].shape[1]
    copies = start_all((key_ref, value_ref), (held_ref.at[0], held_ref.at[1]), sems)
    for kind, copy in enumerate(copies):
        copy.wait()
        for head in range(held_ref.shape[2]):
            kv_refs[head // each][kind, head % each] = held_ref[kind, :, head, :]


def spread_kernel(
    grouped, ring, subs, norm_ref, term_ref, docs_ref, pairs_ref,
    norm_row_ref, term_row_ref, docs_row_ref, doc_col_ref, places_ref,
    held_ref, held_docs, held_pairs, sems,
):
    _, heads, tokens = held_ref.shape
    copies = start_all(
        (pairs_ref, docs_ref, norm_ref, term_ref), (held_pairs, held_docs, held_ref.at[0], held_ref.at[1]), sems
    )
    cols = tokens * grouped
    column = lax.broadcasted_iota(jnp.int32, (tokens, cols), 1)
    token = lax.broadcasted_iota(jnp.int32, (tokens, cols), 0)
    pick = jnp.where(token == column // grouped, 1.0, 0.0).astype(jnp.bfloat16)
    keep = lax.broadcasted_iota(jnp.int32, (grouped, cols), 0) == (
        lax.broadcasted_iota(jnp.int32, (grouped, cols), 1) % grouped
    )
    for copy in copies:
        copy.wait()

    ctx, sub = lax.axis_index("ctx"), lax.axis_index("sub")
    pairs = held_pairs[...]
    lane = lax.broadcasted_iota(jnp.int32, pairs.shape, 1)

    def listed_by(core):
        mask = lane == ctx * subs + core
        span = jnp.sum(jnp.where(mask, pairs, 0).astype(jnp.float32), axis=1, keepdims=True)
        span = jnp.broadcast_to(span, (2, places_ref.shape[1])).astype(jnp.int32)
        return span // subs, span % subs

    def around(gap):
        return jnp.where(gap < 0, gap + ring, gap)

    (mine, mine_sub), (other, other_sub) = listed_by(sub), listed_by(1 - sub)
    places_ref[0:2] = around(ctx - other)
    places_ref[2:4] = jnp.where(mine_sub == sub, around(ctx - mine), ring)
    places_ref[4:6] = jnp.where(mine_sub == sub, around(mine - ctx), ring)
    places_ref[6:8] = jnp.where(other_sub == sub, around(other - ctx), ring)

    pieces = []
    for value in (held_ref[0] * LOG2E, held_ref[1]):
        for _ in range(3):
            piece = value.astype(jnp.bfloat16)
            value = value - piece.astype(jnp.float32)
            pieces.append(piece)
    docs = held_docs[...].astype(jnp.float32)
    pieces.append(jnp.broadcast_to(docs, (grouped, tokens)).astype(jnp.bfloat16))
    spread = jnp.dot(jnp.concatenate(pieces, axis=0), pick, preferred_element_type=jnp.float32)
    for i, out_ref in enumerate((norm_row_ref, term_row_ref)):
        base = 3 * i * heads
        value = spread[base:base + heads] + spread[base + heads:base + 2 * heads]
        value = value + spread[base + 2 * heads:base + 3 * heads]
        for head in range(out_ref.shape[0]):
            group = value[head * grouped:(head + 1) * grouped]
            out_ref[head] = jnp.sum(jnp.where(keep, group, 0.0), axis=0, keepdims=True)
    docs_row_ref[...] = spread[6 * heads:6 * heads + 1]
    doc_col_ref[...] = jnp.broadcast_to(docs, (tokens, tokens)).T


def pick_block(sources, row):
    chosen = sources[0].astype(jnp.float32)
    for step in range(1, len(sources)):
        chosen = jnp.where(row == step, sources[step].astype(jnp.float32), chosen)
    return chosen.astype(jnp.bfloat16)


def choose_kernel(places_ref, *refs):
    *column, _, _, out_ref = refs
    for which in range(2):
        row = places_ref[which:which + 1]
        for kind in range(2):
            for head in range(out_ref.shape[2]):
                out_ref[which, kind, head] = pick_block([ref[kind, head] for ref in column], row)


def far_blocks(places_ref, column, other_ref, head):
    return [
        jnp.concatenate(
            [
                pick_block(
                    [ref[kind, head] for ref in column] + [other_ref[which, kind, head]],
                    places_ref[2 + which:3 + which],
                )
                for which in range(2)
            ],
            axis=0,
        )
        for kind in range(2)
    ]


def local_kernel(factor, rows, *refs):
    *kv_refs, query_ref, up_ref, norm_ref, term_ref, docs_ref, doc_col_ref, dkv_ref, dq_ref, held_ref, sems = refs
    source = Rows(query_ref, up_ref, held_ref, sems, 0, rows)
    tokens, grouped, head_dim = held_ref.shape[2:]
    each = kv_refs[0].shape[1]
    doc_col = jnp.concatenate([doc_col_ref[...]] * (rows // tokens), axis=1)
    for head in range(source.count):
        key_blk, value_blk = kv_refs[head // each][0, head % each], kv_refs[head // each][1, head % each]
        grad_key = jnp.zeros((tokens, head_dim), jnp.float32)
        grad_val = jnp.zeros((tokens, head_dim), jnp.float32)
        for toks, cols, query_blk, upstream in source.blocks(head):
            position = lax.broadcasted_iota(jnp.int32, (tokens, rows), 1) // grouped + toks.start
            allowed = (lax.broadcasted_iota(jnp.int32, (tokens, rows), 0) <= position) & (
                doc_col == docs_ref[:, cols]
            )
            probs, grads = tile_terms(
                key_blk, value_blk, query_blk, upstream, norm_ref[head, :, cols], term_ref[head, :, cols],
                allowed, factor,
            )
            grad_val += jnp.dot(probs, upstream, preferred_element_type=jnp.float32)
            grad_key += jnp.dot(grads, query_blk, preferred_element_type=jnp.float32)
            grad_query = lax.dot_general(
                grads, key_blk, (((0,), (0,)), ((), ())), preferred_element_type=jnp.float32
            )
            dq_ref[toks, head * grouped:(head + 1) * grouped] = (grad_query * factor).reshape(
                rows // grouped, grouped, head_dim
            )
        dkv_ref[0, head] = grad_key * factor
        dkv_ref[1, head] = grad_val


def listed_kernel(factor, rows, first, places_ref, *refs):
    *column, other_ref, query_ref, up_ref, norm_ref, term_ref, dkv_ref, held_ref, sems = refs
    source = Rows(query_ref, up_ref, held_ref, sems, first, rows)
    tokens, grouped, head_dim = held_ref.shape[2:]
    for head in range(source.count):
        key_blk, value_blk = far_blocks(places_ref, column, other_ref, head)
        grad_key = jnp.zeros((2 * tokens, head_dim), jnp.float32)
        grad_val = jnp.zeros((2 * tokens, head_dim), jnp.float32)
        for toks, cols, query_blk, upstream in source.blocks(head):
            probs, grads = tile_terms(
                key_blk, value_blk, query_blk, upstream,
                norm_ref[first + head, :, cols], term_ref[first + head, :, cols], None, factor,
            )
            grad_val += jnp.dot(probs, upstream, preferred_element_type=jnp.float32)
            grad_key += jnp.dot(grads, query_blk, preferred_element_type=jnp.float32)
        grad_key = (grad_key * factor).astype(dkv_ref.dtype)
        grad_val = grad_val.astype(dkv_ref.dtype)
        for which in range(2):
            dkv_ref[which, 0, head] = grad_key[which * tokens:(which + 1) * tokens]
            dkv_ref[which, 1, head] = grad_val[which * tokens:(which + 1) * tokens]


def query_kernel(factor, rows, parts, places_ref, *refs):
    *inputs, query_ref, up_ref, norm_ref, term_ref, near_ref, _, dq_ref, held_ref, sems = refs
    source = Rows(query_ref, up_ref, held_ref, sems, 0, rows)
    tokens, grouped, head_dim = held_ref.shape[2:]
    size = len(inputs) // parts
    each = source.count // parts
    for head in range(source.count):
        *column, other_ref = inputs[head // each * size:(head // each + 1) * size]
        key_blk, value_blk = far_blocks(places_ref, column, other_ref, head % each)
        for toks, cols, query_blk, upstream in source.blocks(head):
            _, grads = tile_terms(
                key_blk, value_blk, query_blk, upstream, norm_ref[head, :, cols], term_ref[head, :, cols],
                None, factor,
            )
            grad_query = lax.dot_general(
                grads, key_blk, (((0,), (0,)), ((), ())), preferred_element_type=jnp.float32
            )
            heads = slice(head * grouped, (head + 1) * grouped)
            dq_ref[toks, heads] = near_ref[toks, heads] + (grad_query * factor).reshape(
                rows // grouped, grouped, head_dim
            )


def combine_kernel(places_ref, mine_ref, other_ref, *out_refs):
    for step, out_ref in enumerate(out_refs):
        for kind in range(2):
            for head in range(out_ref.shape[1]):
                total = None
                for i, ref in enumerate((mine_ref, other_ref)):
                    for which in range(2):
                        row = places_ref[4 + 2 * i + which:5 + 2 * i + which]
                        term = jnp.where(row == step, ref[which, kind, head].astype(jnp.float32), 0.0)
                        total = term if total is None else total + term
                out_ref[kind, head] = total.astype(out_ref.dtype)


def total_kernel(parts, near_ref, *refs):
    *blocks, dk_ref, dv_ref = refs
    count = len(blocks) // parts
    heads = dk_ref.shape[1]
    each = heads // parts
    for kind, out_ref in enumerate((dk_ref, dv_ref)):
        for head in range(heads):
            total = near_ref[kind, head]
            for ref in blocks[head // each * count:(head // each + 1) * count]:
                total += ref[kind, head % each].astype(jnp.float32)
            out_ref[:, head, :] = total


def body(queries, keys, values, grad_out, row_lse, row_delta, doc_ids, pairs):
    tokens, heads, head_dim = queries.shape
    kv_heads = keys.shape[1]
    grouped = QH // KVH
    factor = head_dim ** (-0.5)
    ring = lax.axis_size("ctx")
    subs = lax.axis_size("sub")
    rows = min(ROWS, tokens * grouped)
    cols = tokens * grouped
    parts = PARTS if kv_heads % PARTS == 0 else 1
    each = kv_heads // parts
    span_shape = (2, each, tokens, head_dim)

    def shifted(array, shift):
        return lax.ppermute(array, "ctx", [(i, (i + shift) % ring) for i in range(ring)])

    def swapped(array):
        return lax.ppermute(array, "sub", [(i, i ^ 1) for i in range(subs)])

    def in_hbm(*arrays):
        return [pltpu.with_memory_space_constraint(array, pltpu.HBM) for array in arrays]

    params = pltpu.CompilerParams(vmem_limit_bytes=VMEM_LIMIT)
    kv = pl.pallas_call(
        pack_kernel,
        in_specs=[HBM_SPEC] * 2,
        out_specs=[VMEM_SPEC] * parts,
        out_shape=[jax.ShapeDtypeStruct(span_shape, jnp.bfloat16)] * parts,
        scratch_shapes=[pltpu.VMEM((2, *keys.shape), jnp.bfloat16), pltpu.SemaphoreType.DMA((2,))],
        compiler_params=params,
        name="pack",
    )(*in_hbm(keys, values))
    columns = [[block] + [shifted(block, shift) for shift in range(1, ring)] for block in kv]

    norm, term, docs, doc_col, places = pl.pallas_call(
        functools.partial(spread_kernel, grouped, ring, subs),
        in_specs=[HBM_SPEC] * 4,
        out_specs=[VMEM_SPEC] * 5,
        out_shape=[
            jax.ShapeDtypeStruct((kv_heads, 1, cols), jnp.float32),
            jax.ShapeDtypeStruct((kv_heads, 1, cols), jnp.float32),
            jax.ShapeDtypeStruct((1, cols), jnp.float32),
            jax.ShapeDtypeStruct((tokens, tokens), jnp.float32),
            jax.ShapeDtypeStruct((8, head_dim), jnp.int32),
        ],
        scratch_shapes=[
            pltpu.VMEM((2, heads, tokens), jnp.float32),
            pltpu.VMEM((1, tokens), jnp.int32),
            pltpu.VMEM(pairs.shape[::-1], jnp.int32),
            pltpu.SemaphoreType.DMA((4,)),
        ],
        compiler_params=params,
        name="spread",
    )(*in_hbm(row_lse.T, row_delta.T, doc_ids.reshape(1, tokens), pairs.T))

    work = 2 * tokens * tokens * heads * head_dim
    moved = 2 * queries.size * 2

    def row_scratch(count):
        return [
            pltpu.VMEM((2, count, tokens, grouped, head_dim), jnp.bfloat16),
            pltpu.SemaphoreType.DMA((count, cols // rows, 2)),
        ]

    row_specs = [HBM_SPEC] * 2 + [VMEM_SPEC] * 2
    near_kv, near_query = pl.pallas_call(
        functools.partial(local_kernel, factor, rows),
        in_specs=[VMEM_SPEC] * parts + row_specs + [VMEM_SPEC] * 2,
        out_specs=[VMEM_SPEC] * 2,
        out_shape=[
            jax.ShapeDtypeStruct((2, kv_heads, tokens, head_dim), jnp.float32),
            jax.ShapeDtypeStruct((tokens, heads, head_dim), jnp.float32),
        ],
        scratch_shapes=row_scratch(kv_heads),
        compiler_params=params,
        cost_estimate=pl.CostEstimate(flops=5 * work, bytes_accessed=2 * moved, transcendentals=0),
        name="local_block",
    )(*kv, *in_hbm(queries, grad_out), norm, term, docs, doc_col)

    inputs, sums = [], []
    after = near_kv
    for part, column in enumerate(columns):
        chosen = pl.pallas_call(
            choose_kernel,
            in_specs=[VMEM_SPEC] * (ring + 1) + [ANY_SPEC] * 2,
            out_specs=VMEM_SPEC,
            out_shape=jax.ShapeDtypeStruct((2, *span_shape), jnp.bfloat16),
            compiler_params=params,
            name="choose",
        )(places, *column, near_kv, after)
        other = swapped(chosen)
        inputs += [*column, other]
        far_kv = pl.pallas_call(
            functools.partial(listed_kernel, factor, rows, part * each),
            in_specs=[VMEM_SPEC] * (ring + 2) + row_specs,
            out_specs=VMEM_SPEC,
            out_shape=jax.ShapeDtypeStruct((2, *span_shape), jnp.bfloat16),
            scratch_shapes=row_scratch(each),
            compiler_params=params,
            cost_estimate=pl.CostEstimate(flops=8 * work // parts, bytes_accessed=moved // parts, transcendentals=0),
            name="listed_keys",
        )(places, *column, other, *in_hbm(queries, grad_out), norm, term)
        other_kv = swapped(far_kv)
        blocks = pl.pallas_call(
            combine_kernel,
            in_specs=[VMEM_SPEC] * 3,
            out_specs=[VMEM_SPEC] * ring,
            out_shape=[jax.ShapeDtypeStruct(span_shape, jnp.float32)]
            + [jax.ShapeDtypeStruct(span_shape, jnp.bfloat16)] * (ring - 1),
            compiler_params=params,
            name="combine",
        )(places, far_kv, other_kv)
        sums += [blocks[0]] + [shifted(blocks[shift], shift) for shift in range(1, ring)]
        after = blocks[0]

    grad_queries = pl.pallas_call(
        functools.partial(query_kernel, factor, rows, parts),
        in_specs=[VMEM_SPEC] * (1 + len(inputs)) + row_specs + [VMEM_SPEC, ANY_SPEC],
        out_specs=VMEM_SPEC,
        out_shape=jax.ShapeDtypeStruct((tokens, heads, head_dim), jnp.float32),
        scratch_shapes=row_scratch(kv_heads),
        compiler_params=params,
        cost_estimate=pl.CostEstimate(flops=6 * work, bytes_accessed=3 * moved, transcendentals=0),
        name="listed_queries",
    )(places, *inputs, *in_hbm(queries, grad_out), norm, term, near_query, after)

    grad_keys, grad_values = pl.pallas_call(
        functools.partial(total_kernel, parts),
        in_specs=[VMEM_SPEC] * (parts * ring + 1),
        out_specs=[VMEM_SPEC] * 2,
        out_shape=[jax.ShapeDtypeStruct((tokens, kv_heads, head_dim), jnp.float32)] * 2,
        compiler_params=params,
        name="total",
    )(near_kv, *sums)
    return (grad_queries, grad_keys, grad_values)


def solution(mesh):
    return jax.shard_map(
        body,
        mesh=mesh,
        in_specs=(
            P(("groups", "ctx", "sub"), "head", None),
            P(("groups", "ctx", "sub"), "head", None),
            P(("groups", "ctx", "sub"), "head", None),
            P(("groups", "ctx", "sub"), "head", None),
            P(("groups", "ctx", "sub"), "head"),
            P(("groups", "ctx", "sub"), "head"),
            P(("groups", "ctx", "sub")),
            P("groups", None),
        ),
        out_specs=(
            P(("groups", "ctx", "sub"), "head", None),
            P(("groups", "ctx", "sub"), "head", None),
            P(("groups", "ctx", "sub"), "head", None),
        ),
        check_vma=False,
    )
```

profile of v0, /device:TPU:0, one launch (start us, length us, event | category | flops | bytes accessed | tf_op | source)
XLA Modules:
  0.0 39.5 jit_solution(1705697117358155991)
XLA Ops:
  0.6 1.2 %pack.1.refs_0_ = bf16[2,2,128,128]{3,2,1,0:T(8,128)(2,1)S(1)} custom-call(bf16[128,2,128]{2,1,0:T(2,128)(2,1)} %key_ref.1, bf16[128,2,128]{2,1,0:T(2,128)(2,1)} %value_ref.1), custom_call_target="tpu_custom_call" | custom-call | tf_op jit(solution)/shard_map/pack/pallas_call | solution.py:298
  1.9 3.1 %collective-permute-start = (bf16[2,2,128,128]{3,2,1,0:T(8,128)(2,1)S(1)}, bf16[2,2,128,128]{3,2,1,0:T(8,128)(2,1)S(1)}, u32[]{:S(2)}, u32[]{:S(2)}) collective-permute-start(bf16[2,2,128,128]{3,2,1,0:T(8,128)(2,1)S(1)} %pack.1.refs_0_), channel_id=1, source_target_pairs={{0,4},{4,8},{8,12},{12,0},{1,5},{5,9},{9,13},{13,1},{2,6},{6,10},{... | collective-permute-start | bytes 393224 | tf_op jit(solution)/shard_map/ppermute | solution.py:289
  5.0 2.6 %collective-permute-start.1 = (bf16[2,2,128,128]{3,2,1,0:T(8,128)(2,1)S(1)}, bf16[2,2,128,128]{3,2,1,0:T(8,128)(2,1)S(1)}, u32[]{:S(2)}, u32[]{:S(2)}) collective-permute-start(bf16[2,2,128,128]{3,2,1,0:T(8,128)(2,1)S(1)} %pack.1.refs_0_), channel_id=1, source_target_pairs={{0,8},{4,12},{8,0},{12,4},{1,9},{5,13},{9,1},{13,5},{2,10},{6,14},... | collective-permute-start | bytes 393224 | tf_op jit(solution)/shard_map/ppermute | solution.py:289
  7.5 1.3 %collective-permute-start.2 = (bf16[2,2,128,128]{3,2,1,0:T(8,128)(2,1)S(1)}, bf16[2,2,128,128]{3,2,1,0:T(8,128)(2,1)S(1)}, u32[]{:S(2)}, u32[]{:S(2)}) collective-permute-start(bf16[2,2,128,128]{3,2,1,0:T(8,128)(2,1)S(1)} %pack.1.refs_0_), channel_id=1, source_target_pairs={{0,12},{4,0},{8,4},{12,8},{1,13},{5,1},{9,5},{13,9},{2,14},{6,2},{... | collective-permute-start | bytes 393224 | tf_op jit(solution)/shard_map/ppermute | solution.py:289
  8.9 1.2 %spread.1 = (f32[2,1,2048]{2,1,0:T(1,128)S(1)}, f32[2,1,2048]{2,1,0:T(1,128)S(1)}, f32[1,2048]{1,0:T(1,128)S(1)}, f32[128,128]{1,0:T(8,128)S(1)}, s32[8,128]{1,0:T(8,128)S(1)}) custom-call(f32[32,128]{1,0:T(8,128)} %bitcast.4, f32[32,128]{1,0:T(8,128)} %bitcast.5, s32[1,128]{1,0:T(1,128)} %bitcast.7, s32[2,8]{1,0:T(2,128)} %bitcast.6), custom_call_target="tpu_custom_call" | custom-call | tf_op jit(solution)/shard_map/spread/pallas_call | solution.py:309
  10.1 5.0 %local_block.1 = (f32[2,2,128,128]{3,2,1,0:T(8,128)S(1)}, f32[128,32,128]{2,1,0:T(8,128)S(1)}) custom-call(bf16[2,2,128,128]{3,2,1,0:T(8,128)(2,1)S(1)} %pack.1.refs_0_, bf16[128,32,128]{2,1,0:T(8,128)(2,1)} %refs_5_.3, bf16[128,32,128]{2,1,0:T(8,128)(2,1)} %refs_6_.3, f32[2,1,2048]{2,1,0:T(1,128)S(1)} %get-tuple-element.17.refs_3_.refs_7_, ...), custom_call_target="tpu_custom_call" | custom-call | flops 671088640 | bytes 4194304 | tf_op jit(solution)/shard_map/local_block/pallas_call | solution.py:340
  15.1 0.0 collective-permute-done.refs_1_
  15.1 1.1 %collective-permute-done.1.refs_2_ = bf16[2,2,128,128]{3,2,1,0:T(8,128)(2,1)S(1)} collective-permute-done((bf16[2,2,128,128]{3,2,1,0:T(8,128)(2,1)S(1)}, bf16[2,2,128,128]{3,2,1,0:T(8,128)(2,1)S(1)}, u32[]{:S(2)}, u32[]{:S(2)}) %collective-permute-start.1) | collective-permute-done | bytes 131104 | tf_op jit(solution)/shard_map/ppermute | solution.py:289
  16.2 0.0 collective-permute-done.2.refs_3_
  16.2 0.1 choose.1
  16.3 0.1 collective-permute-start.3
  16.4 1.5 %collective-permute-done.3.refs_4_ = bf16[2,2,2,128,128]{4,3,2,1,0:T(8,128)(2,1)S(1)} collective-permute-done((bf16[2,2,2,128,128]{4,3,2,1,0:T(8,128)(2,1)S(1)}, bf16[2,2,2,128,128]{4,3,2,1,0:T(8,128)(2,1)S(1)}, u32[]{:S(2)}, u32[]{:S(2)}) %collective-permute-start.3) | collective-permute-done | bytes 262176 | tf_op jit(solution)/shard_map/ppermute | solution.py:292
  17.9 4.8 %listed_keys.1.mine_ref = bf16[2,2,2,128,128]{4,3,2,1,0:T(8,128)(2,1)S(1)} custom-call(s32[8,128]{1,0:T(8,128)S(1)} %get-tuple-element.16.places_ref, bf16[2,2,128,128]{3,2,1,0:T(8,128)(2,1)S(1)} %pack.1.refs_0_, bf16[2,2,128,128]{3,2,1,0:T(8,128)(2,1)S(1)} %collective-permute-done.refs_1_, bf16[2,2,128,128]{3,2,1,0:T(8,128)(2,1)S(1)} %collective-permute-done.1.refs_2_, ...), custom_call_target="tpu_custom_call" | custom-call | flops 1073741824 | bytes 2097152 | tf_op jit(solution)/shard_map/listed_keys/pallas_call | solution.py:367
  22.7 0.2 collective-permute-start.4
  22.9 1.4 %collective-permute-done.4.other_ref = bf16[2,2,2,128,128]{4,3,2,1,0:T(8,128)(2,1)S(1)} collective-permute-done((bf16[2,2,2,128,128]{4,3,2,1,0:T(8,128)(2,1)S(1)}, bf16[2,2,2,128,128]{4,3,2,1,0:T(8,128)(2,1)S(1)}, u32[]{:S(2)}, u32[]{:S(2)}) %collective-permute-start.4) | collective-permute-done | bytes 262176 | tf_op jit(solution)/shard_map/ppermute | solution.py:292
  24.3 0.4 %combine.1 = (f32[2,2,128,128]{3,2,1,0:T(8,128)S(1)}, bf16[2,2,128,128]{3,2,1,0:T(8,128)(2,1)S(1)}, bf16[2,2,128,128]{3,2,1,0:T(8,128)(2,1)S(1)}, bf16[2,2,128,128]{3,2,1,0:T(8,128)(2,1)S(1)}) custom-call(s32[8,128]{1,0:T(8,128)S(1)} %get-tuple-element.16.places_ref, bf16[2,2,2,128,128]{4,3,2,1,0:T(8,128)(2,1)S(1)} %listed_keys.1.mine_ref, ...), custom_call_target="tpu_custom_call" | custom-call | tf_op jit(solution)/shard_map/combine/pallas_call | solution.py:378
  24.7 3.3 %collective-permute-start.5 = (bf16[2,2,128,128]{3,2,1,0:T(8,128)(2,1)S(1)}, bf16[2,2,128,128]{3,2,1,0:T(8,128)(2,1)S(1)}, u32[]{:S(2)}, u32[]{:S(2)}) collective-permute-start(bf16[2,2,128,128]{3,2,1,0:T(8,128)(2,1)S(1)} %get-tuple-element.24), channel_id=1, source_target_pairs={{0,4},{4,8},{8,12},{12,0},{1,5},{5,9},{9,13},{13,1},{2,6},{6,10},{... | collective-permute-start | bytes 393224 | tf_op jit(solution)/shard_map/ppermute | solution.py:289
  28.1 1.6 %collective-permute-start.6 = (bf16[2,2,128,128]{3,2,1,0:T(8,128)(2,1)S(1)}, bf16[2,2,128,128]{3,2,1,0:T(8,128)(2,1)S(1)}, u32[]{:S(2)}, u32[]{:S(2)}) collective-permute-start(bf16[2,2,128,128]{3,2,1,0:T(8,128)(2,1)S(1)} %get-tuple-element.25), channel_id=1, source_target_pairs={{0,8},{4,12},{8,0},{12,4},{1,9},{5,13},{9,1},{13,5},{2,10},{6,14},... | collective-permute-start | bytes 393224 | tf_op jit(solution)/shard_map/ppermute | solution.py:289
  29.7 0.8 %collective-permute-start.7 = (bf16[2,2,128,128]{3,2,1,0:T(8,128)(2,1)S(1)}, bf16[2,2,128,128]{3,2,1,0:T(8,128)(2,1)S(1)}, u32[]{:S(2)}, u32[]{:S(2)}) collective-permute-start(bf16[2,2,128,128]{3,2,1,0:T(8,128)(2,1)S(1)} %get-tuple-element.26), channel_id=1, source_target_pairs={{0,12},{4,0},{8,4},{12,8},{1,13},{5,1},{9,5},{13,9},{2,14},{6,2},{... | collective-permute-start | bytes 393224 | tf_op jit(solution)/shard_map/ppermute | solution.py:289
  30.5 7.3 %listed_queries.1 = f32[128,32,128]{2,1,0:T(8,128)} custom-call(s32[8,128]{1,0:T(8,128)S(1)} %get-tuple-element.16.places_ref, bf16[2,2,128,128]{3,2,1,0:T(8,128)(2,1)S(1)} %pack.1.refs_0_, bf16[2,2,128,128]{3,2,1,0:T(8,128)(2,1)S(1)} %collective-permute-done.refs_1_, bf16[2,2,128,128]{3,2,1,0:T(8,128)(2,1)S(1)} %collective-permute-done.1.refs_2_, ...), custom_call_target="tpu_custom_call" | custom-call | flops 805306368 | bytes 6291456 | tf_op jit(solution)/shard_map/listed_queries/pallas_call | solution.py:390
  37.8 0.0 collective-permute-done.5.refs_1_
  37.9 0.8 %collective-permute-done.6.refs_2_ = bf16[2,2,128,128]{3,2,1,0:T(8,128)(2,1)S(1)} collective-permute-done((bf16[2,2,128,128]{3,2,1,0:T(8,128)(2,1)S(1)}, bf16[2,2,128,128]{3,2,1,0:T(8,128)(2,1)S(1)}, u32[]{:S(2)}, u32[]{:S(2)}) %collective-permute-start.6) | collective-permute-done | bytes 131104 | tf_op jit(solution)/shard_map/ppermute | solution.py:289
  38.6 0.0 collective-permute-done.7.refs_3_
  38.6 0.8 %total.1 = (f32[128,2,128]{2,1,0:T(2,128)}, f32[128,2,128]{2,1,0:T(2,128)}) custom-call(f32[2,2,128,128]{3,2,1,0:T(8,128)S(1)} %get-tuple-element.21.refs_4_.refs_5_.near_ref, f32[2,2,128,128]{3,2,1,0:T(8,128)S(1)} %get-tuple-element.23.refs_10_.refs_0_, bf16[2,2,128,128]{3,2,1,0:T(8,128)(2,1)S(1)} %collective-permute-done.5.refs_1_, ...), custom_call_target="tpu_custom_call" | custom-call | tf_op jit(solution)/shard_map/total/pallas_call | solution.py:401
Async XLA Ops:
  1.9 13.2 %collective-permute-start = (bf16[2,2,128,128]{3,2,1,0:T(8,128)(2,1)S(1)}, bf16[2,2,128,128]{3,2,1,0:T(8,128)(2,1)S(1)}, u32[]{:S(2)}, u32[]{:S(2)}) collective-permute-start(bf16[2,2,128,128]{3,2,1,0:T(8,128)(2,1)S(1)} %pack.1.refs_0_), channel_id=1, source_target_pairs={{0,4},{4,8},{8,12},{12,0},{1,5},{5,9},{9,13},{13,1},{2,6},{6,10},{... | collective-permute-start | bytes 393224 | tf_op jit(solution)/shard_map/ppermute | solution.py:289
  5.0 11.2 %collective-permute-start.1 = (bf16[2,2,128,128]{3,2,1,0:T(8,128)(2,1)S(1)}, bf16[2,2,128,128]{3,2,1,0:T(8,128)(2,1)S(1)}, u32[]{:S(2)}, u32[]{:S(2)}) collective-permute-start(bf16[2,2,128,128]{3,2,1,0:T(8,128)(2,1)S(1)} %pack.1.refs_0_), channel_id=1, source_target_pairs={{0,8},{4,12},{8,0},{12,4},{1,9},{5,13},{9,1},{13,5},{2,10},{6,14},... | collective-permute-start | bytes 393224 | tf_op jit(solution)/shard_map/ppermute | solution.py:289
  7.5 8.6 %collective-permute-start.2 = (bf16[2,2,128,128]{3,2,1,0:T(8,128)(2,1)S(1)}, bf16[2,2,128,128]{3,2,1,0:T(8,128)(2,1)S(1)}, u32[]{:S(2)}, u32[]{:S(2)}) collective-permute-start(bf16[2,2,128,128]{3,2,1,0:T(8,128)(2,1)S(1)} %pack.1.refs_0_), channel_id=1, source_target_pairs={{0,12},{4,0},{8,4},{12,8},{1,13},{5,1},{9,5},{13,9},{2,14},{6,2},{... | collective-permute-start | bytes 393224 | tf_op jit(solution)/shard_map/ppermute | solution.py:289
  16.3 1.6 %collective-permute-start.3 = (bf16[2,2,2,128,128]{4,3,2,1,0:T(8,128)(2,1)S(1)}, bf16[2,2,2,128,128]{4,3,2,1,0:T(8,128)(2,1)S(1)}, u32[]{:S(2)}, u32[]{:S(2)}) collective-permute-start(bf16[2,2,2,128,128]{4,3,2,1,0:T(8,128)(2,1)S(1)} %choose.1), channel_id=1, source_target_pairs={{0,1},{1,0},{2,3},{3,2},{4,5},{5,4},{6,7},{7,6},{8,9},{9,8},{10,11... | collective-permute-start | bytes 786440 | tf_op jit(solution)/shard_map/ppermute | solution.py:292
  22.7 1.6 %collective-permute-start.4 = (bf16[2,2,2,128,128]{4,3,2,1,0:T(8,128)(2,1)S(1)}, bf16[2,2,2,128,128]{4,3,2,1,0:T(8,128)(2,1)S(1)}, u32[]{:S(2)}, u32[]{:S(2)}) collective-permute-start(bf16[2,2,2,128,128]{4,3,2,1,0:T(8,128)(2,1)S(1)} %listed_keys.1.mine_ref), channel_id=1, source_target_pairs={{0,1},{1,0},{2,3},{3,2},{4,5},{5,4},{6,7},{7,6},{8,9},{9,8},{10,11... | collective-permute-start | bytes 786440 | tf_op jit(solution)/shard_map/ppermute | solution.py:292
  24.7 13.1 %collective-permute-start.5 = (bf16[2,2,128,128]{3,2,1,0:T(8,128)(2,1)S(1)}, bf16[2,2,128,128]{3,2,1,0:T(8,128)(2,1)S(1)}, u32[]{:S(2)}, u32[]{:S(2)}) collective-permute-start(bf16[2,2,128,128]{3,2,1,0:T(8,128)(2,1)S(1)} %get-tuple-element.24), channel_id=1, source_target_pairs={{0,4},{4,8},{8,12},{12,0},{1,5},{5,9},{9,13},{13,1},{2,6},{6,10},{... | collective-permute-start | bytes 393224 | tf_op jit(solution)/shard_map/ppermute | solution.py:289
  28.1 10.6 %collective-permute-start.6 = (bf16[2,2,128,128]{3,2,1,0:T(8,128)(2,1)S(1)}, bf16[2,2,128,128]{3,2,1,0:T(8,128)(2,1)S(1)}, u32[]{:S(2)}, u32[]{:S(2)}) collective-permute-start(bf16[2,2,128,128]{3,2,1,0:T(8,128)(2,1)S(1)} %get-tuple-element.25), channel_id=1, source_target_pairs={{0,8},{4,12},{8,0},{12,4},{1,9},{5,13},{9,1},{13,5},{2,10},{6,14},... | collective-permute-start | bytes 393224 | tf_op jit(solution)/shard_map/ppermute | solution.py:289
  29.7 8.9 %collective-permute-start.7 = (bf16[2,2,128,128]{3,2,1,0:T(8,128)(2,1)S(1)}, bf16[2,2,128,128]{3,2,1,0:T(8,128)(2,1)S(1)}, u32[]{:S(2)}, u32[]{:S(2)}) collective-permute-start(bf16[2,2,128,128]{3,2,1,0:T(8,128)(2,1)S(1)} %get-tuple-element.26), channel_id=1, source_target_pairs={{0,12},{4,0},{8,4},{12,8},{1,13},{5,1},{9,5},{13,9},{2,14},{6,2},{... | collective-permute-start | bytes 393224 | tf_op jit(solution)/shard_map/ppermute | solution.py:289
where the time goes:
time: 40.2 us; the launch traced here: 39.5 us
  Pallas kernels  20.9 us (52%)
  starting transfers between devices  13.1 us (33%)
  waiting for transfers between devices  4.81 us (12%)
  between operations  0.71 us (2%)
    ppermute x6, starting transfers between devices, shifted(): lax.ppermute(array, 'ctx', [(i, (i + shift) % ring) for i in range(ring)])  12.8 us
    pallas_call x1, Pallas kernels, body(): pl.pallas_call(functools.partial(query_kernel, factor, rows, parts), in_s...  7.34 us
    pallas_call x1, Pallas kernels, body(): pl.pallas_call(functools.partial(local_kernel, factor, rows), in_specs=[V...  4.99 us
    pallas_call x1, Pallas kernels, body(): pl.pallas_call(functools.partial(listed_kernel, factor, rows, part * each...  4.78 us
    ppermute x2, waiting for transfers between devices, swapped(): return lax.ppermute(array, 'sub', [(i, i ^ 1) for i in range(subs)])  2.92 us
    ppermute x6, waiting for transfers between devices, shifted(): lax.ppermute(array, 'ctx', [(i, (i + shift) % ring) for i in range(ring)])  1.89 us
    pallas_call x1, Pallas kernels, body(): pl.pallas_call(pack_kernel, in_specs=[HBM_SPEC] * 2, out_specs=[VMEM_SPEC...  1.24 us
    pallas_call x1, Pallas kernels, body(): pl.pallas_call(functools.partial(spread_kernel, grouped, ring, subs), in_...  1.18 us
  transfers between devices with their start and end apart: 8, of which 4 were waited for; matrix products, arithmetic and copies ran while one was open for 0% of the time, Pallas kernels for 34%

commit v1 on v0

--- a/solution.py
+++ b/solution.py
@@ -45,29 +45,27 @@
     return copies
 
 
-class Rows:
-    def __init__(self, query_ref, up_ref, held_ref, sems, first, rows):
-        _, self.count, tokens, self.grouped, self.head_dim = held_ref.shape
-        self.held, self.rows = held_ref, rows
-        self.steps = chunks(tokens, self.grouped, rows)
-        self.copies = {}
-        for head in range(self.count):
-            heads = slice((first + head) * self.grouped, (first + head + 1) * self.grouped)
-            for i, toks, _ in self.steps:
-                for kind, ref in enumerate((query_ref, up_ref)):
-                    copy = pltpu.make_async_copy(
-                        ref.at[toks, heads], held_ref.at[kind, head, toks], sems.at[head, i, kind]
-                    )
-                    copy.start()
-                    self.copies[head, i, kind] = copy
-
-    def blocks(self, head):
-        for i, toks, cols in self.steps:
-            pair = []
-            for kind in range(2):
-                self.copies[head, i, kind].wait()
-                pair.append(self.held[kind, head, toks].reshape(self.rows, self.head_dim))
-            yield toks, cols, *pair
+def bring_rows(query_ref, up_ref, held_ref, sems, rows):
+    _, count, tokens, grouped, _ = held_ref.shape
+    copies = {}
+    for head in range(count):
+        heads = slice(head * grouped, (head + 1) * grouped)
+        for i, toks, _ in chunks(tokens, grouped, rows):
+            copies[head, i] = [
+                pltpu.make_async_copy(ref.at[toks, heads], held_ref.at[kind, head, toks], sems.at[head, i, kind])
+                for kind, ref in enumerate((query_ref, up_ref))
+            ]
+            for copy in copies[head, i]:
+                copy.start()
+    return copies
+
+
+def row_blocks(held_ref, head, rows, copies=None):
+    _, _, tokens, grouped, head_dim = held_ref.shape
+    for i, toks, cols in chunks(tokens, grouped, rows):
+        for copy in copies[head, i] if copies else ():
+            copy.wait()
+        yield toks, cols, *(held_ref[kind, head, toks].reshape(rows, head_dim) for kind in range(2))
 
 
 def pack_kernel(key_ref, value_ref, *refs):
@@ -172,15 +170,15 @@
 
 def local_kernel(factor, rows, *refs):
     *kv_refs, query_ref, up_ref, norm_ref, term_ref, docs_ref, doc_col_ref, dkv_ref, dq_ref, held_ref, sems = refs
-    source = Rows(query_ref, up_ref, held_ref, sems, 0, rows)
+    copies = bring_rows(query_ref, up_ref, held_ref, sems, rows)
     tokens, grouped, head_dim = held_ref.shape[2:]
     each = kv_refs[0].shape[1]
     doc_col = jnp.concatenate([doc_col_ref[...]] * (rows // tokens), axis=1)
-    for head in range(source.count):
+    for head in range(held_ref.shape[1]):
         key_blk, value_blk = kv_refs[head // each][0, head % each], kv_refs[head // each][1, head % each]
         grad_key = jnp.zeros((tokens, head_dim), jnp.float32)
         grad_val = jnp.zeros((tokens, head_dim), jnp.float32)
-        for toks, cols, query_blk, upstream in source.blocks(head):
+        for toks, cols, query_blk, upstream in row_blocks(held_ref, head, rows, copies):
             position = lax.broadcasted_iota(jnp.int32, (tokens, rows), 1) // grouped + toks.start
             allowed = (lax.broadcasted_iota(jnp.int32, (tokens, rows), 0) <= position) & (
                 doc_col == docs_ref[:, cols]
@@ -202,14 +200,13 @@
 
 
 def listed_kernel(factor, rows, first, places_ref, *refs):
-    *column, other_ref, query_ref, up_ref, norm_ref, term_ref, dkv_ref, held_ref, sems = refs
-    source = Rows(query_ref, up_ref, held_ref, sems, first, rows)
+    *column, other_ref, held_ref, norm_ref, term_ref, dkv_ref = refs
     tokens, grouped, head_dim = held_ref.shape[2:]
-    for head in range(source.count):
+    for head in range(other_ref.shape[2]):
         key_blk, value_blk = far_blocks(places_ref, column, other_ref, head)
         grad_key = jnp.zeros((2 * tokens, head_dim), jnp.float32)
         grad_val = jnp.zeros((2 * tokens, head_dim), jnp.float32)
-        for toks, cols, query_blk, upstream in source.blocks(head):
+        for toks, cols, query_blk, upstream in row_blocks(held_ref, first + head, rows):
             probs, grads = tile_terms(
                 key_blk, value_blk, query_blk, upstream,
                 norm_ref[first + head, :, cols], term_ref[first + head, :, cols], None, factor,
@@ -224,15 +221,14 @@
 
 
 def query_kernel(factor, rows, parts, places_ref, *refs):
-    *inputs, query_ref, up_ref, norm_ref, term_ref, near_ref, _, dq_ref, held_ref, sems = refs
-    source = Rows(query_ref, up_ref, held_ref, sems, 0, rows)
+    *inputs, held_ref, norm_ref, term_ref, near_ref, _, dq_ref = refs
     tokens, grouped, head_dim = held_ref.shape[2:]
     size = len(inputs) // parts
-    each = source.count // parts
-    for head in range(source.count):
+    each = held_ref.shape[1] // parts
+    for head in range(held_ref.shape[1]):
         *column, other_ref = inputs[head // each * size:(head // each + 1) * size]
         key_blk, value_blk = far_blocks(places_ref, column, other_ref, head % each)
-        for toks, cols, query_blk, upstream in source.blocks(head):
+        for toks, cols, query_blk, upstream in row_blocks(held_ref, head, rows):
             _, grads = tile_terms(
                 key_blk, value_blk, query_blk, upstream, norm_ref[head, :, cols], term_ref[head, :, cols],
                 None, factor,
@@ -330,22 +326,17 @@
     work = 2 * tokens * tokens * heads * head_dim
     moved = 2 * queries.size * 2
 
-    def row_scratch(count):
-        return [
-            pltpu.VMEM((2, count, tokens, grouped, head_dim), jnp.bfloat16),
-            pltpu.SemaphoreType.DMA((count, cols // rows, 2)),
-        ]
-
-    row_specs = [HBM_SPEC] * 2 + [VMEM_SPEC] * 2
-    near_kv, near_query = pl.pallas_call(
+    row_specs = [VMEM_SPEC] * 3
+    near_kv, near_query, held = pl.pallas_call(
         functools.partial(local_kernel, factor, rows),
-        in_specs=[VMEM_SPEC] * parts + row_specs + [VMEM_SPEC] * 2,
-        out_specs=[VMEM_SPEC] * 2,
+        in_specs=[VMEM_SPEC] * parts + [HBM_SPEC] * 2 + [VMEM_SPEC] * 4,
+        out_specs=[VMEM_SPEC] * 3,
         out_shape=[
             jax.ShapeDtypeStruct((2, kv_heads, tokens, head_dim), jnp.float32),
             jax.ShapeDtypeStruct((tokens, heads, head_dim), jnp.float32),
+            jax.ShapeDtypeStruct((2, kv_heads, tokens, grouped, head_dim), jnp.bfloat16),
         ],
-        scratch_shapes=row_scratch(kv_heads),
+        scratch_shapes=[pltpu.SemaphoreType.DMA((kv_heads, cols // rows, 2))],
         compiler_params=params,
         cost_estimate=pl.CostEstimate(flops=5 * work, bytes_accessed=2 * moved, transcendentals=0),
         name="local_block",
@@ -369,11 +360,10 @@
             in_specs=[VMEM_SPEC] * (ring + 2) + row_specs,
             out_specs=VMEM_SPEC,
             out_shape=jax.ShapeDtypeStruct((2, *span_shape), jnp.bfloat16),
-            scratch_shapes=row_scratch(each),
             compiler_params=params,
             cost_estimate=pl.CostEstimate(flops=8 * work // parts, bytes_accessed=moved // parts, transcendentals=0),
             name="listed_keys",
-        )(places, *column, other, *in_hbm(queries, grad_out), norm, term)
+        )(places, *column, other, held, norm, term)
         other_kv = swapped(far_kv)
         blocks = pl.pallas_call(
             combine_kernel,
@@ -392,11 +382,10 @@
         in_specs=[VMEM_SPEC] * (1 + len(inputs)) + row_specs + [VMEM_SPEC, ANY_SPEC],
         out_specs=VMEM_SPEC,
         out_shape=jax.ShapeDtypeStruct((tokens, heads, head_dim), jnp.float32),
-        scratch_shapes=row_scratch(kv_heads),
         compiler_params=params,
         cost_estimate=pl.CostEstimate(flops=6 * work, bytes_accessed=3 * moved, transcendentals=0),
         name="listed_queries",
-    )(places, *inputs, *in_hbm(queries, grad_out), norm, term, near_query, after)
+    )(places, *inputs, held, norm, term, near_query, after)
 
     grad_keys, grad_values = pl.pallas_call(
         functools.partial(total_kernel, parts),

time: 40.2 us -> 37.8 us (0.940)
  Pallas kernels: 20.9 us -> 15.7 us
  waiting for transfers between devices: 4.81 us -> 7.72 us
    ppermute x6, waiting for transfers between devices: 1.89 us -> 4.8 us  [shifted(): lax.ppermute(array, 'ctx', [(i, (i + shift) % ring) for i in range(ring)])]
    pallas_call x1, Pallas kernels: 7.34 us -> 4.51 us  [body(): pl.pallas_call(functools.partial(query_kernel, factor, rows, parts), in_s...]
    pallas_call x1, Pallas kernels: 4.78 us -> 2.45 us  [body(): pl.pallas_call(functools.partial(listed_kernel, factor, rows, part * each...]
  transfers between devices with their start and end apart: 8 -> 8, of which waited for: 4 -> 4; matrix products, arithmetic and copies ran while one was open for 0% -> 0% of each run, Pallas kernels for 34% -> 29%
where the time goes in v1:
time: 37.8 us; the launch traced here: 37.1 us
  Pallas kernels  15.7 us (42%)
  starting transfers between devices  13.1 us (35%)
  waiting for transfers between devices  7.72 us (20%)
  between operations  0.69 us (2%)
    ppermute x6, starting transfers between devices, shifted(): lax.ppermute(array, 'ctx', [(i, (i + shift) % ring) for i in range(ring)])  12.8 us
    pallas_call x1, Pallas kernels, body(): pl.pallas_call(functools.partial(local_kernel, factor, rows), in_specs=[V...  4.93 us
    ppermute x6, waiting for transfers between devices, shifted(): lax.ppermute(array, 'ctx', [(i, (i + shift) % ring) for i in range(ring)])  4.8 us
    pallas_call x1, Pallas kernels, body(): pl.pallas_call(functools.partial(query_kernel, factor, rows, parts), in_s...  4.51 us
    ppermute x2, waiting for transfers between devices, swapped(): return lax.ppermute(array, 'sub', [(i, i ^ 1) for i in range(subs)])  2.92 us
    pallas_call x1, Pallas kernels, body(): pl.pallas_call(functools.partial(listed_kernel, factor, rows, part * each...  2.45 us
    pallas_call x1, Pallas kernels, body(): pl.pallas_call(pack_kernel, in_specs=[HBM_SPEC] * 2, out_specs=[VMEM_SPEC...  1.24 us
    pallas_call x1, Pallas kernels, body(): pl.pallas_call(functools.partial(spread_kernel, grouped, ring, subs), in_...  1.18 us
  transfers between devices with their start and end apart: 8, of which 4 were waited for; matrix products, arithmetic and copies ran while one was open for 0% of the time, Pallas kernels for 29%

profile of v1, /device:TPU:0, one launch (start us, length us, event | category | flops | bytes accessed | tf_op | source)
XLA Modules:
  0.0 37.1 jit_solution(15762110393223544232)
XLA Ops:
  0.6 1.2 %pack.1.refs_0_ = bf16[2,2,128,128]{3,2,1,0:T(8,128)(2,1)S(1)} custom-call(bf16[128,2,128]{2,1,0:T(2,128)(2,1)} %key_ref.1, bf16[128,2,128]{2,1,0:T(2,128)(2,1)} %value_ref.1), custom_call_target="tpu_custom_call" | custom-call | tf_op jit(solution)/shard_map/pack/pallas_call | solution.py:294
  1.9 3.1 %collective-permute-start = (bf16[2,2,128,128]{3,2,1,0:T(8,128)(2,1)S(1)}, bf16[2,2,128,128]{3,2,1,0:T(8,128)(2,1)S(1)}, u32[]{:S(2)}, u32[]{:S(2)}) collective-permute-start(bf16[2,2,128,128]{3,2,1,0:T(8,128)(2,1)S(1)} %pack.1.refs_0_), channel_id=1, source_target_pairs={{0,4},{4,8},{8,12},{12,0},{1,5},{5,9},{9,13},{13,1},{2,6},{6,10},{... | collective-permute-start | bytes 393224 | tf_op jit(solution)/shard_map/ppermute | solution.py:285
  5.0 2.6 %collective-permute-start.1 = (bf16[2,2,128,128]{3,2,1,0:T(8,128)(2,1)S(1)}, bf16[2,2,128,128]{3,2,1,0:T(8,128)(2,1)S(1)}, u32[]{:S(2)}, u32[]{:S(2)}) collective-permute-start(bf16[2,2,128,128]{3,2,1,0:T(8,128)(2,1)S(1)} %pack.1.refs_0_), channel_id=1, source_target_pairs={{0,8},{4,12},{8,0},{12,4},{1,9},{5,13},{9,1},{13,5},{2,10},{6,14},... | collective-permute-start | bytes 393224 | tf_op jit(solution)/shard_map/ppermute | solution.py:285
  7.5 1.3 %collective-permute-start.2 = (bf16[2,2,128,128]{3,2,1,0:T(8,128)(2,1)S(1)}, bf16[2,2,128,128]{3,2,1,0:T(8,128)(2,1)S(1)}, u32[]{:S(2)}, u32[]{:S(2)}) collective-permute-start(bf16[2,2,128,128]{3,2,1,0:T(8,128)(2,1)S(1)} %pack.1.refs_0_), channel_id=1, source_target_pairs={{0,12},{4,0},{8,4},{12,8},{1,13},{5,1},{9,5},{13,9},{2,14},{6,2},{... | collective-permute-start | bytes 393224 | tf_op jit(solution)/shard_map/ppermute | solution.py:285
  8.9 1.2 %spread.1 = (f32[2,1,2048]{2,1,0:T(1,128)S(1)}, f32[2,1,2048]{2,1,0:T(1,128)S(1)}, f32[1,2048]{1,0:T(1,128)S(1)}, f32[128,128]{1,0:T(8,128)S(1)}, s32[8,128]{1,0:T(8,128)S(1)}) custom-call(f32[32,128]{1,0:T(8,128)} %bitcast.4, f32[32,128]{1,0:T(8,128)} %bitcast.5, s32[1,128]{1,0:T(1,128)} %bitcast.7, s32[2,8]{1,0:T(2,128)} %bitcast.6), custom_call_target="tpu_custom_call" | custom-call | tf_op jit(solution)/shard_map/spread/pallas_call | solution.py:305
  10.1 4.9 %local_block.1 = (f32[2,2,128,128]{3,2,1,0:T(8,128)S(1)}, f32[128,32,128]{2,1,0:T(8,128)S(1)}, bf16[2,2,128,16,128]{4,3,2,1,0:T(8,128)(2,1)S(1)}) custom-call(bf16[2,2,128,128]{3,2,1,0:T(8,128)(2,1)S(1)} %pack.1.refs_0_, bf16[128,32,128]{2,1,0:T(8,128)(2,1)} %refs_1_.1, bf16[128,32,128]{2,1,0:T(8,128)(2,1)} %refs_2_.1, ...), custom_call_target="tpu_custom_call" | custom-call | flops 671088640 | bytes 4194304 | tf_op jit(solution)/shard_map/local_block/pallas_call | solution.py:330
  15.0 0.0 collective-permute-done.refs_1_
  15.0 1.2 %collective-permute-done.1.refs_2_ = bf16[2,2,128,128]{3,2,1,0:T(8,128)(2,1)S(1)} collective-permute-done((bf16[2,2,128,128]{3,2,1,0:T(8,128)(2,1)S(1)}, bf16[2,2,128,128]{3,2,1,0:T(8,128)(2,1)S(1)}, u32[]{:S(2)}, u32[]{:S(2)}) %collective-permute-start.1) | collective-permute-done | bytes 131104 | tf_op jit(solution)/shard_map/ppermute | solution.py:285
  16.2 0.0 collective-permute-done.2.refs_3_
  16.2 0.1 choose.1
  16.3 0.1 collective-permute-start.3
  16.4 1.5 %collective-permute-done.3.refs_4_ = bf16[2,2,2,128,128]{4,3,2,1,0:T(8,128)(2,1)S(1)} collective-permute-done((bf16[2,2,2,128,128]{4,3,2,1,0:T(8,128)(2,1)S(1)}, bf16[2,2,2,128,128]{4,3,2,1,0:T(8,128)(2,1)S(1)}, u32[]{:S(2)}, u32[]{:S(2)}) %collective-permute-start.3) | collective-permute-done | bytes 262176 | tf_op jit(solution)/shard_map/ppermute | solution.py:288
  17.9 2.5 %listed_keys.1.mine_ref = bf16[2,2,2,128,128]{4,3,2,1,0:T(8,128)(2,1)S(1)} custom-call(s32[8,128]{1,0:T(8,128)S(1)} %get-tuple-element.17.places_ref, bf16[2,2,128,128]{3,2,1,0:T(8,128)(2,1)S(1)} %pack.1.refs_0_, bf16[2,2,128,128]{3,2,1,0:T(8,128)(2,1)S(1)} %collective-permute-done.refs_1_, bf16[2,2,128,128]{3,2,1,0:T(8,128)(2,1)S(1)} %collective-permute-done.1.refs_2_, ...), custom_call_target="tpu_custom_call" | custom-call | flops 1073741824 | bytes 2097152 | tf_op jit(solution)/shard_map/listed_keys/pallas_call | solution.py:358
  20.4 0.2 collective-permute-start.4
  20.6 1.4 %collective-permute-done.4.other_ref = bf16[2,2,2,128,128]{4,3,2,1,0:T(8,128)(2,1)S(1)} collective-permute-done((bf16[2,2,2,128,128]{4,3,2,1,0:T(8,128)(2,1)S(1)}, bf16[2,2,2,128,128]{4,3,2,1,0:T(8,128)(2,1)S(1)}, u32[]{:S(2)}, u32[]{:S(2)}) %collective-permute-start.4) | collective-permute-done | bytes 262176 | tf_op jit(solution)/shard_map/ppermute | solution.py:288
  22.0 0.4 %combine.1 = (f32[2,2,128,128]{3,2,1,0:T(8,128)S(1)}, bf16[2,2,128,128]{3,2,1,0:T(8,128)(2,1)S(1)}, bf16[2,2,128,128]{3,2,1,0:T(8,128)(2,1)S(1)}, bf16[2,2,128,128]{3,2,1,0:T(8,128)(2,1)S(1)}) custom-call(s32[8,128]{1,0:T(8,128)S(1)} %get-tuple-element.17.places_ref, bf16[2,2,2,128,128]{4,3,2,1,0:T(8,128)(2,1)S(1)} %listed_keys.1.mine_ref, ...), custom_call_target="tpu_custom_call" | custom-call | tf_op jit(solution)/shard_map/combine/pallas_call | solution.py:368
  22.4 3.3 %collective-permute-start.5 = (bf16[2,2,128,128]{3,2,1,0:T(8,128)(2,1)S(1)}, bf16[2,2,128,128]{3,2,1,0:T(8,128)(2,1)S(1)}, u32[]{:S(2)}, u32[]{:S(2)}) collective-permute-start(bf16[2,2,128,128]{3,2,1,0:T(8,128)(2,1)S(1)} %get-tuple-element.26), channel_id=1, source_target_pairs={{0,4},{4,8},{8,12},{12,0},{1,5},{5,9},{9,13},{13,1},{2,6},{6,10},{... | collective-permute-start | bytes 393224 | tf_op jit(solution)/shard_map/ppermute | solution.py:285
  25.7 1.6 %collective-permute-start.6 = (bf16[2,2,128,128]{3,2,1,0:T(8,128)(2,1)S(1)}, bf16[2,2,128,128]{3,2,1,0:T(8,128)(2,1)S(1)}, u32[]{:S(2)}, u32[]{:S(2)}) collective-permute-start(bf16[2,2,128,128]{3,2,1,0:T(8,128)(2,1)S(1)} %get-tuple-element.27), channel_id=1, source_target_pairs={{0,8},{4,12},{8,0},{12,4},{1,9},{5,13},{9,1},{13,5},{2,10},{6,14},... | collective-permute-start | bytes 393224 | tf_op jit(solution)/shard_map/ppermute | solution.py:285
  27.4 0.8 %collective-permute-start.7 = (bf16[2,2,128,128]{3,2,1,0:T(8,128)(2,1)S(1)}, bf16[2,2,128,128]{3,2,1,0:T(8,128)(2,1)S(1)}, u32[]{:S(2)}, u32[]{:S(2)}) collective-permute-start(bf16[2,2,128,128]{3,2,1,0:T(8,128)(2,1)S(1)} %get-tuple-element.28), channel_id=1, source_target_pairs={{0,12},{4,0},{8,4},{12,8},{1,13},{5,1},{9,5},{13,9},{2,14},{6,2},{... | collective-permute-start | bytes 393224 | tf_op jit(solution)/shard_map/ppermute | solution.py:285
  28.2 4.5 %listed_queries.1 = f32[128,32,128]{2,1,0:T(8,128)} custom-call(s32[8,128]{1,0:T(8,128)S(1)} %get-tuple-element.17.places_ref, bf16[2,2,128,128]{3,2,1,0:T(8,128)(2,1)S(1)} %pack.1.refs_0_, bf16[2,2,128,128]{3,2,1,0:T(8,128)(2,1)S(1)} %collective-permute-done.refs_1_, bf16[2,2,128,128]{3,2,1,0:T(8,128)(2,1)S(1)} %collective-permute-done.1.refs_2_, ...), custom_call_target="tpu_custom_call" | custom-call | flops 805306368 | bytes 6291456 | tf_op jit(solution)/shard_map/listed_queries/pallas_call | solution.py:380
  32.7 0.0 collective-permute-done.5.refs_1_
  32.7 3.6 %collective-permute-done.6.refs_2_ = bf16[2,2,128,128]{3,2,1,0:T(8,128)(2,1)S(1)} collective-permute-done((bf16[2,2,128,128]{3,2,1,0:T(8,128)(2,1)S(1)}, bf16[2,2,128,128]{3,2,1,0:T(8,128)(2,1)S(1)}, u32[]{:S(2)}, u32[]{:S(2)}) %collective-permute-start.6) | collective-permute-done | bytes 131104 | tf_op jit(solution)/shard_map/ppermute | solution.py:285
  36.3 0.0 collective-permute-done.7.refs_3_
  36.3 0.8 %total.1 = (f32[128,2,128]{2,1,0:T(2,128)}, f32[128,2,128]{2,1,0:T(2,128)}) custom-call(f32[2,2,128,128]{3,2,1,0:T(8,128)S(1)} %get-tuple-element.22.refs_4_.refs_5_.near_ref, f32[2,2,128,128]{3,2,1,0:T(8,128)S(1)} %get-tuple-element.25.refs_9_.refs_0_, bf16[2,2,128,128]{3,2,1,0:T(8,128)(2,1)S(1)} %collective-permute-done.5.refs_1_, ...), custom_call_target="tpu_custom_call" | custom-call | tf_op jit(solution)/shard_map/total/pallas_call | solution.py:390
Async XLA Ops:
  1.9 13.1 %collective-permute-start = (bf16[2,2,128,128]{3,2,1,0:T(8,128)(2,1)S(1)}, bf16[2,2,128,128]{3,2,1,0:T(8,128)(2,1)S(1)}, u32[]{:S(2)}, u32[]{:S(2)}) collective-permute-start(bf16[2,2,128,128]{3,2,1,0:T(8,128)(2,1)S(1)} %pack.1.refs_0_), channel_id=1, source_target_pairs={{0,4},{4,8},{8,12},{12,0},{1,5},{5,9},{9,13},{13,1},{2,6},{6,10},{... | collective-permute-start | bytes 393224 | tf_op jit(solution)/shard_map/ppermute | solution.py:285
  5.0 11.2 %collective-permute-start.1 = (bf16[2,2,128,128]{3,2,1,0:T(8,128)(2,1)S(1)}, bf16[2,2,128,128]{3,2,1,0:T(8,128)(2,1)S(1)}, u32[]{:S(2)}, u32[]{:S(2)}) collective-permute-start(bf16[2,2,128,128]{3,2,1,0:T(8,128)(2,1)S(1)} %pack.1.refs_0_), channel_id=1, source_target_pairs={{0,8},{4,12},{8,0},{12,4},{1,9},{5,13},{9,1},{13,5},{2,10},{6,14},... | collective-permute-start | bytes 393224 | tf_op jit(solution)/shard_map/ppermute | solution.py:285
  7.5 8.6 %collective-permute-start.2 = (bf16[2,2,128,128]{3,2,1,0:T(8,128)(2,1)S(1)}, bf16[2,2,128,128]{3,2,1,0:T(8,128)(2,1)S(1)}, u32[]{:S(2)}, u32[]{:S(2)}) collective-permute-start(bf16[2,2,128,128]{3,2,1,0:T(8,128)(2,1)S(1)} %pack.1.refs_0_), channel_id=1, source_target_pairs={{0,12},{4,0},{8,4},{12,8},{1,13},{5,1},{9,5},{13,9},{2,14},{6,2},{... | collective-permute-start | bytes 393224 | tf_op jit(solution)/shard_map/ppermute | solution.py:285
  16.3 1.6 %collective-permute-start.3 = (bf16[2,2,2,128,128]{4,3,2,1,0:T(8,128)(2,1)S(1)}, bf16[2,2,2,128,128]{4,3,2,1,0:T(8,128)(2,1)S(1)}, u32[]{:S(2)}, u32[]{:S(2)}) collective-permute-start(bf16[2,2,2,128,128]{4,3,2,1,0:T(8,128)(2,1)S(1)} %choose.1), channel_id=1, source_target_pairs={{0,1},{1,0},{2,3},{3,2},{4,5},{5,4},{6,7},{7,6},{8,9},{9,8},{10,11... | collective-permute-start | bytes 786440 | tf_op jit(solution)/shard_map/ppermute | solution.py:288
  20.4 1.6 %collective-permute-start.4 = (bf16[2,2,2,128,128]{4,3,2,1,0:T(8,128)(2,1)S(1)}, bf16[2,2,2,128,128]{4,3,2,1,0:T(8,128)(2,1)S(1)}, u32[]{:S(2)}, u32[]{:S(2)}) collective-permute-start(bf16[2,2,2,128,128]{4,3,2,1,0:T(8,128)(2,1)S(1)} %listed_keys.1.mine_ref), channel_id=1, source_target_pairs={{0,1},{1,0},{2,3},{3,2},{4,5},{5,4},{6,7},{7,6},{8,9},{9,8},{10,11... | collective-permute-start | bytes 786440 | tf_op jit(solution)/shard_map/ppermute | solution.py:288
  22.4 10.3 %collective-permute-start.5 = (bf16[2,2,128,128]{3,2,1,0:T(8,128)(2,1)S(1)}, bf16[2,2,128,128]{3,2,1,0:T(8,128)(2,1)S(1)}, u32[]{:S(2)}, u32[]{:S(2)}) collective-permute-start(bf16[2,2,128,128]{3,2,1,0:T(8,128)(2,1)S(1)} %get-tuple-element.26), channel_id=1, source_target_pairs={{0,4},{4,8},{8,12},{12,0},{1,5},{5,9},{9,13},{13,1},{2,6},{6,10},{... | collective-permute-start | bytes 393224 | tf_op jit(solution)/shard_map/ppermute | solution.py:285
  25.7 10.6 %collective-permute-start.6 = (bf16[2,2,128,128]{3,2,1,0:T(8,128)(2,1)S(1)}, bf16[2,2,128,128]{3,2,1,0:T(8,128)(2,1)S(1)}, u32[]{:S(2)}, u32[]{:S(2)}) collective-permute-start(bf16[2,2,128,128]{3,2,1,0:T(8,128)(2,1)S(1)} %get-tuple-element.27), channel_id=1, source_target_pairs={{0,8},{4,12},{8,0},{12,4},{1,9},{5,13},{9,1},{13,5},{2,10},{6,14},... | collective-permute-start | bytes 393224 | tf_op jit(solution)/shard_map/ppermute | solution.py:285
  27.4 8.9 %collective-permute-start.7 = (bf16[2,2,128,128]{3,2,1,0:T(8,128)(2,1)S(1)}, bf16[2,2,128,128]{3,2,1,0:T(8,128)(2,1)S(1)}, u32[]{:S(2)}, u32[]{:S(2)}) collective-permute-start(bf16[2,2,128,128]{3,2,1,0:T(8,128)(2,1)S(1)} %get-tuple-element.28), channel_id=1, source_target_pairs={{0,12},{4,0},{8,4},{12,8},{1,13},{5,1},{9,5},{13,9},{2,14},{6,2},{... | collective-permute-start | bytes 393224 | tf_op jit(solution)/shard_map/ppermute | solution.py:285

commit v2 on v1

--- a/solution.py
+++ b/solution.py
@@ -11,7 +11,6 @@
 KVH = 4
 LOG2E = 1.4426950408889634
 ROWS = 512
-PARTS = 1
 VMEM_LIMIT = 24 * 1024 * 1024
 
 VMEM_SPEC = pl.BlockSpec(memory_space=pltpu.VMEM)
@@ -68,14 +67,12 @@
         yield toks, cols, *(held_ref[kind, head, toks].reshape(rows, head_dim) for kind in range(2))
 
 
-def pack_kernel(key_ref, value_ref, *refs):
-    *kv_refs, held_ref, sems = refs
-    each = kv_refs[0].shape[1]
+def pack_kernel(key_ref, value_ref, kv_ref, held_ref, sems):
     copies = start_all((key_ref, value_ref), (held_ref.at[0], held_ref.at[1]), sems)
     for kind, copy in enumerate(copies):
         copy.wait()
         for head in range(held_ref.shape[2]):
-            kv_refs[head // each][kind, head % each] = held_ref[kind, :, head, :]
+            kv_ref[kind, head] = held_ref[kind, :, head, :]
 
 
 def spread_kernel(
@@ -112,7 +109,7 @@
 
     (mine, mine_sub), (other, other_sub) = listed_by(sub), listed_by(1 - sub)
     places_ref[0:2] = around(ctx - other)
-    places_ref[2:4] = jnp.where(mine_sub == sub, around(ctx - mine), ring)
+    places_ref[2:4] = around(ctx - mine) + jnp.where(mine_sub == sub, 0, ring)
     places_ref[4:6] = jnp.where(mine_sub == sub, around(mine - ctx), ring)
     places_ref[6:8] = jnp.where(other_sub == sub, around(other - ctx), ring)
 
@@ -136,46 +133,46 @@
     doc_col_ref[...] = jnp.broadcast_to(docs, (tokens, tokens)).T
 
 
-def pick_block(sources, row):
-    chosen = sources[0].astype(jnp.float32)
-    for step in range(1, len(sources)):
-        chosen = jnp.where(row == step, sources[step].astype(jnp.float32), chosen)
+def pick_block(first, others, row):
+    chosen = first.astype(jnp.float32)
+    for code, block in others:
+        chosen = jnp.where(row == code, block.astype(jnp.float32), chosen)
     return chosen.astype(jnp.bfloat16)
 
 
-def choose_kernel(places_ref, *refs):
-    *column, _, _, out_ref = refs
+def choose_kernel(shifts, places_ref, *refs):
+    *column, _, out_ref = refs
     for which in range(2):
         row = places_ref[which:which + 1]
         for kind in range(2):
             for head in range(out_ref.shape[2]):
-                out_ref[which, kind, head] = pick_block([ref[kind, head] for ref in column], row)
-
-
-def far_blocks(places_ref, column, other_ref, head):
-    return [
-        jnp.concatenate(
-            [
-                pick_block(
-                    [ref[kind, head] for ref in column] + [other_ref[which, kind, head]],
-                    places_ref[2 + which:3 + which],
-                )
-                for which in range(2)
-            ],
-            axis=0,
-        )
-        for kind in range(2)
-    ]
-
-
-def local_kernel(factor, rows, *refs):
-    *kv_refs, query_ref, up_ref, norm_ref, term_ref, docs_ref, doc_col_ref, dkv_ref, dq_ref, held_ref, sems = refs
+                blocks = [(shift, ref[kind, head]) for shift, ref in zip(shifts, column)]
+                out_ref[which, kind, head] = pick_block(blocks[0][1], blocks[1:], row)
+
+
+def far_blocks(groups, ring, places_ref, column, others, head):
+    held = []
+    for kind in range(2):
+        pair = []
+        for which in range(2):
+            given = [
+                (ring + shift, other_ref[which, kind, head])
+                for shifts, other_ref in zip(groups[1:], others[1:]) for shift in shifts
+            ]
+            own = [(shift, ref[kind, head]) for shift, ref in zip(sum(groups, []), column)]
+            pair.append(pick_block(others[0][which, kind, head], given + own, places_ref[2 + which:3 + which]))
+        held.append(jnp.concatenate(pair, axis=0))
+    return held
+
+
+def local_kernel(
+    factor, rows, kv_ref, query_ref, up_ref, norm_ref, term_ref, docs_ref, doc_col_ref, dkv_ref, dq_ref, held_ref, sems
+):
     copies = bring_rows(query_ref, up_ref, held_ref, sems, rows)
     tokens, grouped, head_dim = held_ref.shape[2:]
-    each = kv_refs[0].shape[1]
     doc_col = jnp.concatenate([doc_col_ref[...]] * (rows // tokens), axis=1)
     for head in range(held_ref.shape[1]):
-        key_blk, value_blk = kv_refs[head // each][0, head % each], kv_refs[head // each][1, head % each]
+        key_blk, value_blk = kv_ref[0, head], kv_ref[1, head]
         grad_key = jnp.zeros((tokens, head_dim), jnp.float32)
         grad_val = jnp.zeros((tokens, head_dim), jnp.float32)
         for toks, cols, query_blk, upstream in row_blocks(held_ref, head, rows, copies):
@@ -199,17 +196,17 @@
         dkv_ref[1, head] = grad_val
 
 
-def listed_kernel(factor, rows, first, places_ref, *refs):
-    *column, other_ref, held_ref, norm_ref, term_ref, dkv_ref = refs
+def listed_kernel(factor, rows, shifts, ring, places_ref, *refs):
+    *column, other_ref, held_ref, norm_ref, term_ref, _, dkv_ref = refs
     tokens, grouped, head_dim = held_ref.shape[2:]
     for head in range(other_ref.shape[2]):
-        key_blk, value_blk = far_blocks(places_ref, column, other_ref, head)
+        key_blk, value_blk = far_blocks([shifts], ring, places_ref, column, [other_ref], head)
         grad_key = jnp.zeros((2 * tokens, head_dim), jnp.float32)
         grad_val = jnp.zeros((2 * tokens, head_dim), jnp.float32)
-        for toks, cols, query_blk, upstream in row_blocks(held_ref, first + head, rows):
+        for toks, cols, query_blk, upstream in row_blocks(held_ref, head, rows):
             probs, grads = tile_terms(
                 key_blk, value_blk, query_blk, upstream,
-                norm_ref[first + head, :, cols], term_ref[first + head, :, cols], None, factor,
+                norm_ref[head, :, cols], term_ref[head, :, cols], None, factor,
             )
             grad_val += jnp.dot(probs, upstream, preferred_element_type=jnp.float32)
             grad_key += jnp.dot(grads, query_blk, preferred_element_type=jnp.float32)
@@ -220,14 +217,12 @@
             dkv_ref[which, 1, head] = grad_val[which * tokens:(which + 1) * tokens]
 
 
-def query_kernel(factor, rows, parts, places_ref, *refs):
+def query_kernel(factor, rows, groups, ring, places_ref, *refs):
     *inputs, held_ref, norm_ref, term_ref, near_ref, _, dq_ref = refs
     tokens, grouped, head_dim = held_ref.shape[2:]
-    size = len(inputs) // parts
-    each = held_ref.shape[1] // parts
+    column, others = inputs[:ring], inputs[ring:]
     for head in range(held_ref.shape[1]):
-        *column, other_ref = inputs[head // each * size:(head // each + 1) * size]
-        key_blk, value_blk = far_blocks(places_ref, column, other_ref, head % each)
+        key_blk, value_blk = far_blocks(groups, ring, places_ref, column, others, head)
         for toks, cols, query_blk, upstream in row_blocks(held_ref, head, rows):
             _, grads = tile_terms(
                 key_blk, value_blk, query_blk, upstream, norm_ref[head, :, cols], term_ref[head, :, cols],
@@ -242,29 +237,26 @@
             )
 
 
-def combine_kernel(places_ref, mine_ref, other_ref, *out_refs):
-    for step, out_ref in enumerate(out_refs):
+def combine_kernel(shifts, places_ref, mine_ref, other_ref, *refs):
+    for shift, out_ref in zip(shifts, refs[1:]):
         for kind in range(2):
             for head in range(out_ref.shape[1]):
                 total = None
                 for i, ref in enumerate((mine_ref, other_ref)):
                     for which in range(2):
                         row = places_ref[4 + 2 * i + which:5 + 2 * i + which]
-                        term = jnp.where(row == step, ref[which, kind, head].astype(jnp.float32), 0.0)
+                        term = jnp.where(row == shift, ref[which, kind, head].astype(jnp.float32), 0.0)
                         total = term if total is None else total + term
                 out_ref[kind, head] = total.astype(out_ref.dtype)
 
 
-def total_kernel(parts, near_ref, *refs):
+def total_kernel(near_ref, *refs):
     *blocks, dk_ref, dv_ref = refs
-    count = len(blocks) // parts
-    heads = dk_ref.shape[1]
-    each = heads // parts
     for kind, out_ref in enumerate((dk_ref, dv_ref)):
-        for head in range(heads):
+        for head in range(out_ref.shape[1]):
             total = near_ref[kind, head]
-            for ref in blocks[head // each * count:(head // each + 1) * count]:
-                total += ref[kind, head % each].astype(jnp.float32)
+            for ref in blocks:
+                total += ref[kind, head].astype(jnp.float32)
             out_ref[:, head, :] = total
 
 
@@ -277,9 +269,9 @@
     subs = lax.axis_size("sub")
     rows = min(ROWS, tokens * grouped)
     cols = tokens * grouped
-    parts = PARTS if kv_heads % PARTS == 0 else 1
-    each = kv_heads // parts
-    span_shape = (2, each, tokens, head_dim)
+    span_shape = (2, kv_heads, tokens, head_dim)
+    near = [shift for shift in range(1, ring) if min(shift, ring - shift) <= ring // 4]
+    groups = [[shift for shift in range(ring) if shift not in near], near]
 
     def shifted(array, shift):
         return lax.ppermute(array, "ctx", [(i, (i + shift) % ring) for i in range(ring)])
@@ -294,13 +286,13 @@
     kv = pl.pallas_call(
         pack_kernel,
         in_specs=[HBM_SPEC] * 2,
-        out_specs=[VMEM_SPEC] * parts,
-        out_shape=[jax.ShapeDtypeStruct(span_shape, jnp.bfloat16)] * parts,
+        out_specs=VMEM_SPEC,
+        out_shape=jax.ShapeDtypeStruct(span_shape, jnp.bfloat16),
         scratch_shapes=[pltpu.VMEM((2, *keys.shape), jnp.bfloat16), pltpu.SemaphoreType.DMA((2,))],
         compiler_params=params,
         name="pack",
     )(*in_hbm(keys, values))
-    columns = [[block] + [shifted(block, shift) for shift in range(1, ring)] for block in kv]
+    columns = [[shifted(kv, shift) if shift else kv for shift in shifts] for shifts in groups]
 
     norm, term, docs, doc_col, places = pl.pallas_call(
         functools.partial(spread_kernel, grouped, ring, subs),
@@ -329,7 +321,7 @@
     row_specs = [VMEM_SPEC] * 3
     near_kv, near_query, held = pl.pallas_call(
         functools.partial(local_kernel, factor, rows),
-        in_specs=[VMEM_SPEC] * parts + [HBM_SPEC] * 2 + [VMEM_SPEC] * 4,
+        in_specs=[VMEM_SPEC] + [HBM_SPEC] * 2 + [VMEM_SPEC] * 4,
         out_specs=[VMEM_SPEC] * 3,
         out_shape=[
             jax.ShapeDtypeStruct((2, kv_heads, tokens, head_dim), jnp.float32),
@@ -340,56 +332,66 @@
         compiler_params=params,
         cost_estimate=pl.CostEstimate(flops=5 * work, bytes_accessed=2 * moved, transcendentals=0),
         name="local_block",
-    )(*kv, *in_hbm(queries, grad_out), norm, term, docs, doc_col)
-
-    inputs, sums = [], []
-    after = near_kv
-    for part, column in enumerate(columns):
-        chosen = pl.pallas_call(
-            choose_kernel,
-            in_specs=[VMEM_SPEC] * (ring + 1) + [ANY_SPEC] * 2,
+    )(kv, *in_hbm(queries, grad_out), norm, term, docs, doc_col)
+
+    def choose(group, after):
+        return pl.pallas_call(
+            functools.partial(choose_kernel, groups[group]),
+            in_specs=[VMEM_SPEC] * (len(groups[group]) + 1) + [ANY_SPEC],
             out_specs=VMEM_SPEC,
             out_shape=jax.ShapeDtypeStruct((2, *span_shape), jnp.bfloat16),
             compiler_params=params,
             name="choose",
-        )(places, *column, near_kv, after)
-        other = swapped(chosen)
-        inputs += [*column, other]
-        far_kv = pl.pallas_call(
-            functools.partial(listed_kernel, factor, rows, part * each),
-            in_specs=[VMEM_SPEC] * (ring + 2) + row_specs,
+        )(places, *columns[group], after)
+
+    def listed(group, other, after):
+        return pl.pallas_call(
+            functools.partial(listed_kernel, factor, rows, groups[group], ring),
+            in_specs=[VMEM_SPEC] * (len(groups[group]) + 2) + row_specs + [ANY_SPEC],
             out_specs=VMEM_SPEC,
             out_shape=jax.ShapeDtypeStruct((2, *span_shape), jnp.bfloat16),
             compiler_params=params,
-            cost_estimate=pl.CostEstimate(flops=8 * work // parts, bytes_accessed=moved // parts, transcendentals=0),
+            cost_estimate=pl.CostEstimate(flops=8 * work, bytes_accessed=moved, transcendentals=0),
             name="listed_keys",
-        )(places, *column, other, held, norm, term)
-        other_kv = swapped(far_kv)
-        blocks = pl.pallas_call(
-            combine_kernel,
-            in_specs=[VMEM_SPEC] * 3,
-            out_specs=[VMEM_SPEC] * ring,
-            out_shape=[jax.ShapeDtypeStruct(span_shape, jnp.float32)]
-            + [jax.ShapeDtypeStruct(span_shape, jnp.bfloat16)] * (ring - 1),
+        )(places, *columns[group], other, held, norm, term, after)
+
+    def combine(group, far_kv, other_kv, after):
+        return pl.pallas_call(
+            functools.partial(combine_kernel, groups[group]),
+            in_specs=[VMEM_SPEC] * 3 + [ANY_SPEC],
+            out_specs=[VMEM_SPEC] * len(groups[group]),
+            out_shape=[
+                jax.ShapeDtypeStruct(span_shape, jnp.bfloat16 if shift else jnp.float32) for shift in groups[group]
+            ],
             compiler_params=params,
             name="combine",
-        )(places, far_kv, other_kv)
-        sums += [blocks[0]] + [shifted(blocks[shift], shift) for shift in range(1, ring)]
-        after = blocks[0]
+        )(places, far_kv, other_kv, after)
+
+    chosen = choose(0, near_kv)
+    others = [swapped(chosen)]
+    far_kv = listed(0, others[0], near_kv)
+    other_kv = swapped(far_kv)
+    chosen = choose(1, far_kv)
+    others.append(swapped(chosen))
+    blocks = combine(0, far_kv, other_kv, chosen)
+    sums = [shifted(block, shift) if shift else block for shift, block in zip(groups[0], blocks)]
+    far_kv = listed(1, others[1], blocks[0])
+    blocks = combine(1, far_kv, swapped(far_kv), far_kv)
+    sums += [shifted(block, shift) for shift, block in zip(groups[1], blocks)]
 
     grad_queries = pl.pallas_call(
-        functools.partial(query_kernel, factor, rows, parts),
-        in_specs=[VMEM_SPEC] * (1 + len(inputs)) + row_specs + [VMEM_SPEC, ANY_SPEC],
+        functools.partial(query_kernel, factor, rows, groups, ring),
+        in_specs=[VMEM_SPEC] * (1 + ring + len(groups)) + row_specs + [VMEM_SPEC, ANY_SPEC],
         out_specs=VMEM_SPEC,
         out_shape=jax.ShapeDtypeStruct((tokens, heads, head_dim), jnp.float32),
         compiler_params=params,
         cost_estimate=pl.CostEstimate(flops=6 * work, bytes_accessed=3 * moved, transcendentals=0),
         name="listed_queries",
-    )(places, *inputs, held, norm, term, near_query, after)
+    )(places, *columns[0], *columns[1], *others, held, norm, term, near_query, blocks[0])
 
     grad_keys, grad_values = pl.pallas_call(
-        functools.partial(total_kernel, parts),
-        in_specs=[VMEM_SPEC] * (parts * ring + 1),
+        total_kernel,
+        in_specs=[VMEM_SPEC] * (ring + 1),
         out_specs=[VMEM_SPEC] * 2,
         out_shape=[jax.ShapeDtypeStruct((tokens, kv_heads, head_dim), jnp.float32)] * 2,
         compiler_params=params,

time: 37.8 us -> 41 us (1.085)
  Pallas kernels: 15.7 us -> 18.1 us
  waiting for transfers between devices: 7.72 us -> 8.3 us
  starting transfers between devices: 13.1 us -> 13.6 us
    pallas_call x6 -> x9, Pallas kernels: 9.57 us -> 12 us  [the longest x2 4.86 us: listed(): pl.pallas_call(functools.partial(listed_kernel, factor, rows, groups[grou...]
    ppermute x6, waiting for transfers between devices: 4.8 us -> 6.89 us  [shifted(): lax.ppermute(array, 'ctx', [(i, (i + shift) % ring) for i in range(ring)])]
    ppermute x2 -> x4, waiting for transfers between devices: 2.92 us -> 1.41 us  [swapped(): return lax.ppermute(array, 'sub', [(i, i ^ 1) for i in range(subs)])]
  transfers between devices with their start and end apart: 8 -> 10, of which waited for: 4 -> 7; matrix products, arithmetic and copies ran while one was open for 0% -> 0% of each run, Pallas kernels for 29% -> 33%
where the time goes in v2:
time: 41 us; the launch traced here: 40.7 us
  Pallas kernels  18.1 us (44%)
  starting transfers between devices  13.6 us (33%)
  waiting for transfers between devices  8.3 us (20%)
  between operations  0.72 us (2%)
    ppermute x6, starting transfers between devices, shifted(): lax.ppermute(array, 'ctx', [(i, (i + shift) % ring) for i in range(ring)])  13.2 us
    ppermute x6, waiting for transfers between devices, shifted(): lax.ppermute(array, 'ctx', [(i, (i + shift) % ring) for i in range(ring)])  6.89 us
    pallas_call x1, Pallas kernels, body(): pl.pallas_call(functools.partial(local_kernel, factor, rows), in_specs=[V...  4.95 us
    pallas_call x2, Pallas kernels, listed(): pl.pallas_call(functools.partial(listed_kernel, factor, rows, groups[grou...  4.86 us
    pallas_call x1, Pallas kernels, body(): pl.pallas_call(functools.partial(query_kernel, factor, rows, groups, ring...  4.54 us
    ppermute x4, waiting for transfers between devices, swapped(): return lax.ppermute(array, 'sub', [(i, i ^ 1) for i in range(subs)])  1.41 us
    pallas_call x1, Pallas kernels, body(): pl.pallas_call(pack_kernel, in_specs=[HBM_SPEC] * 2, out_specs=VMEM_SPEC,...  1.24 us
    pallas_call x1, Pallas kernels, body(): pl.pallas_call(functools.partial(spread_kernel, grouped, ring, subs), in_...  1.17 us
  transfers between devices with their start and end apart: 10, of which 7 were waited for; matrix products, arithmetic and copies ran while one was open for 0% of the time, Pallas kernels for 33%

profile of v2, /device:TPU:0, one launch (start us, length us, event | category | flops | bytes accessed | tf_op | source)
XLA Modules:
  0.0 40.7 jit_solution(12183568031916562842)
XLA Ops:
  0.6 1.2 %pack.1.kv_ref.refs_0_ = bf16[2,2,128,128]{3,2,1,0:T(8,128)(2,1)S(1)} custom-call(bf16[128,2,128]{2,1,0:T(2,128)(2,1)} %key_ref.1, bf16[128,2,128]{2,1,0:T(2,128)(2,1)} %value_ref.1), custom_call_target="tpu_custom_call" | custom-call | tf_op jit(solution)/shard_map/pack/pallas_call | solution.py:286
  1.9 4.1 %collective-permute-start = (bf16[2,2,128,128]{3,2,1,0:T(8,128)(2,1)S(1)}, bf16[2,2,128,128]{3,2,1,0:T(8,128)(2,1)S(1)}, u32[]{:S(2)}, u32[]{:S(2)}) collective-permute-start(bf16[2,2,128,128]{3,2,1,0:T(8,128)(2,1)S(1)} %pack.1.kv_ref.refs_0_), channel_id=1, source_target_pairs={{0,8},{4,12},{8,0},{12,4},{1,9},{5,13},{9,1},{13,5},{2,10},{6,14},... | collective-permute-start | bytes 393224 | tf_op jit(solution)/shard_map/ppermute | solution.py:277
  6.0 1.2 %spread.1 = (f32[2,1,2048]{2,1,0:T(1,128)S(1)}, f32[2,1,2048]{2,1,0:T(1,128)S(1)}, f32[1,2048]{1,0:T(1,128)S(1)}, f32[128,128]{1,0:T(8,128)S(1)}, s32[8,128]{1,0:T(8,128)S(1)}) custom-call(f32[32,128]{1,0:T(8,128)} %bitcast.4, f32[32,128]{1,0:T(8,128)} %bitcast.5, s32[1,128]{1,0:T(1,128)} %bitcast.7, s32[2,8]{1,0:T(2,128)} %bitcast.6), custom_call_target="tpu_custom_call" | custom-call | tf_op jit(solution)/shard_map/spread/pallas_call | solution.py:297
  7.2 5.0 %local_block.1 = (f32[2,2,128,128]{3,2,1,0:T(8,128)S(1)}, f32[128,32,128]{2,1,0:T(8,128)S(1)}, bf16[2,2,128,16,128]{4,3,2,1,0:T(8,128)(2,1)S(1)}) custom-call(bf16[2,2,128,128]{3,2,1,0:T(8,128)(2,1)S(1)} %pack.1.kv_ref.refs_0_, bf16[128,32,128]{2,1,0:T(8,128)(2,1)} %query_ref.1, bf16[128,32,128]{2,1,0:T(8,128)(2,1)} %up_ref.1, ...), custom_call_target="tpu_custom_call" | custom-call | flops 671088640 | bytes 4194304 | tf_op jit(solution)/shard_map/local_block/pallas_call | solution.py:322
  12.1 0.2 collective-permute-done.refs_1_
  12.3 0.1 choose.2
  12.4 0.1 collective-permute-start.3
  12.4 1.5 %collective-permute-start.1 = (bf16[2,2,128,128]{3,2,1,0:T(8,128)(2,1)S(1)}, bf16[2,2,128,128]{3,2,1,0:T(8,128)(2,1)S(1)}, u32[]{:S(2)}, u32[]{:S(2)}) collective-permute-start(bf16[2,2,128,128]{3,2,1,0:T(8,128)(2,1)S(1)} %pack.1.kv_ref.refs_0_), channel_id=1, source_target_pairs={{0,4},{4,8},{8,12},{12,0},{1,5},{5,9},{9,13},{13,1},{2,6},{6,10},{... | collective-permute-start | bytes 393224 | tf_op jit(solution)/shard_map/ppermute | solution.py:277
  13.9 2.4 %collective-permute-start.2 = (bf16[2,2,128,128]{3,2,1,0:T(8,128)(2,1)S(1)}, bf16[2,2,128,128]{3,2,1,0:T(8,128)(2,1)S(1)}, u32[]{:S(2)}, u32[]{:S(2)}) collective-permute-start(bf16[2,2,128,128]{3,2,1,0:T(8,128)(2,1)S(1)} %pack.1.kv_ref.refs_0_), channel_id=1, source_target_pairs={{0,12},{4,0},{8,4},{12,8},{1,13},{5,1},{9,5},{13,9},{2,14},{6,2},{... | collective-permute-start | bytes 393224 | tf_op jit(solution)/shard_map/ppermute | solution.py:277
  16.3 0.0 collective-permute-done.3.refs_2_.refs_4_
  16.3 2.4 %listed_keys.2.refs_2_.mine_ref = bf16[2,2,2,128,128]{4,3,2,1,0:T(8,128)(2,1)S(1)} custom-call(s32[8,128]{1,0:T(8,128)S(1)} %get-tuple-element.17.places_ref, bf16[2,2,128,128]{3,2,1,0:T(8,128)(2,1)S(1)} %pack.1.kv_ref.refs_0_, bf16[2,2,128,128]{3,2,1,0:T(8,128)(2,1)S(1)} %collective-permute-done.refs_1_, ...), custom_call_target="tpu_custom_call" | custom-call | flops 1073741824 | bytes 2097152 | tf_op jit(solution)/shard_map/listed_keys/pallas_call | solution.py:348
  18.7 0.1 collective-permute-start.5
  18.8 1.8 %collective-permute-done.1.refs_0_.refs_2_ = bf16[2,2,128,128]{3,2,1,0:T(8,128)(2,1)S(1)} collective-permute-done((bf16[2,2,128,128]{3,2,1,0:T(8,128)(2,1)S(1)}, bf16[2,2,128,128]{3,2,1,0:T(8,128)(2,1)S(1)}, u32[]{:S(2)}, u32[]{:S(2)}) %collective-permute-start.1) | collective-permute-done | bytes 131104 | tf_op jit(solution)/shard_map/ppermute | solution.py:277
  20.6 1.6 %collective-permute-done.2.refs_1_.refs_3_ = bf16[2,2,128,128]{3,2,1,0:T(8,128)(2,1)S(1)} collective-permute-done((bf16[2,2,128,128]{3,2,1,0:T(8,128)(2,1)S(1)}, bf16[2,2,128,128]{3,2,1,0:T(8,128)(2,1)S(1)}, u32[]{:S(2)}, u32[]{:S(2)}) %collective-permute-start.2) | collective-permute-done | bytes 131104 | tf_op jit(solution)/shard_map/ppermute | solution.py:277
  22.3 0.1 choose.3.refs_0_
  22.3 0.1 collective-permute-start.4
  22.4 0.0 collective-permute-done.5.other_ref
  22.4 0.2 combine.2
  22.6 1.3 %collective-permute-done.4.refs_2_.refs_5_ = bf16[2,2,2,128,128]{4,3,2,1,0:T(8,128)(2,1)S(1)} collective-permute-done((bf16[2,2,2,128,128]{4,3,2,1,0:T(8,128)(2,1)S(1)}, bf16[2,2,2,128,128]{4,3,2,1,0:T(8,128)(2,1)S(1)}, u32[]{:S(2)}, u32[]{:S(2)}) %collective-permute-start.4) | collective-permute-done | bytes 262176 | tf_op jit(solution)/shard_map/ppermute | solution.py:280
  23.9 2.4 %listed_keys.3.mine_ref.refs_0_ = bf16[2,2,2,128,128]{4,3,2,1,0:T(8,128)(2,1)S(1)} custom-call(s32[8,128]{1,0:T(8,128)S(1)} %get-tuple-element.17.places_ref, bf16[2,2,128,128]{3,2,1,0:T(8,128)(2,1)S(1)} %collective-permute-done.1.refs_0_.refs_2_, bf16[2,2,128,128]{3,2,1,0:T(8,128)(2,1)S(1)} %collective-permute-done.2.refs_1_.refs_3_, ...), custom_call_target="tpu_custom_call" | custom-call | flops 1073741824 | bytes 2097152 | tf_op jit(solution)/shard_map/listed_keys/pallas_call | solution.py:348
  26.4 0.2 collective-permute-start.6
  26.6 1.3 %collective-permute-start.7 = (bf16[2,2,128,128]{3,2,1,0:T(8,128)(2,1)S(1)}, bf16[2,2,128,128]{3,2,1,0:T(8,128)(2,1)S(1)}, u32[]{:S(2)}, u32[]{:S(2)}) collective-permute-start(bf16[2,2,128,128]{3,2,1,0:T(8,128)(2,1)S(1)} %get-tuple-element.27), channel_id=1, source_target_pairs={{0,8},{4,12},{8,0},{12,4},{1,9},{5,13},{9,1},{13,5},{2,10},{6,14},... | collective-permute-start | bytes 393224 | tf_op jit(solution)/shard_map/ppermute | solution.py:277
  27.9 0.1 collective-permute-done.6.other_ref
  28.0 0.2 combine.3
  28.2 1.7 %collective-permute-start.8 = (bf16[2,2,128,128]{3,2,1,0:T(8,128)(2,1)S(1)}, bf16[2,2,128,128]{3,2,1,0:T(8,128)(2,1)S(1)}, u32[]{:S(2)}, u32[]{:S(2)}) collective-permute-start(bf16[2,2,128,128]{3,2,1,0:T(8,128)(2,1)S(1)} %get-tuple-element.26.refs_10_), channel_id=1, source_target_pairs={{0,4},{4,8},{8,12},{12,0},{1,5},{5,9},{9,13},{13,1},{2,6},{6,10},{... | collective-permute-start | bytes 393224 | tf_op jit(solution)/shard_map/ppermute | solution.py:277
  29.8 2.2 %collective-permute-start.9 = (bf16[2,2,128,128]{3,2,1,0:T(8,128)(2,1)S(1)}, bf16[2,2,128,128]{3,2,1,0:T(8,128)(2,1)S(1)}, u32[]{:S(2)}, u32[]{:S(2)}) collective-permute-start(bf16[2,2,128,128]{3,2,1,0:T(8,128)(2,1)S(1)} %get-tuple-element.28), channel_id=1, source_target_pairs={{0,12},{4,0},{8,4},{12,8},{1,13},{5,1},{9,5},{13,9},{2,14},{6,2},{... | collective-permute-start | bytes 393224 | tf_op jit(solution)/shard_map/ppermute | solution.py:277
  32.1 4.5 %listed_queries.1 = f32[128,32,128]{2,1,0:T(8,128)} custom-call(s32[8,128]{1,0:T(8,128)S(1)} %get-tuple-element.17.places_ref, bf16[2,2,128,128]{3,2,1,0:T(8,128)(2,1)S(1)} %pack.1.kv_ref.refs_0_, bf16[2,2,128,128]{3,2,1,0:T(8,128)(2,1)S(1)} %collective-permute-done.refs_1_, bf16[2,2,128,128]{3,2,1,0:T(8,128)(2,1)S(1)} %collective-permute-done.1.refs_0_.refs_2_, ...), custom_call_target="tpu_custom_call" | custom-call | flops 805306368 | bytes 6291456 | tf_op jit(solution)/shard_map/listed_queries/pallas_call | solution.py:382
  36.6 2.9 %collective-permute-done.7.refs_1_ = bf16[2,2,128,128]{3,2,1,0:T(8,128)(2,1)S(1)} collective-permute-done((bf16[2,2,128,128]{3,2,1,0:T(8,128)(2,1)S(1)}, bf16[2,2,128,128]{3,2,1,0:T(8,128)(2,1)S(1)}, u32[]{:S(2)}, u32[]{:S(2)}) %collective-permute-start.7) | collective-permute-done | bytes 131104 | tf_op jit(solution)/shard_map/ppermute | solution.py:277
  39.5 0.0 collective-permute-done.8.refs_2_
  39.5 0.4 %collective-permute-done.9.refs_3_ = bf16[2,2,128,128]{3,2,1,0:T(8,128)(2,1)S(1)} collective-permute-done((bf16[2,2,128,128]{3,2,1,0:T(8,128)(2,1)S(1)}, bf16[2,2,128,128]{3,2,1,0:T(8,128)(2,1)S(1)}, u32[]{:S(2)}, u32[]{:S(2)}) %collective-permute-start.9) | collective-permute-done | bytes 131104 | tf_op jit(solution)/shard_map/ppermute | solution.py:277
  39.9 0.8 %total.1 = (f32[128,2,128]{2,1,0:T(2,128)}, f32[128,2,128]{2,1,0:T(2,128)}) custom-call(f32[2,2,128,128]{3,2,1,0:T(8,128)S(1)} %get-tuple-element.22.refs_2_.refs_6_.near_ref, f32[2,2,128,128]{3,2,1,0:T(8,128)S(1)} %get-tuple-element.25.refs_6_.refs_0_, bf16[2,2,128,128]{3,2,1,0:T(8,128)(2,1)S(1)} %collective-permute-done.7.refs_1_, ...), custom_call_target="tpu_custom_call" | custom-call | tf_op jit(solution)/shard_map/total/pallas_call | solution.py:392
Async XLA Ops:
  1.9 10.4 %collective-permute-start = (bf16[2,2,128,128]{3,2,1,0:T(8,128)(2,1)S(1)}, bf16[2,2,128,128]{3,2,1,0:T(8,128)(2,1)S(1)}, u32[]{:S(2)}, u32[]{:S(2)}) collective-permute-start(bf16[2,2,128,128]{3,2,1,0:T(8,128)(2,1)S(1)} %pack.1.kv_ref.refs_0_), channel_id=1, source_target_pairs={{0,8},{4,12},{8,0},{12,4},{1,9},{5,13},{9,1},{13,5},{2,10},{6,14},... | collective-permute-start | bytes 393224 | tf_op jit(solution)/shard_map/ppermute | solution.py:277
  12.4 4.0 %collective-permute-start.3 = (bf16[2,2,2,128,128]{4,3,2,1,0:T(8,128)(2,1)S(1)}, bf16[2,2,2,128,128]{4,3,2,1,0:T(8,128)(2,1)S(1)}, u32[]{:S(2)}, u32[]{:S(2)}) collective-permute-start(bf16[2,2,2,128,128]{4,3,2,1,0:T(8,128)(2,1)S(1)} %choose.2), channel_id=1, source_target_pairs={{0,1},{1,0},{2,3},{3,2},{4,5},{5,4},{6,7},{7,6},{8,9},{9,8},{10,11... | collective-permute-start | bytes 786440 | tf_op jit(solution)/shard_map/ppermute | solution.py:280
  12.4 8.2 %collective-permute-start.1 = (bf16[2,2,128,128]{3,2,1,0:T(8,128)(2,1)S(1)}, bf16[2,2,128,128]{3,2,1,0:T(8,128)(2,1)S(1)}, u32[]{:S(2)}, u32[]{:S(2)}) collective-permute-start(bf16[2,2,128,128]{3,2,1,0:T(8,128)(2,1)S(1)} %pack.1.kv_ref.refs_0_), channel_id=1, source_target_pairs={{0,4},{4,8},{8,12},{12,0},{1,5},{5,9},{9,13},{13,1},{2,6},{6,10},{... | collective-permute-start | bytes 393224 | tf_op jit(solution)/shard_map/ppermute | solution.py:277
  13.9 8.4 %collective-permute-start.2 = (bf16[2,2,128,128]{3,2,1,0:T(8,128)(2,1)S(1)}, bf16[2,2,128,128]{3,2,1,0:T(8,128)(2,1)S(1)}, u32[]{:S(2)}, u32[]{:S(2)}) collective-permute-start(bf16[2,2,128,128]{3,2,1,0:T(8,128)(2,1)S(1)} %pack.1.kv_ref.refs_0_), channel_id=1, source_target_pairs={{0,12},{4,0},{8,4},{12,8},{1,13},{5,1},{9,5},{13,9},{2,14},{6,2},{... | collective-permute-start | bytes 393224 | tf_op jit(solution)/shard_map/ppermute | solution.py:277
  18.7 3.7 %collective-permute-start.5 = (bf16[2,2,2,128,128]{4,3,2,1,0:T(8,128)(2,1)S(1)}, bf16[2,2,2,128,128]{4,3,2,1,0:T(8,128)(2,1)S(1)}, u32[]{:S(2)}, u32[]{:S(2)}) collective-permute-start(bf16[2,2,2,128,128]{4,3,2,1,0:T(8,128)(2,1)S(1)} %listed_keys.2.refs_2_.mine_ref), channel_id=1, source_target_pairs={{0,1},{1,0},{2,3},{3,2},{4,5},{5,4},{6,7},{7,6},{8,9},{9,8},{10,11... | collective-permute-start | bytes 786440 | tf_op jit(solution)/shard_map/ppermute | solution.py:280
  22.3 1.6 %collective-permute-start.4 = (bf16[2,2,2,128,128]{4,3,2,1,0:T(8,128)(2,1)S(1)}, bf16[2,2,2,128,128]{4,3,2,1,0:T(8,128)(2,1)S(1)}, u32[]{:S(2)}, u32[]{:S(2)}) collective-permute-start(bf16[2,2,2,128,128]{4,3,2,1,0:T(8,128)(2,1)S(1)} %choose.3.refs_0_), channel_id=1, source_target_pairs={{0,1},{1,0},{2,3},{3,2},{4,5},{5,4},{6,7},{7,6},{8,9},{9,8},{10,11... | collective-permute-start | bytes 786440 | tf_op jit(solution)/shard_map/ppermute | solution.py:280
  26.4 1.6 %collective-permute-start.6 = (bf16[2,2,2,128,128]{4,3,2,1,0:T(8,128)(2,1)S(1)}, bf16[2,2,2,128,128]{4,3,2,1,0:T(8,128)(2,1)S(1)}, u32[]{:S(2)}, u32[]{:S(2)}) collective-permute-start(bf16[2,2,2,128,128]{4,3,2,1,0:T(8,128)(2,1)S(1)} %listed_keys.3.mine_ref.refs_0_), channel_id=1, source_target_pairs={{0,1},{1,0},{2,3},{3,2},{4,5},{5,4},{6,7},{7,6},{8,9},{9,8},{10,11... | collective-permute-start | bytes 786440 | tf_op jit(solution)/shard_map/ppermute | solution.py:280
  26.6 12.9 %collective-permute-start.7 = (bf16[2,2,128,128]{3,2,1,0:T(8,128)(2,1)S(1)}, bf16[2,2,128,128]{3,2,1,0:T(8,128)(2,1)S(1)}, u32[]{:S(2)}, u32[]{:S(2)}) collective-permute-start(bf16[2,2,128,128]{3,2,1,0:T(8,128)(2,1)S(1)} %get-tuple-element.27), channel_id=1, source_target_pairs={{0,8},{4,12},{8,0},{12,4},{1,9},{5,13},{9,1},{13,5},{2,10},{6,14},... | collective-permute-start | bytes 393224 | tf_op jit(solution)/shard_map/ppermute | solution.py:277
  28.2 11.3 %collective-permute-start.8 = (bf16[2,2,128,128]{3,2,1,0:T(8,128)(2,1)S(1)}, bf16[2,2,128,128]{3,2,1,0:T(8,128)(2,1)S(1)}, u32[]{:S(2)}, u32[]{:S(2)}) collective-permute-start(bf16[2,2,128,128]{3,2,1,0:T(8,128)(2,1)S(1)} %get-tuple-element.26.refs_10_), channel_id=1, source_target_pairs={{0,4},{4,8},{8,12},{12,0},{1,5},{5,9},{9,13},{13,1},{2,6},{6,10},{... | collective-permute-start | bytes 393224 | tf_op jit(solution)/shard_map/ppermute | solution.py:277
  29.8 10.0 %collective-permute-start.9 = (bf16[2,2,128,128]{3,2,1,0:T(8,128)(2,1)S(1)}, bf16[2,2,128,128]{3,2,1,0:T(8,128)(2,1)S(1)}, u32[]{:S(2)}, u32[]{:S(2)}) collective-permute-start(bf16[2,2,128,128]{3,2,1,0:T(8,128)(2,1)S(1)} %get-tuple-element.28), channel_id=1, source_target_pairs={{0,12},{4,0},{8,4},{12,8},{1,13},{5,1},{9,5},{13,9},{2,14},{6,2},{... | collective-permute-start | bytes 393224 | tf_op jit(solution)/shard_map/ppermute | solution.py:277

commit v3 on v1

v3 whole, which is shorter than its diff:
```python
import functools

import jax
import jax.numpy as jnp
from jax import lax
from jax.experimental import pallas as pl
from jax.experimental.pallas import tpu as pltpu
from jax.sharding import PartitionSpec as P

QH = 64
KVH = 4
LOG2E = 1.4426950408889634
ROWS = 512
VMEM_LIMIT = 24 * 1024 * 1024

VMEM_SPEC = pl.BlockSpec(memory_space=pltpu.VMEM)
ANY_SPEC = pl.BlockSpec(memory_space=pl.ANY)
HBM_SPEC = pl.BlockSpec(memory_space=pltpu.HBM)


def rows_dot(left, right):
    return lax.dot_general(left, right, (((1,), (1,)), ((), ())), preferred_element_type=jnp.float32)


def tile_terms(key_blk, value_blk, query_blk, upstream, log_norm, row_terms, allowed, factor):
    scores = rows_dot(key_blk, query_blk)
    probs = jnp.exp2(scores * (factor * LOG2E) - log_norm)
    if allowed is not None:
        probs = jnp.where(allowed, probs, 0.0)
    grad_probs = rows_dot(value_blk, upstream)
    grad_scores = probs * (grad_probs - row_terms)
    return probs.astype(jnp.bfloat16), grad_scores.astype(jnp.bfloat16)


def chunks(tokens, grouped, rows):
    step = rows // grouped
    return [(i, slice(i * step, (i + 1) * step), slice(i * rows, (i + 1) * rows)) for i in range(tokens // step)]


def start_all(sources, targets, sems):
    copies = [pltpu.make_async_copy(source, target, sems.at[i]) for i, (source, target) in enumerate(zip(sources, targets))]
    for copy in copies:
        copy.start()
    return copies


def bring_rows(query_ref, up_ref, held_ref, sems, rows):
    _, count, tokens, grouped, _ = held_ref.shape
    copies = {}
    for head in range(count):
        heads = slice(head * grouped, (head + 1) * grouped)
        for i, toks, _ in chunks(tokens, grouped, rows):
            copies[head, i] = [
                pltpu.make_async_copy(ref.at[toks, heads], held_ref.at[kind, head, toks], sems.at[head, i, kind])
                for kind, ref in enumerate((query_ref, up_ref))
            ]
            for copy in copies[head, i]:
                copy.start()
    return copies


def row_blocks(held_ref, head, rows):
    _, _, tokens, grouped, head_dim = held_ref.shape
    for _, toks, cols in chunks(tokens, grouped, rows):
        yield toks, cols, *(held_ref[kind, head, toks].reshape(rows, head_dim) for kind in range(2))


def pack_kernel(key_ref, value_ref, kv_ref, held_ref, sems):
    copies = start_all((key_ref, value_ref), (held_ref.at[0], held_ref.at[1]), sems)
    for kind, copy in enumerate(copies):
        copy.wait()
        for head in range(held_ref.shape[2]):
            kv_ref[kind, head] = held_ref[kind, :, head, :]


def spread_kernel(
    grouped, ring, subs, rows, norm_ref, term_ref, docs_ref, pairs_ref, query_ref, up_ref,
    norm_row_ref, term_row_ref, docs_row_ref, doc_col_ref, places_ref, row_ref,
    held_ref, held_docs, held_pairs, sems, row_sems,
):
    _, heads, tokens = held_ref.shape
    copies = start_all(
        (pairs_ref, docs_ref, norm_ref, term_ref), (held_pairs, held_docs, held_ref.at[0], held_ref.at[1]), sems
    )
    brought = bring_rows(query_ref, up_ref, row_ref, row_sems, rows)
    cols = tokens * grouped
    column = lax.broadcasted_iota(jnp.int32, (tokens, cols), 1)
    token = lax.broadcasted_iota(jnp.int32, (tokens, cols), 0)
    pick = jnp.where(token == column // grouped, 1.0, 0.0).astype(jnp.bfloat16)
    keep = lax.broadcasted_iota(jnp.int32, (grouped, cols), 0) == (
        lax.broadcasted_iota(jnp.int32, (grouped, cols), 1) % grouped
    )
    for copy in copies:
        copy.wait()

    ctx, sub = lax.axis_index("ctx"), lax.axis_index("sub")
    pairs = held_pairs[...]
    lane = lax.broadcasted_iota(jnp.int32, pairs.shape, 1)

    def listed_by(core):
        mask = lane == ctx * subs + core
        span = jnp.sum(jnp.where(mask, pairs, 0).astype(jnp.float32), axis=1, keepdims=True)
        span = jnp.broadcast_to(span, (2, places_ref.shape[1])).astype(jnp.int32)
        return span // subs, span % subs

    (mine, mine_sub), (other, other_sub) = listed_by(sub), listed_by(1 - sub)
    places_ref[0:2] = other ^ ctx
    places_ref[2:4] = jnp.where(mine_sub == sub, mine ^ ctx, ring)
    places_ref[4:6] = places_ref[2:4]
    places_ref[6:8] = jnp.where(other_sub == sub, other ^ ctx, ring)

    pieces = []
    for value in (held_ref[0] * LOG2E, held_ref[1]):
        for _ in range(3):
            piece = value.astype(jnp.bfloat16)
            value = value - piece.astype(jnp.float32)
            pieces.append(piece)
    docs = held_docs[...].astype(jnp.float32)
    pieces.append(jnp.broadcast_to(docs, (grouped, tokens)).astype(jnp.bfloat16))
    spread = jnp.dot(jnp.concatenate(pieces, axis=0), pick, preferred_element_type=jnp.float32)
    for i, out_ref in enumerate((norm_row_ref, term_row_ref)):
        base = 3 * i * heads
        value = spread[base:base + heads] + spread[base + heads:base + 2 * heads]
        value = value + spread[base + 2 * heads:base + 3 * heads]
        for head in range(out_ref.shape[0]):
            group = value[head * grouped:(head + 1) * grouped]
            out_ref[head] = jnp.sum(jnp.where(keep, group, 0.0), axis=0, keepdims=True)
    docs_row_ref[...] = spread[6 * heads:6 * heads + 1]
    doc_col_ref[...] = jnp.broadcast_to(docs, (tokens, tokens)).T
    for pair in brought.values():
        for copy in pair:
            copy.wait()


def pick_block(sources, row):
    chosen = sources[0].astype(jnp.float32)
    for step in range(1, len(sources)):
        chosen = jnp.where(row == step, sources[step].astype(jnp.float32), chosen)
    return chosen.astype(jnp.bfloat16)


def choose_kernel(places_ref, *refs):
    *column, _, out_ref = refs
    for which in range(2):
        row = places_ref[which:which + 1]
        for kind in range(2):
            for head in range(out_ref.shape[2]):
                out_ref[which, kind, head] = pick_block([ref[kind, head] for ref in column], row)


def far_blocks(places_ref, column, other_ref, head):
    return [
        jnp.concatenate(
            [
                pick_block(
                    [ref[kind, head] for ref in column] + [other_ref[which, kind, head]],
                    places_ref[2 + which:3 + which],
                )
                for which in range(2)
            ],
            axis=0,
        )
        for kind in range(2)
    ]


def local_kernel(
    factor, rows, first, kv_ref, row_ref, norm_ref, term_ref, docs_ref, doc_col_ref, _, dkv_ref, dq_ref
):
    tokens, grouped, head_dim = row_ref.shape[2:]
    doc_col = jnp.concatenate([doc_col_ref[...]] * (rows // tokens), axis=1)
    for place in range(dkv_ref.shape[1]):
        head = first + place
        key_blk, value_blk = kv_ref[0, head], kv_ref[1, head]
        grad_key = jnp.zeros((tokens, head_dim), jnp.float32)
        grad_val = jnp.zeros((tokens, head_dim), jnp.float32)
        for toks, cols, query_blk, upstream in row_blocks(row_ref, head, rows):
            position = lax.broadcasted_iota(jnp.int32, (tokens, rows), 1) // grouped + toks.start
            allowed = (lax.broadcasted_iota(jnp.int32, (tokens, rows), 0) <= position) & (
                doc_col == docs_ref[:, cols]
            )
            probs, grads = tile_terms(
                key_blk, value_blk, query_blk, upstream, norm_ref[head, :, cols], term_ref[head, :, cols],
                allowed, factor,
            )
            grad_val += jnp.dot(probs, upstream, preferred_element_type=jnp.float32)
            grad_key += jnp.dot(grads, query_blk, preferred_element_type=jnp.float32)
            grad_query = lax.dot_general(
                grads, key_blk, (((0,), (0,)), ((), ())), preferred_element_type=jnp.float32
            )
            dq_ref[toks, place * grouped:(place + 1) * grouped] = (grad_query * factor).reshape(
                rows // grouped, grouped, head_dim
            )
        dkv_ref[0, place] = grad_key * factor
        dkv_ref[1, place] = grad_val


def listed_kernel(factor, rows, places_ref, *refs):
    *column, other_ref, held_ref, norm_ref, term_ref, dkv_ref = refs
    tokens, grouped, head_dim = held_ref.shape[2:]
    for head in range(other_ref.shape[2]):
        key_blk, value_blk = far_blocks(places_ref, column, other_ref, head)
        grad_key = jnp.zeros((2 * tokens, head_dim), jnp.float32)
        grad_val = jnp.zeros((2 * tokens, head_dim), jnp.float32)
        for toks, cols, query_blk, upstream in row_blocks(held_ref, head, rows):
            probs, grads = tile_terms(
                key_blk, value_blk, query_blk, upstream,
                norm_ref[head, :, cols], term_ref[head, :, cols], None, factor,
            )
            grad_val += jnp.dot(probs, upstream, preferred_element_type=jnp.float32)
            grad_key += jnp.dot(grads, query_blk, preferred_element_type=jnp.float32)
        grad_key = (grad_key * factor).astype(dkv_ref.dtype)
        grad_val = grad_val.astype(dkv_ref.dtype)
        for which in range(2):
            dkv_ref[which, 0, head] = grad_key[which * tokens:(which + 1) * tokens]
            dkv_ref[which, 1, head] = grad_val[which * tokens:(which + 1) * tokens]


def query_kernel(factor, rows, places_ref, *refs):
    *column, other_ref, held_ref, norm_ref, term_ref, near_one, near_two, _, dq_ref = refs
    tokens, grouped, head_dim = held_ref.shape[2:]
    half = near_one.shape[1] // grouped
    for head in range(held_ref.shape[1]):
        near_ref, place = (near_one, head) if head < half else (near_two, head - half)
        key_blk, value_blk = far_blocks(places_ref, column, other_ref, head)
        for toks, cols, query_blk, upstream in row_blocks(held_ref, head, rows):
            _, grads = tile_terms(
                key_blk, value_blk, query_blk, upstream, norm_ref[head, :, cols], term_ref[head, :, cols],
                None, factor,
            )
            grad_query = lax.dot_general(
                grads, key_blk, (((0,), (0,)), ((), ())), preferred_element_type=jnp.float32
            )
            near = near_ref[toks, place * grouped:(place + 1) * grouped]
            dq_ref[toks, head * grouped:(head + 1) * grouped] = near + (grad_query * factor).reshape(
                rows // grouped, grouped, head_dim
            )


def combine_kernel(places_ref, mine_ref, other_ref, *out_refs):
    for step, out_ref in enumerate(out_refs):
        for kind in range(2):
            for head in range(out_ref.shape[1]):
                total = None
                for i, ref in enumerate((mine_ref, other_ref)):
                    for which in range(2):
                        row = places_ref[4 + 2 * i + which:5 + 2 * i + which]
                        term = jnp.where(row == step, ref[which, kind, head].astype(jnp.float32), 0.0)
                        total = term if total is None else total + term
                out_ref[kind, head] = total.astype(out_ref.dtype)


def merge_kernel(own_ref, *refs):
    *arrived, _, out_ref = refs
    total = own_ref[...]
    for ref in arrived:
        total += ref[...].astype(jnp.float32)
    out_ref[...] = total.astype(out_ref.dtype)


def total_kernel(near_one, near_two, *refs):
    *blocks, dk_ref, dv_ref = refs
    half = near_one.shape[1]
    for kind, out_ref in enumerate((dk_ref, dv_ref)):
        for head in range(out_ref.shape[1]):
            total = near_one[kind, head] if head < half else near_two[kind, head - half]
            for ref in blocks:
                total += ref[kind, head].astype(jnp.float32)
            out_ref[:, head, :] = total


def body(queries, keys, values, grad_out, row_lse, row_delta, doc_ids, pairs):
    tokens, heads, head_dim = queries.shape
    kv_heads = keys.shape[1]
    grouped = QH // KVH
    factor = head_dim ** (-0.5)
    ring = lax.axis_size("ctx")
    subs = lax.axis_size("sub")
    rows = min(ROWS, tokens * grouped)
    cols = tokens * grouped
    span_shape = (2, kv_heads, tokens, head_dim)

    def crossed(array, bit):
        return lax.ppermute(array, "ctx", [(i, i ^ bit) for i in range(ring)])

    def swapped(array):
        return lax.ppermute(array, "sub", [(i, i ^ 1) for i in range(subs)])

    def in_hbm(*arrays):
        return [pltpu.with_memory_space_constraint(array, pltpu.HBM) for array in arrays]

    params = pltpu.CompilerParams(vmem_limit_bytes=VMEM_LIMIT)
    kv = pl.pallas_call(
        pack_kernel,
        in_specs=[HBM_SPEC] * 2,
        out_specs=VMEM_SPEC,
        out_shape=jax.ShapeDtypeStruct(span_shape, jnp.bfloat16),
        scratch_shapes=[pltpu.VMEM((2, *keys.shape), jnp.bfloat16), pltpu.SemaphoreType.DMA((2,))],
        compiler_params=params,
        name="pack",
    )(*in_hbm(keys, values))
    column = {0: kv}
    for place in sorted(range(1, ring), key=lambda place: -(place & -place)):
        low = place & -place
        column[place] = crossed(column[place ^ low], low)
    column = [column[place] for place in range(ring)]

    norm, term, docs, doc_col, places, held = pl.pallas_call(
        functools.partial(spread_kernel, grouped, ring, subs, rows),
        in_specs=[HBM_SPEC] * 6,
        out_specs=[VMEM_SPEC] * 6,
        out_shape=[
            jax.ShapeDtypeStruct((kv_heads, 1, cols), jnp.float32),
            jax.ShapeDtypeStruct((kv_heads, 1, cols), jnp.float32),
            jax.ShapeDtypeStruct((1, cols), jnp.float32),
            jax.ShapeDtypeStruct((tokens, tokens), jnp.float32),
            jax.ShapeDtypeStruct((8, head_dim), jnp.int32),
            jax.ShapeDtypeStruct((2, kv_heads, tokens, grouped, head_dim), jnp.bfloat16),
        ],
        scratch_shapes=[
            pltpu.VMEM((2, heads, tokens), jnp.float32),
            pltpu.VMEM((1, tokens), jnp.int32),
            pltpu.VMEM(pairs.shape[::-1], jnp.int32),
            pltpu.SemaphoreType.DMA((4,)),
            pltpu.SemaphoreType.DMA((kv_heads, cols // rows, 2)),
        ],
        compiler_params=params,
        name="spread",
    )(*in_hbm(row_lse.T, row_delta.T, doc_ids.reshape(1, tokens), pairs.T, queries, grad_out))

    work = 2 * tokens * tokens * heads * head_dim
    moved = 2 * queries.size * 2

    row_specs = [VMEM_SPEC] * 3
    half = (kv_heads + 1) // 2

    def local(first, count, after):
        return pl.pallas_call(
            functools.partial(local_kernel, factor, rows, first),
            in_specs=[VMEM_SPEC] + row_specs + [VMEM_SPEC] * 2 + [ANY_SPEC],
            out_specs=[VMEM_SPEC] * 2,
            out_shape=[
                jax.ShapeDtypeStruct((2, count, tokens, head_dim), jnp.float32),
                jax.ShapeDtypeStruct((tokens, count * grouped, head_dim), jnp.float32),
            ],
            compiler_params=params,
            cost_estimate=pl.CostEstimate(
                flops=5 * work * count // kv_heads, bytes_accessed=2 * moved * count // kv_heads, transcendentals=0
            ),
            name="local_block",
        )(kv, held, norm, term, docs, doc_col, after)

    near_kv, near_query = local(0, half, places)

    chosen = pl.pallas_call(
        choose_kernel,
        in_specs=[VMEM_SPEC] * (ring + 1) + [ANY_SPEC],
        out_specs=VMEM_SPEC,
        out_shape=jax.ShapeDtypeStruct((2, *span_shape), jnp.bfloat16),
        compiler_params=params,
        name="choose",
    )(places, *column, near_kv)
    other = swapped(chosen)
    far_kv = pl.pallas_call(
        functools.partial(listed_kernel, factor, rows),
        in_specs=[VMEM_SPEC] * (ring + 2) + row_specs,
        out_specs=VMEM_SPEC,
        out_shape=jax.ShapeDtypeStruct((2, *span_shape), jnp.bfloat16),
        compiler_params=params,
        cost_estimate=pl.CostEstimate(flops=8 * work, bytes_accessed=moved, transcendentals=0),
        name="listed_keys",
    )(places, *column, other, held, norm, term)
    other_kv = swapped(far_kv)
    sums = pl.pallas_call(
        combine_kernel,
        in_specs=[VMEM_SPEC] * 3,
        out_specs=[VMEM_SPEC] * ring,
        out_shape=[
            jax.ShapeDtypeStruct(span_shape, jnp.bfloat16 if place % 2 else jnp.float32) for place in range(ring)
        ],
        compiler_params=params,
        name="combine",
    )(places, far_kv, other_kv)

    after, last = sums[0], (near_kv, near_query)
    if half < kv_heads:
        last = local(half, kv_heads - half, after)
        after = last[0]
    arrived = {place: [] for place in range(ring)}
    for place in sorted(range(1, ring), key=lambda place: (place & -place, -place)):
        low = place & -place
        block = sums[place]
        if arrived[place]:
            block = pl.pallas_call(
                merge_kernel,
                in_specs=[VMEM_SPEC] * (1 + len(arrived[place])) + [ANY_SPEC],
                out_specs=VMEM_SPEC,
                out_shape=jax.ShapeDtypeStruct(span_shape, jnp.bfloat16),
                compiler_params=params,
                name="merge",
            )(block, *arrived[place], after)
            after = block
        arrived[place ^ low].append(crossed(block, low))

    grad_queries = pl.pallas_call(
        functools.partial(query_kernel, factor, rows),
        in_specs=[VMEM_SPEC] * (2 + ring) + row_specs + [VMEM_SPEC] * 2 + [ANY_SPEC],
        out_specs=VMEM_SPEC,
        out_shape=jax.ShapeDtypeStruct((tokens, heads, head_dim), jnp.float32),
        compiler_params=params,
        cost_estimate=pl.CostEstimate(flops=6 * work, bytes_accessed=3 * moved, transcendentals=0),
        name="listed_queries",
    )(places, *column, other, held, norm, term, near_query, last[1], after)

    grad_keys, grad_values = pl.pallas_call(
        total_kernel,
        in_specs=[VMEM_SPEC] * (3 + len(arrived[0])),
        out_specs=[VMEM_SPEC] * 2,
        out_shape=[jax.ShapeDtypeStruct((tokens, kv_heads, head_dim), jnp.float32)] * 2,
        compiler_params=params,
        name="total",
    )(near_kv, last[0], sums[0], *arrived[0])
    return (grad_queries, grad_keys, grad_values)


def solution(mesh):
    return jax.shard_map(
        body,
        mesh=mesh,
        in_specs=(
            P(("groups", "ctx", "sub"), "head", None),
            P(("groups", "ctx", "sub"), "head", None),
            P(("groups", "ctx", "sub"), "head", None),
            P(("groups", "ctx", "sub"), "head", None),
            P(("groups", "ctx", "sub"), "head"),
            P(("groups", "ctx", "sub"), "head"),
            P(("groups", "ctx", "sub")),
            P("groups", None),
        ),
        out_specs=(
            P(("groups", "ctx", "sub"), "head", None),
            P(("groups", "ctx", "sub"), "head", None),
            P(("groups", "ctx", "sub"), "head", None),
        ),
        check_vma=False,
    )
```

time: 37.8 us -> 39.2 us (1.037); the launches traced: 37.1 us -> 39 us
  waiting for transfers between devices: 7.72 us -> 12.6 us
  starting transfers between devices: 13.1 us -> 11.4 us
  Pallas kernels: 15.7 us -> 14.2 us
    ppermute x6, waiting for transfers between devices: 4.8 us -> 9.72 us  [crossed(): return lax.ppermute(array, 'ctx', [(i, i ^ bit) for i in range(ring)])]
    ppermute x6, starting transfers between devices: 12.8 us -> 11.2 us  [crossed(): return lax.ppermute(array, 'ctx', [(i, i ^ bit) for i in range(ring)])]
    pallas_call x6 -> x8, Pallas kernels: 15.1 us -> 13.7 us  [the longest x1 4.52 us: body(): pl.pallas_call(functools.partial(query_kernel, factor, rows), in_specs=[V...]
  transfers between devices with their start and end apart: 8 -> 8, of which waited for: 4 -> 6; matrix products, arithmetic and copies ran while one was open for 0% -> 0% of each run, Pallas kernels for 29% -> 23%
where the time goes in v3:
time: 39.2 us; the launch traced here: 39 us
  Pallas kernels  14.2 us (36%)
  waiting for transfers between devices  12.6 us (32%)
  starting transfers between devices  11.4 us (29%)
  between operations  0.7 us (2%)
    ppermute x6, starting transfers between devices, crossed(): return lax.ppermute(array, 'ctx', [(i, i ^ bit) for i in range(ring)])  11.2 us
    ppermute x6, waiting for transfers between devices, crossed(): return lax.ppermute(array, 'ctx', [(i, i ^ bit) for i in range(ring)])  9.72 us
    pallas_call x1, Pallas kernels, body(): pl.pallas_call(functools.partial(query_kernel, factor, rows), in_specs=[V...  4.52 us
    ppermute x2, waiting for transfers between devices, swapped(): return lax.ppermute(array, 'sub', [(i, i ^ 1) for i in range(subs)])  2.92 us
    pallas_call x2, Pallas kernels, local(): pl.pallas_call(functools.partial(local_kernel, factor, rows, first), in_s...  2.62 us
    pallas_call x1, Pallas kernels, body(): pl.pallas_call(functools.partial(listed_kernel, factor, rows), in_specs=[...  2.45 us
    pallas_call x1, Pallas kernels, body(): pl.pallas_call(functools.partial(spread_kernel, grouped, ring, subs, rows...  1.98 us
    pallas_call x1, Pallas kernels, body(): pl.pallas_call(pack_kernel, in_specs=[HBM_SPEC] * 2, out_specs=VMEM_SPEC,...  1.24 us
  transfers between devices with their start and end apart: 8, of which 6 were waited for; matrix products, arithmetic and copies ran while one was open for 0% of the time, Pallas kernels for 23%

profile of v3, /device:TPU:0, one launch (start us, length us, event | category | flops | bytes accessed | tf_op | source)
XLA Modules:
  0.0 39.0 jit_solution(4710173024786352853)
XLA Ops:
  0.6 1.2 %pack.1.kv_ref.refs_0_ = bf16[2,2,128,128]{3,2,1,0:T(8,128)(2,1)S(1)} custom-call(bf16[128,2,128]{2,1,0:T(2,128)(2,1)} %key_ref.1, bf16[128,2,128]{2,1,0:T(2,128)(2,1)} %value_ref.1), custom_call_target="tpu_custom_call" | custom-call | tf_op jit(solution)/shard_map/pack/pallas_call | solution.py:293
  1.9 4.1 %collective-permute-start.1 = (bf16[2,2,128,128]{3,2,1,0:T(8,128)(2,1)S(1)}, bf16[2,2,128,128]{3,2,1,0:T(8,128)(2,1)S(1)}, u32[]{:S(2)}, u32[]{:S(2)}) collective-permute-start(bf16[2,2,128,128]{3,2,1,0:T(8,128)(2,1)S(1)} %pack.1.kv_ref.refs_0_), channel_id=1, source_target_pairs={{0,8},{4,12},{8,0},{12,4},{1,9},{5,13},{9,1},{13,5},{2,10},{6,14},... | collective-permute-start | bytes 393224 | tf_op jit(solution)/shard_map/ppermute | solution.py:284
  6.0 1.6 %collective-permute-start = (bf16[2,2,128,128]{3,2,1,0:T(8,128)(2,1)S(1)}, bf16[2,2,128,128]{3,2,1,0:T(8,128)(2,1)S(1)}, u32[]{:S(2)}, u32[]{:S(2)}) collective-permute-start(bf16[2,2,128,128]{3,2,1,0:T(8,128)(2,1)S(1)} %pack.1.kv_ref.refs_0_), channel_id=1, source_target_pairs={{0,4},{4,0},{8,12},{12,8},{1,5},{5,1},{9,13},{13,9},{2,6},{6,2},{1... | collective-permute-start | bytes 393224 | tf_op jit(solution)/shard_map/ppermute | solution.py:284
  7.6 4.8 %collective-permute-done.1.refs_2_ = bf16[2,2,128,128]{3,2,1,0:T(8,128)(2,1)S(1)} collective-permute-done((bf16[2,2,128,128]{3,2,1,0:T(8,128)(2,1)S(1)}, bf16[2,2,128,128]{3,2,1,0:T(8,128)(2,1)S(1)}, u32[]{:S(2)}, u32[]{:S(2)}) %collective-permute-start.1) | collective-permute-done | bytes 131104 | tf_op jit(solution)/shard_map/ppermute | solution.py:284
  12.4 0.6 %collective-permute-start.2 = (bf16[2,2,128,128]{3,2,1,0:T(8,128)(2,1)S(1)}, bf16[2,2,128,128]{3,2,1,0:T(8,128)(2,1)S(1)}, u32[]{:S(2)}, u32[]{:S(2)}) collective-permute-start(bf16[2,2,128,128]{3,2,1,0:T(8,128)(2,1)S(1)} %collective-permute-done.1.refs_2_), channel_id=1, source_target_pairs={{0,4},{4,0},{8,12},{12,8},{1,5},{5,1},{9,13},{13,9},{2,6},{6,2},{1... | collective-permute-start | bytes 393224 | tf_op jit(solution)/shard_map/ppermute | solution.py:284
  13.0 2.0 %spread.1 = (f32[2,1,2048]{2,1,0:T(1,128)S(1)}, f32[2,1,2048]{2,1,0:T(1,128)S(1)}, f32[1,2048]{1,0:T(1,128)S(1)}, f32[128,128]{1,0:T(8,128)S(1)}, s32[8,128]{1,0...) custom-call(f32[32,128]{1,0:T(8,128)} %bitcast.4, f32[32,128]{1,0:T(8,128)} %bitcast.5, s32[1,128]{1,0:T(1,128)} %bitcast.7, ...), custom_call_target="tpu_custom_call" | custom-call | tf_op jit(solution)/shard_map/spread/pallas_call | solution.py:308
  15.0 1.3 %local_block.2 = (f32[2,1,128,128]{3,2,1,0:T(8,128)S(1)}, f32[128,16,128]{2,1,0:T(8,128)S(1)}) custom-call(bf16[2,2,128,128]{3,2,1,0:T(8,128)(2,1)S(1)} %pack.1.kv_ref.refs_0_, bf16[2,2,128,16,128]{4,3,2,1,0:T(8,128)(2,1)S(1)} %get-tuple-element.20.row_ref.refs_5_, f32[2,1,2048]{2,1,0:T(1,128)S(1)} %get-tuple-element.21.norm_ref.refs_6_, ...), custom_call_target="tpu_custom_call" | custom-call | flops 335544320 | bytes 2097152 | tf_op jit(solution)/shard_map/local_block/pallas_call | solution.py:338
  16.3 0.0 collective-permute-done.refs_1_
  16.3 1.0 %collective-permute-done.2.refs_3_ = bf16[2,2,128,128]{3,2,1,0:T(8,128)(2,1)S(1)} collective-permute-done((bf16[2,2,128,128]{3,2,1,0:T(8,128)(2,1)S(1)}, bf16[2,2,128,128]{3,2,1,0:T(8,128)(2,1)S(1)}, u32[]{:S(2)}, u32[]{:S(2)}) %collective-permute-start.2) | collective-permute-done | bytes 131104 | tf_op jit(solution)/shard_map/ppermute | solution.py:284
  17.4 0.1 choose.1
  17.5 0.1 collective-permute-start.3
  17.6 1.5 %collective-permute-done.3.refs_4_ = bf16[2,2,2,128,128]{4,3,2,1,0:T(8,128)(2,1)S(1)} collective-permute-done((bf16[2,2,2,128,128]{4,3,2,1,0:T(8,128)(2,1)S(1)}, bf16[2,2,2,128,128]{4,3,2,1,0:T(8,128)(2,1)S(1)}, u32[]{:S(2)}, u32[]{:S(2)}) %collective-permute-start.3) | collective-permute-done | bytes 262176 | tf_op jit(solution)/shard_map/ppermute | solution.py:287
  19.1 2.5 %listed_keys.1.mine_ref = bf16[2,2,2,128,128]{4,3,2,1,0:T(8,128)(2,1)S(1)} custom-call(s32[8,128]{1,0:T(8,128)S(1)} %get-tuple-element.19._.places_ref, bf16[2,2,128,128]{3,2,1,0:T(8,128)(2,1)S(1)} %pack.1.kv_ref.refs_0_, bf16[2,2,128,128]{3,2,1,0:T(8,128)(2,1)S(1)} %collective-permute-done.refs_1_, ...), custom_call_target="tpu_custom_call" | custom-call | flops 1073741824 | bytes 2097152 | tf_op jit(solution)/shard_map/listed_keys/pallas_call | solution.py:364
  21.5 0.2 collective-permute-start.4
  21.8 1.4 %collective-permute-done.4.other_ref = bf16[2,2,2,128,128]{4,3,2,1,0:T(8,128)(2,1)S(1)} collective-permute-done((bf16[2,2,2,128,128]{4,3,2,1,0:T(8,128)(2,1)S(1)}, bf16[2,2,2,128,128]{4,3,2,1,0:T(8,128)(2,1)S(1)}, u32[]{:S(2)}, u32[]{:S(2)}) %collective-permute-start.4) | collective-permute-done | bytes 262176 | tf_op jit(solution)/shard_map/ppermute | solution.py:287
  23.2 0.4 %combine.1 = (f32[2,2,128,128]{3,2,1,0:T(8,128)S(1)}, bf16[2,2,128,128]{3,2,1,0:T(8,128)(2,1)S(1)}, f32[2,2,128,128]{3,2,1,0:T(8,128)S(1)}, bf16[2,2,128,128]{3,2,1,0:T(8,128)(2,1)S(1)}) custom-call(s32[8,128]{1,0:T(8,128)S(1)} %get-tuple-element.19._.places_ref, bf16[2,2,2,128,128]{4,3,2,1,0:T(8,128)(2,1)S(1)} %listed_keys.1.mine_ref, ...), custom_call_target="tpu_custom_call" | custom-call | tf_op jit(solution)/shard_map/combine/pallas_call | solution.py:374
  23.6 1.1 %collective-permute-start.5 = (bf16[2,2,128,128]{3,2,1,0:T(8,128)(2,1)S(1)}, bf16[2,2,128,128]{3,2,1,0:T(8,128)(2,1)S(1)}, u32[]{:S(2)}, u32[]{:S(2)}) collective-permute-start(bf16[2,2,128,128]{3,2,1,0:T(8,128)(2,1)S(1)} %get-tuple-element.30), channel_id=1, source_target_pairs={{0,4},{4,0},{8,12},{12,8},{1,5},{5,1},{9,13},{13,9},{2,6},{6,2},{1... | collective-permute-start | bytes 393224 | tf_op jit(solution)/shard_map/ppermute | solution.py:284
  24.7 1.0 %collective-permute-start.6 = (bf16[2,2,128,128]{3,2,1,0:T(8,128)(2,1)S(1)}, bf16[2,2,128,128]{3,2,1,0:T(8,128)(2,1)S(1)}, u32[]{:S(2)}, u32[]{:S(2)}) collective-permute-start(bf16[2,2,128,128]{3,2,1,0:T(8,128)(2,1)S(1)} %get-tuple-element.32), channel_id=1, source_target_pairs={{0,4},{4,0},{8,12},{12,8},{1,5},{5,1},{9,13},{13,9},{2,6},{6,2},{1... | collective-permute-start | bytes 393224 | tf_op jit(solution)/shard_map/ppermute | solution.py:284
  25.6 1.3 %local_block.3 = (f32[2,1,128,128]{3,2,1,0:T(8,128)S(1)}, f32[128,16,128]{2,1,0:T(8,128)S(1)}) custom-call(bf16[2,2,128,128]{3,2,1,0:T(8,128)(2,1)S(1)} %pack.1.kv_ref.refs_0_, bf16[2,2,128,16,128]{4,3,2,1,0:T(8,128)(2,1)S(1)} %get-tuple-element.20.row_ref.refs_5_, f32[2,1,2048]{2,1,0:T(1,128)S(1)} %get-tuple-element.21.norm_ref.refs_6_, ...), custom_call_target="tpu_custom_call" | custom-call | flops 335544320 | bytes 2097152 | tf_op jit(solution)/shard_map/local_block/pallas_call | solution.py:338
  27.0 3.0 %collective-permute-done.5.refs_0_ = bf16[2,2,128,128]{3,2,1,0:T(8,128)(2,1)S(1)} collective-permute-done((bf16[2,2,128,128]{3,2,1,0:T(8,128)(2,1)S(1)}, bf16[2,2,128,128]{3,2,1,0:T(8,128)(2,1)S(1)}, u32[]{:S(2)}, u32[]{:S(2)}) %collective-permute-start.5) | collective-permute-done | bytes 131104 | tf_op jit(solution)/shard_map/ppermute | solution.py:284
  30.0 2.8 %collective-permute-start.7 = (bf16[2,2,128,128]{3,2,1,0:T(8,128)(2,1)S(1)}, bf16[2,2,128,128]{3,2,1,0:T(8,128)(2,1)S(1)}, u32[]{:S(2)}, u32[]{:S(2)}) collective-permute-start(bf16[2,2,128,128]{3,2,1,0:T(8,128)(2,1)S(1)} %merge.1.refs_10_), channel_id=1, source_target_pairs={{0,8},{4,12},{8,0},{12,4},{1,9},{5,13},{9,1},{13,5},{2,10},{6,14},... | collective-permute-start | bytes 393224 | tf_op jit(solution)/shard_map/ppermute | solution.py:284
  32.8 4.5 %listed_queries.1 = f32[128,32,128]{2,1,0:T(8,128)} custom-call(s32[8,128]{1,0:T(8,128)S(1)} %get-tuple-element.19._.places_ref, bf16[2,2,128,128]{3,2,1,0:T(8,128)(2,1)S(1)} %pack.1.kv_ref.refs_0_, bf16[2,2,128,128]{3,2,1,0:T(8,128)(2,1)S(1)} %collective-permute-done.refs_1_, bf16[2,2,128,128]{3,2,1,0:T(8,128)(2,1)S(1)} %collective-permute-done.1.refs_2_, ...), custom_call_target="tpu_custom_call" | custom-call | flops 805306368 | bytes 6291456 | tf_op jit(solution)/shard_map/listed_queries/pallas_call | solution.py:405
  37.3 0.0 collective-permute-done.6.refs_1_
  37.3 0.9 %collective-permute-done.7.refs_2_ = bf16[2,2,128,128]{3,2,1,0:T(8,128)(2,1)S(1)} collective-permute-done((bf16[2,2,128,128]{3,2,1,0:T(8,128)(2,1)S(1)}, bf16[2,2,128,128]{3,2,1,0:T(8,128)(2,1)S(1)}, u32[]{:S(2)}, u32[]{:S(2)}) %collective-permute-start.7) | collective-permute-done | bytes 131104 | tf_op jit(solution)/shard_map/ppermute | solution.py:284
  38.1 0.8 %total.1 = (f32[128,2,128]{2,1,0:T(2,128)}, f32[128,2,128]{2,1,0:T(2,128)}) custom-call(f32[2,1,128,128]{3,2,1,0:T(8,128)S(1)} %get-tuple-element.25.refs_4_.near_one, f32[2,1,128,128]{3,2,1,0:T(8,128)S(1)} %get-tuple-element.31.refs_1_.near_two, f32[2,2,128,128]{3,2,1,0:T(8,128)S(1)} %get-tuple-element.27._.refs_0_, ...), custom_call_target="tpu_custom_call" | custom-call | tf_op jit(solution)/shard_map/total/pallas_call | solution.py:415
  (1 shorter events, 0.0 us)
Async XLA Ops:
  1.9 10.5 %collective-permute-start.1 = (bf16[2,2,128,128]{3,2,1,0:T(8,128)(2,1)S(1)}, bf16[2,2,128,128]{3,2,1,0:T(8,128)(2,1)S(1)}, u32[]{:S(2)}, u32[]{:S(2)}) collective-permute-start(bf16[2,2,128,128]{3,2,1,0:T(8,128)(2,1)S(1)} %pack.1.kv_ref.refs_0_), channel_id=1, source_target_pairs={{0,8},{4,12},{8,0},{12,4},{1,9},{5,13},{9,1},{13,5},{2,10},{6,14},... | collective-permute-start | bytes 393224 | tf_op jit(solution)/shard_map/ppermute | solution.py:284
  6.0 10.3 %collective-permute-start = (bf16[2,2,128,128]{3,2,1,0:T(8,128)(2,1)S(1)}, bf16[2,2,128,128]{3,2,1,0:T(8,128)(2,1)S(1)}, u32[]{:S(2)}, u32[]{:S(2)}) collective-permute-start(bf16[2,2,128,128]{3,2,1,0:T(8,128)(2,1)S(1)} %pack.1.kv_ref.refs_0_), channel_id=1, source_target_pairs={{0,4},{4,0},{8,12},{12,8},{1,5},{5,1},{9,13},{13,9},{2,6},{6,2},{1... | collective-permute-start | bytes 393224 | tf_op jit(solution)/shard_map/ppermute | solution.py:284
  12.4 5.0 %collective-permute-start.2 = (bf16[2,2,128,128]{3,2,1,0:T(8,128)(2,1)S(1)}, bf16[2,2,128,128]{3,2,1,0:T(8,128)(2,1)S(1)}, u32[]{:S(2)}, u32[]{:S(2)}) collective-permute-start(bf16[2,2,128,128]{3,2,1,0:T(8,128)(2,1)S(1)} %collective-permute-done.1.refs_2_), channel_id=1, source_target_pairs={{0,4},{4,0},{8,12},{12,8},{1,5},{5,1},{9,13},{13,9},{2,6},{6,2},{1... | collective-permute-start | bytes 393224 | tf_op jit(solution)/shard_map/ppermute | solution.py:284
  17.5 1.6 %collective-permute-start.3 = (bf16[2,2,2,128,128]{4,3,2,1,0:T(8,128)(2,1)S(1)}, bf16[2,2,2,128,128]{4,3,2,1,0:T(8,128)(2,1)S(1)}, u32[]{:S(2)}, u32[]{:S(2)}) collective-permute-start(bf16[2,2,2,128,128]{4,3,2,1,0:T(8,128)(2,1)S(1)} %choose.1), channel_id=1, source_target_pairs={{0,1},{1,0},{2,3},{3,2},{4,5},{5,4},{6,7},{7,6},{8,9},{9,8},{10,11... | collective-permute-start | bytes 786440 | tf_op jit(solution)/shard_map/ppermute | solution.py:287
  21.5 1.6 %collective-permute-start.4 = (bf16[2,2,2,128,128]{4,3,2,1,0:T(8,128)(2,1)S(1)}, bf16[2,2,2,128,128]{4,3,2,1,0:T(8,128)(2,1)S(1)}, u32[]{:S(2)}, u32[]{:S(2)}) collective-permute-start(bf16[2,2,2,128,128]{4,3,2,1,0:T(8,128)(2,1)S(1)} %listed_keys.1.mine_ref), channel_id=1, source_target_pairs={{0,1},{1,0},{2,3},{3,2},{4,5},{5,4},{6,7},{7,6},{8,9},{9,8},{10,11... | collective-permute-start | bytes 786440 | tf_op jit(solution)/shard_map/ppermute | solution.py:287
  23.6 6.4 %collective-permute-start.5 = (bf16[2,2,128,128]{3,2,1,0:T(8,128)(2,1)S(1)}, bf16[2,2,128,128]{3,2,1,0:T(8,128)(2,1)S(1)}, u32[]{:S(2)}, u32[]{:S(2)}) collective-permute-start(bf16[2,2,128,128]{3,2,1,0:T(8,128)(2,1)S(1)} %get-tuple-element.30), channel_id=1, source_target_pairs={{0,4},{4,0},{8,12},{12,8},{1,5},{5,1},{9,13},{13,9},{2,6},{6,2},{1... | collective-permute-start | bytes 393224 | tf_op jit(solution)/shard_map/ppermute | solution.py:284
  24.7 12.6 %collective-permute-start.6 = (bf16[2,2,128,128]{3,2,1,0:T(8,128)(2,1)S(1)}, bf16[2,2,128,128]{3,2,1,0:T(8,128)(2,1)S(1)}, u32[]{:S(2)}, u32[]{:S(2)}) collective-permute-start(bf16[2,2,128,128]{3,2,1,0:T(8,128)(2,1)S(1)} %get-tuple-element.32), channel_id=1, source_target_pairs={{0,4},{4,0},{8,12},{12,8},{1,5},{5,1},{9,13},{13,9},{2,6},{6,2},{1... | collective-permute-start | bytes 393224 | tf_op jit(solution)/shard_map/ppermute | solution.py:284
  30.0 8.1 %collective-permute-start.7 = (bf16[2,2,128,128]{3,2,1,0:T(8,128)(2,1)S(1)}, bf16[2,2,128,128]{3,2,1,0:T(8,128)(2,1)S(1)}, u32[]{:S(2)}, u32[]{:S(2)}) collective-permute-start(bf16[2,2,128,128]{3,2,1,0:T(8,128)(2,1)S(1)} %merge.1.refs_10_), channel_id=1, source_target_pairs={{0,8},{4,12},{8,0},{12,4},{1,9},{5,13},{9,1},{13,5},{2,10},{6,14},... | collective-permute-start | bytes 393224 | tf_op jit(solution)/shard_map/ppermute | solution.py:284

commit v4 on v3

--- a/solution.py
+++ b/solution.py
@@ -216,11 +216,13 @@
             dkv_ref[which, 1, head] = grad_val[which * tokens:(which + 1) * tokens]
 
 
-def query_kernel(factor, rows, places_ref, *refs):
+def query_kernel(factor, rows, ready, places_ref, *refs):
     *column, other_ref, held_ref, norm_ref, term_ref, near_one, near_two, _, dq_ref = refs
     tokens, grouped, head_dim = held_ref.shape[2:]
     half = near_one.shape[1] // grouped
-    for head in range(held_ref.shape[1]):
+    if ready:
+        dq_ref[:, :ready * grouped] = near_one[...]
+    for head in range(ready, dq_ref.shape[1] // grouped):
         near_ref, place = (near_one, head) if head < half else (near_two, head - half)
         key_blk, value_blk = far_blocks(places_ref, column, other_ref, head)
         for toks, cols, query_blk, upstream in row_blocks(held_ref, head, rows):
@@ -251,11 +253,12 @@
 
 
 def merge_kernel(own_ref, *refs):
-    *arrived, _, out_ref = refs
+    *arrived, later_ref, _, out_ref, later_out = refs
     total = own_ref[...]
     for ref in arrived:
         total += ref[...].astype(jnp.float32)
     out_ref[...] = total.astype(out_ref.dtype)
+    later_out[...] = later_ref[...]
 
 
 def total_kernel(near_one, near_two, *refs):
@@ -382,35 +385,44 @@
         name="combine",
     )(places, far_kv, other_kv)
 
-    after, last = sums[0], (near_kv, near_query)
+    def queries_of(count, ready, near_one, near_two, after):
+        share = count - ready
+        return pl.pallas_call(
+            functools.partial(query_kernel, factor, rows, ready),
+            in_specs=[VMEM_SPEC] * (2 + ring) + row_specs + [VMEM_SPEC] * 2 + [ANY_SPEC],
+            out_specs=VMEM_SPEC,
+            out_shape=jax.ShapeDtypeStruct((tokens, count * grouped, head_dim), jnp.float32),
+            compiler_params=params,
+            cost_estimate=pl.CostEstimate(
+                flops=6 * work * share // kv_heads, bytes_accessed=3 * moved * share // kv_heads, transcendentals=0
+            ),
+            name="listed_queries",
+        )(places, *column, other, held, norm, term, near_one, near_two, after)
+
+    after, last, ready = sums[0], (near_kv, near_query), 0
     if half < kv_heads:
         last = local(half, kv_heads - half, after)
-        after = last[0]
+        near_query = queries_of(half, 0, near_query, last[1], last[0])
+        after, ready = near_query, half
     arrived = {place: [] for place in range(ring)}
-    for place in sorted(range(1, ring), key=lambda place: (place & -place, -place)):
+    later = sums[1]
+    for place in sorted(range(2, ring), key=lambda place: (place & -place, -place)):
         low = place & -place
         block = sums[place]
         if arrived[place]:
-            block = pl.pallas_call(
+            block, later = pl.pallas_call(
                 merge_kernel,
-                in_specs=[VMEM_SPEC] * (1 + len(arrived[place])) + [ANY_SPEC],
-                out_specs=VMEM_SPEC,
-                out_shape=jax.ShapeDtypeStruct(span_shape, jnp.bfloat16),
+                in_specs=[VMEM_SPEC] * (2 + len(arrived[place])) + [ANY_SPEC],
+                out_specs=[VMEM_SPEC] * 2,
+                out_shape=[jax.ShapeDtypeStruct(span_shape, jnp.bfloat16)] * 2,
                 compiler_params=params,
                 name="merge",
-            )(block, *arrived[place], after)
+            )(block, *arrived[place], later, after)
             after = block
         arrived[place ^ low].append(crossed(block, low))
-
-    grad_queries = pl.pallas_call(
-        functools.partial(query_kernel, factor, rows),
-        in_specs=[VMEM_SPEC] * (2 + ring) + row_specs + [VMEM_SPEC] * 2 + [ANY_SPEC],
-        out_specs=VMEM_SPEC,
-        out_shape=jax.ShapeDtypeStruct((tokens, heads, head_dim), jnp.float32),
-        compiler_params=params,
-        cost_estimate=pl.CostEstimate(flops=6 * work, bytes_accessed=3 * moved, transcendentals=0),
-        name="listed_queries",
-    )(places, *column, other, held, norm, term, near_query, last[1], after)
+    arrived[0].append(crossed(later, 1))
+
+    grad_queries = queries_of(kv_heads, ready, near_query, last[1], after)
 
     grad_keys, grad_values = pl.pallas_call(
         total_kernel,

time: 39.2 us -> 39.2 us (level)
  waiting for transfers between devices: 12.6 us -> 11.6 us
  starting transfers between devices: 11.4 us -> 12.2 us
    ppermute x6, waiting for transfers between devices: 9.72 us -> 8.66 us  [crossed(): return lax.ppermute(array, 'ctx', [(i, i ^ bit) for i in range(ring)])]
    ppermute x6, starting transfers between devices: 11.2 us -> 11.9 us  [crossed(): return lax.ppermute(array, 'ctx', [(i, i ^ bit) for i in range(ring)])]
    pallas_call x2 -> x3, Pallas kernels: 4.54 us -> 4.81 us  [the longest x2 4.78 us: queries_of(): pl.pallas_call(functools.partial(query_kernel, factor, rows, ready), in_s...]
  transfers between devices with their start and end apart: 8 -> 8, of which waited for: 6 -> 7; matrix products, arithmetic and copies ran while one was open for 0% -> 0% of each run, Pallas kernels for 23% -> 24%
where the time goes in v4:
time: 39.2 us; the launch traced here: 39 us
  Pallas kernels  14.5 us (37%)
  starting transfers between devices  12.2 us (31%)
  waiting for transfers between devices  11.6 us (30%)
  between operations  0.7 us (2%)
    ppermute x6, starting transfers between devices, crossed(): return lax.ppermute(array, 'ctx', [(i, i ^ bit) for i in range(ring)])  11.9 us
    ppermute x6, waiting for transfers between devices, crossed(): return lax.ppermute(array, 'ctx', [(i, i ^ bit) for i in range(ring)])  8.66 us
    pallas_call x2, Pallas kernels, queries_of(): pl.pallas_call(functools.partial(query_kernel, factor, rows, ready), in_s...  4.78 us
    ppermute x2, waiting for transfers between devices, swapped(): return lax.ppermute(array, 'sub', [(i, i ^ 1) for i in range(subs)])  2.92 us
    pallas_call x2, Pallas kernels, local(): pl.pallas_call(functools.partial(local_kernel, factor, rows, first), in_s...  2.63 us
    pallas_call x1, Pallas kernels, body(): pl.pallas_call(functools.partial(listed_kernel, factor, rows), in_specs=[...  2.44 us
    pallas_call x1, Pallas kernels, body(): pl.pallas_call(functools.partial(spread_kernel, grouped, ring, subs, rows...  1.98 us
    pallas_call x1, Pallas kernels, body(): pl.pallas_call(pack_kernel, in_specs=[HBM_SPEC] * 2, out_specs=VMEM_SPEC,...  1.24 us
  transfers between devices with their start and end apart: 8, of which 7 were waited for; matrix products, arithmetic and copies ran while one was open for 0% of the time, Pallas kernels for 24%

profile of v4, /device:TPU:0, one launch (start us, length us, event | category | flops | bytes accessed | tf_op | source)
XLA Modules:
  0.0 39.0 jit_solution(14179107741262275585)
XLA Ops:
  0.6 1.2 %pack.1.kv_ref.refs_0_ = bf16[2,2,128,128]{3,2,1,0:T(8,128)(2,1)S(1)} custom-call(bf16[128,2,128]{2,1,0:T(2,128)(2,1)} %key_ref.1, bf16[128,2,128]{2,1,0:T(2,128)(2,1)} %value_ref.1), custom_call_target="tpu_custom_call" | custom-call | tf_op jit(solution)/shard_map/pack/pallas_call | solution.py:296
  1.9 4.1 %collective-permute-start.1 = (bf16[2,2,128,128]{3,2,1,0:T(8,128)(2,1)S(1)}, bf16[2,2,128,128]{3,2,1,0:T(8,128)(2,1)S(1)}, u32[]{:S(2)}, u32[]{:S(2)}) collective-permute-start(bf16[2,2,128,128]{3,2,1,0:T(8,128)(2,1)S(1)} %pack.1.kv_ref.refs_0_), channel_id=1, source_target_pairs={{0,8},{4,12},{8,0},{12,4},{1,9},{5,13},{9,1},{13,5},{2,10},{6,14},... | collective-permute-start | bytes 393224 | tf_op jit(solution)/shard_map/ppermute | solution.py:287
  6.0 1.6 %collective-permute-start = (bf16[2,2,128,128]{3,2,1,0:T(8,128)(2,1)S(1)}, bf16[2,2,128,128]{3,2,1,0:T(8,128)(2,1)S(1)}, u32[]{:S(2)}, u32[]{:S(2)}) collective-permute-start(bf16[2,2,128,128]{3,2,1,0:T(8,128)(2,1)S(1)} %pack.1.kv_ref.refs_0_), channel_id=1, source_target_pairs={{0,4},{4,0},{8,12},{12,8},{1,5},{5,1},{9,13},{13,9},{2,6},{6,2},{1... | collective-permute-start | bytes 393224 | tf_op jit(solution)/shard_map/ppermute | solution.py:287
  7.6 4.8 %collective-permute-done.1.refs_2_ = bf16[2,2,128,128]{3,2,1,0:T(8,128)(2,1)S(1)} collective-permute-done((bf16[2,2,128,128]{3,2,1,0:T(8,128)(2,1)S(1)}, bf16[2,2,128,128]{3,2,1,0:T(8,128)(2,1)S(1)}, u32[]{:S(2)}, u32[]{:S(2)}) %collective-permute-start.1) | collective-permute-done | bytes 131104 | tf_op jit(solution)/shard_map/ppermute | solution.py:287
  12.4 0.6 %collective-permute-start.2 = (bf16[2,2,128,128]{3,2,1,0:T(8,128)(2,1)S(1)}, bf16[2,2,128,128]{3,2,1,0:T(8,128)(2,1)S(1)}, u32[]{:S(2)}, u32[]{:S(2)}) collective-permute-start(bf16[2,2,128,128]{3,2,1,0:T(8,128)(2,1)S(1)} %collective-permute-done.1.refs_2_), channel_id=1, source_target_pairs={{0,4},{4,0},{8,12},{12,8},{1,5},{5,1},{9,13},{13,9},{2,6},{6,2},{1... | collective-permute-start | bytes 393224 | tf_op jit(solution)/shard_map/ppermute | solution.py:287
  13.0 2.0 %spread.1 = (f32[2,1,2048]{2,1,0:T(1,128)S(1)}, f32[2,1,2048]{2,1,0:T(1,128)S(1)}, f32[1,2048]{1,0:T(1,128)S(1)}, f32[128,128]{1,0:T(8,128)S(1)}, s32[8,128]{1,0...) custom-call(f32[32,128]{1,0:T(8,128)} %bitcast.4, f32[32,128]{1,0:T(8,128)} %bitcast.5, s32[1,128]{1,0:T(1,128)} %bitcast.7, ...), custom_call_target="tpu_custom_call" | custom-call | tf_op jit(solution)/shard_map/spread/pallas_call | solution.py:311
  15.0 1.3 %local_block.2 = (f32[2,1,128,128]{3,2,1,0:T(8,128)S(1)}, f32[128,16,128]{2,1,0:T(8,128)S(1)}) custom-call(bf16[2,2,128,128]{3,2,1,0:T(8,128)(2,1)S(1)} %pack.1.kv_ref.refs_0_, bf16[2,2,128,16,128]{4,3,2,1,0:T(8,128)(2,1)S(1)} %get-tuple-element.22.row_ref.refs_5_, f32[2,1,2048]{2,1,0:T(1,128)S(1)} %get-tuple-element.23.norm_ref.refs_6_, ...), custom_call_target="tpu_custom_call" | custom-call | flops 335544320 | bytes 2097152 | tf_op jit(solution)/shard_map/local_block/pallas_call | solution.py:341
  16.3 0.0 collective-permute-done.refs_1_
  16.3 1.0 %collective-permute-done.2.refs_3_ = bf16[2,2,128,128]{3,2,1,0:T(8,128)(2,1)S(1)} collective-permute-done((bf16[2,2,128,128]{3,2,1,0:T(8,128)(2,1)S(1)}, bf16[2,2,128,128]{3,2,1,0:T(8,128)(2,1)S(1)}, u32[]{:S(2)}, u32[]{:S(2)}) %collective-permute-start.2) | collective-permute-done | bytes 131104 | tf_op jit(solution)/shard_map/ppermute | solution.py:287
  17.4 0.1 choose.1
  17.5 0.1 collective-permute-start.3
  17.6 1.5 %collective-permute-done.3.refs_4_ = bf16[2,2,2,128,128]{4,3,2,1,0:T(8,128)(2,1)S(1)} collective-permute-done((bf16[2,2,2,128,128]{4,3,2,1,0:T(8,128)(2,1)S(1)}, bf16[2,2,2,128,128]{4,3,2,1,0:T(8,128)(2,1)S(1)}, u32[]{:S(2)}, u32[]{:S(2)}) %collective-permute-start.3) | collective-permute-done | bytes 262176 | tf_op jit(solution)/shard_map/ppermute | solution.py:290
  19.1 2.4 %listed_keys.1.mine_ref = bf16[2,2,2,128,128]{4,3,2,1,0:T(8,128)(2,1)S(1)} custom-call(s32[8,128]{1,0:T(8,128)S(1)} %get-tuple-element.21._.places_ref, bf16[2,2,128,128]{3,2,1,0:T(8,128)(2,1)S(1)} %pack.1.kv_ref.refs_0_, bf16[2,2,128,128]{3,2,1,0:T(8,128)(2,1)S(1)} %collective-permute-done.refs_1_, ...), custom_call_target="tpu_custom_call" | custom-call | flops 1073741824 | bytes 2097152 | tf_op jit(solution)/shard_map/listed_keys/pallas_call | solution.py:367
  21.6 0.2 collective-permute-start.4
  21.8 1.4 %collective-permute-done.4.other_ref = bf16[2,2,2,128,128]{4,3,2,1,0:T(8,128)(2,1)S(1)} collective-permute-done((bf16[2,2,2,128,128]{4,3,2,1,0:T(8,128)(2,1)S(1)}, bf16[2,2,2,128,128]{4,3,2,1,0:T(8,128)(2,1)S(1)}, u32[]{:S(2)}, u32[]{:S(2)}) %collective-permute-start.4) | collective-permute-done | bytes 262176 | tf_op jit(solution)/shard_map/ppermute | solution.py:290
  23.2 0.4 %combine.1 = (f32[2,2,128,128]{3,2,1,0:T(8,128)S(1)}, bf16[2,2,128,128]{3,2,1,0:T(8,128)(2,1)S(1)}, f32[2,2,128,128]{3,2,1,0:T(8,128)S(1)}, bf16[2,2,128,128]{3,2,1,0:T(8,128)(2,1)S(1)}) custom-call(s32[8,128]{1,0:T(8,128)S(1)} %get-tuple-element.21._.places_ref, bf16[2,2,2,128,128]{4,3,2,1,0:T(8,128)(2,1)S(1)} %listed_keys.1.mine_ref, ...), custom_call_target="tpu_custom_call" | custom-call | tf_op jit(solution)/shard_map/combine/pallas_call | solution.py:377
  23.6 1.1 %collective-permute-start.5 = (bf16[2,2,128,128]{3,2,1,0:T(8,128)(2,1)S(1)}, bf16[2,2,128,128]{3,2,1,0:T(8,128)(2,1)S(1)}, u32[]{:S(2)}, u32[]{:S(2)}) collective-permute-start(bf16[2,2,128,128]{3,2,1,0:T(8,128)(2,1)S(1)} %get-tuple-element.33), channel_id=1, source_target_pairs={{0,4},{4,0},{8,12},{12,8},{1,5},{5,1},{9,13},{13,9},{2,6},{6,2},{1... | collective-permute-start | bytes 393224 | tf_op jit(solution)/shard_map/ppermute | solution.py:287
  24.7 1.3 %local_block.3 = (f32[2,1,128,128]{3,2,1,0:T(8,128)S(1)}, f32[128,16,128]{2,1,0:T(8,128)S(1)}) custom-call(bf16[2,2,128,128]{3,2,1,0:T(8,128)(2,1)S(1)} %pack.1.kv_ref.refs_0_, bf16[2,2,128,16,128]{4,3,2,1,0:T(8,128)(2,1)S(1)} %get-tuple-element.22.row_ref.refs_5_, f32[2,1,2048]{2,1,0:T(1,128)S(1)} %get-tuple-element.23.norm_ref.refs_6_, ...), custom_call_target="tpu_custom_call" | custom-call | flops 335544320 | bytes 2097152 | tf_op jit(solution)/shard_map/local_block/pallas_call | solution.py:341
  26.0 1.7 %listed_queries.2.refs_2_.refs_8_ = f32[128,16,128]{2,1,0:T(8,128)S(1)} custom-call(s32[8,128]{1,0:T(8,128)S(1)} %get-tuple-element.21._.places_ref, bf16[2,2,128,128]{3,2,1,0:T(8,128)(2,1)S(1)} %pack.1.kv_ref.refs_0_, bf16[2,2,128,128]{3,2,1,0:T(8,128)(2,1)S(1)} %collective-permute-done.refs_1_, ...), custom_call_target="tpu_custom_call" | custom-call | flops 402653184 | bytes 3145728 | tf_op jit(solution)/shard_map/listed_queries/pallas_call | solution.py:390
  27.7 1.4 %collective-permute-done.5.refs_0_ = bf16[2,2,128,128]{3,2,1,0:T(8,128)(2,1)S(1)} collective-permute-done((bf16[2,2,128,128]{3,2,1,0:T(8,128)(2,1)S(1)}, bf16[2,2,128,128]{3,2,1,0:T(8,128)(2,1)S(1)}, u32[]{:S(2)}, u32[]{:S(2)}) %collective-permute-start.5) | collective-permute-done | bytes 131104 | tf_op jit(solution)/shard_map/ppermute | solution.py:287
  29.2 2.8 %collective-permute-start.6 = (bf16[2,2,128,128]{3,2,1,0:T(8,128)(2,1)S(1)}, bf16[2,2,128,128]{3,2,1,0:T(8,128)(2,1)S(1)}, u32[]{:S(2)}, u32[]{:S(2)}) collective-permute-start(bf16[2,2,128,128]{3,2,1,0:T(8,128)(2,1)S(1)} %get-tuple-element.35.refs_10_), channel_id=1, source_target_pairs={{0,8},{4,12},{8,0},{12,4},{1,9},{5,13},{9,1},{13,5},{2,10},{6,14},... | collective-permute-start | bytes 393224 | tf_op jit(solution)/shard_map/ppermute | solution.py:287
  32.0 1.7 %collective-permute-start.7 = (bf16[2,2,128,128]{3,2,1,0:T(8,128)(2,1)S(1)}, bf16[2,2,128,128]{3,2,1,0:T(8,128)(2,1)S(1)}, u32[]{:S(2)}, u32[]{:S(2)}) collective-permute-start(bf16[2,2,128,128]{3,2,1,0:T(8,128)(2,1)S(1)} %get-tuple-element.36), channel_id=1, source_target_pairs={{0,4},{4,0},{8,12},{12,8},{1,5},{5,1},{9,13},{13,9},{2,6},{6,2},{1... | collective-permute-start | bytes 393224 | tf_op jit(solution)/shard_map/ppermute | solution.py:287
  33.7 3.1 %listed_queries.3 = f32[128,32,128]{2,1,0:T(8,128)} custom-call(s32[8,128]{1,0:T(8,128)S(1)} %get-tuple-element.21._.places_ref, bf16[2,2,128,128]{3,2,1,0:T(8,128)(2,1)S(1)} %pack.1.kv_ref.refs_0_, bf16[2,2,128,128]{3,2,1,0:T(8,128)(2,1)S(1)} %collective-permute-done.refs_1_, bf16[2,2,128,128]{3,2,1,0:T(8,128)(2,1)S(1)} %collective-permute-done.1.refs_2_, ...), custom_call_target="tpu_custom_call" | custom-call | flops 402653184 | bytes 3145728 | tf_op jit(solution)/shard_map/listed_queries/pallas_call | solution.py:390
  36.8 1.1 %collective-permute-done.6.refs_1_ = bf16[2,2,128,128]{3,2,1,0:T(8,128)(2,1)S(1)} collective-permute-done((bf16[2,2,128,128]{3,2,1,0:T(8,128)(2,1)S(1)}, bf16[2,2,128,128]{3,2,1,0:T(8,128)(2,1)S(1)}, u32[]{:S(2)}, u32[]{:S(2)}) %collective-permute-start.6) | collective-permute-done | bytes 131104 | tf_op jit(solution)/shard_map/ppermute | solution.py:287
  37.9 0.3 collective-permute-done.7.refs_2_
  38.1 0.8 %total.1 = (f32[128,2,128]{2,1,0:T(2,128)}, f32[128,2,128]{2,1,0:T(2,128)}) custom-call(f32[2,1,128,128]{3,2,1,0:T(8,128)S(1)} %get-tuple-element.27.refs_4_.near_one, f32[2,1,128,128]{3,2,1,0:T(8,128)S(1)} %get-tuple-element.31.refs_10_.near_two, f32[2,2,128,128]{3,2,1,0:T(8,128)S(1)} %get-tuple-element.29._.refs_0_, ...), custom_call_target="tpu_custom_call" | custom-call | tf_op jit(solution)/shard_map/total/pallas_call | solution.py:427
  (1 shorter events, 0.0 us)
Async XLA Ops:
  1.9 10.5 %collective-permute-start.1 = (bf16[2,2,128,128]{3,2,1,0:T(8,128)(2,1)S(1)}, bf16[2,2,128,128]{3,2,1,0:T(8,128)(2,1)S(1)}, u32[]{:S(2)}, u32[]{:S(2)}) collective-permute-start(bf16[2,2,128,128]{3,2,1,0:T(8,128)(2,1)S(1)} %pack.1.kv_ref.refs_0_), channel_id=1, source_target_pairs={{0,8},{4,12},{8,0},{12,4},{1,9},{5,13},{9,1},{13,5},{2,10},{6,14},... | collective-permute-start | bytes 393224 | tf_op jit(solution)/shard_map/ppermute | solution.py:287
  6.0 10.3 %collective-permute-start = (bf16[2,2,128,128]{3,2,1,0:T(8,128)(2,1)S(1)}, bf16[2,2,128,128]{3,2,1,0:T(8,128)(2,1)S(1)}, u32[]{:S(2)}, u32[]{:S(2)}) collective-permute-start(bf16[2,2,128,128]{3,2,1,0:T(8,128)(2,1)S(1)} %pack.1.kv_ref.refs_0_), channel_id=1, source_target_pairs={{0,4},{4,0},{8,12},{12,8},{1,5},{5,1},{9,13},{13,9},{2,6},{6,2},{1... | collective-permute-start | bytes 393224 | tf_op jit(solution)/shard_map/ppermute | solution.py:287
  12.4 5.0 %collective-permute-start.2 = (bf16[2,2,128,128]{3,2,1,0:T(8,128)(2,1)S(1)}, bf16[2,2,128,128]{3,2,1,0:T(8,128)(2,1)S(1)}, u32[]{:S(2)}, u32[]{:S(2)}) collective-permute-start(bf16[2,2,128,128]{3,2,1,0:T(8,128)(2,1)S(1)} %collective-permute-done.1.refs_2_), channel_id=1, source_target_pairs={{0,4},{4,0},{8,12},{12,8},{1,5},{5,1},{9,13},{13,9},{2,6},{6,2},{1... | collective-permute-start | bytes 393224 | tf_op jit(solution)/shard_map/ppermute | solution.py:287
  17.5 1.6 %collective-permute-start.3 = (bf16[2,2,2,128,128]{4,3,2,1,0:T(8,128)(2,1)S(1)}, bf16[2,2,2,128,128]{4,3,2,1,0:T(8,128)(2,1)S(1)}, u32[]{:S(2)}, u32[]{:S(2)}) collective-permute-start(bf16[2,2,2,128,128]{4,3,2,1,0:T(8,128)(2,1)S(1)} %choose.1), channel_id=1, source_target_pairs={{0,1},{1,0},{2,3},{3,2},{4,5},{5,4},{6,7},{7,6},{8,9},{9,8},{10,11... | collective-permute-start | bytes 786440 | tf_op jit(solution)/shard_map/ppermute | solution.py:290
  21.6 1.6 %collective-permute-start.4 = (bf16[2,2,2,128,128]{4,3,2,1,0:T(8,128)(2,1)S(1)}, bf16[2,2,2,128,128]{4,3,2,1,0:T(8,128)(2,1)S(1)}, u32[]{:S(2)}, u32[]{:S(2)}) collective-permute-start(bf16[2,2,2,128,128]{4,3,2,1,0:T(8,128)(2,1)S(1)} %listed_keys.1.mine_ref), channel_id=1, source_target_pairs={{0,1},{1,0},{2,3},{3,2},{4,5},{5,4},{6,7},{7,6},{8,9},{9,8},{10,11... | collective-permute-start | bytes 786440 | tf_op jit(solution)/shard_map/ppermute | solution.py:290
  23.6 5.6 %collective-permute-start.5 = (bf16[2,2,128,128]{3,2,1,0:T(8,128)(2,1)S(1)}, bf16[2,2,128,128]{3,2,1,0:T(8,128)(2,1)S(1)}, u32[]{:S(2)}, u32[]{:S(2)}) collective-permute-start(bf16[2,2,128,128]{3,2,1,0:T(8,128)(2,1)S(1)} %get-tuple-element.33), channel_id=1, source_target_pairs={{0,4},{4,0},{8,12},{12,8},{1,5},{5,1},{9,13},{13,9},{2,6},{6,2},{1... | collective-permute-start | bytes 393224 | tf_op jit(solution)/shard_map/ppermute | solution.py:287
  29.2 8.7 %collective-permute-start.6 = (bf16[2,2,128,128]{3,2,1,0:T(8,128)(2,1)S(1)}, bf16[2,2,128,128]{3,2,1,0:T(8,128)(2,1)S(1)}, u32[]{:S(2)}, u32[]{:S(2)}) collective-permute-start(bf16[2,2,128,128]{3,2,1,0:T(8,128)(2,1)S(1)} %get-tuple-element.35.refs_10_), channel_id=1, source_target_pairs={{0,8},{4,12},{8,0},{12,4},{1,9},{5,13},{9,1},{13,5},{2,10},{6,14},... | collective-permute-start | bytes 393224 | tf_op jit(solution)/shard_map/ppermute | solution.py:287
  32.0 6.2 %collective-permute-start.7 = (bf16[2,2,128,128]{3,2,1,0:T(8,128)(2,1)S(1)}, bf16[2,2,128,128]{3,2,1,0:T(8,128)(2,1)S(1)}, u32[]{:S(2)}, u32[]{:S(2)}) collective-permute-start(bf16[2,2,128,128]{3,2,1,0:T(8,128)(2,1)S(1)} %get-tuple-element.36), channel_id=1, source_target_pairs={{0,4},{4,0},{8,12},{12,8},{1,5},{5,1},{9,13},{13,9},{2,6},{6,2},{1... | collective-permute-start | bytes 393224 | tf_op jit(solution)/shard_map/ppermute | solution.py:287

commit v5 on v1

--- a/solution.py
+++ b/solution.py
@@ -11,7 +11,6 @@
 KVH = 4
 LOG2E = 1.4426950408889634
 ROWS = 512
-PARTS = 1
 VMEM_LIMIT = 24 * 1024 * 1024
 
 VMEM_SPEC = pl.BlockSpec(memory_space=pltpu.VMEM)
@@ -107,14 +106,11 @@
         span = jnp.broadcast_to(span, (2, places_ref.shape[1])).astype(jnp.int32)
         return span // subs, span % subs
 
-    def around(gap):
-        return jnp.where(gap < 0, gap + ring, gap)
-
     (mine, mine_sub), (other, other_sub) = listed_by(sub), listed_by(1 - sub)
-    places_ref[0:2] = around(ctx - other)
-    places_ref[2:4] = jnp.where(mine_sub == sub, around(ctx - mine), ring)
-    places_ref[4:6] = jnp.where(mine_sub == sub, around(mine - ctx), ring)
-    places_ref[6:8] = jnp.where(other_sub == sub, around(other - ctx), ring)
+    places_ref[0:2] = other ^ ctx
+    places_ref[2:4] = jnp.where(mine_sub == sub, mine ^ ctx, ring)
+    places_ref[4:6] = places_ref[2:4]
+    places_ref[6:8] = jnp.where(other_sub == sub, other ^ ctx, ring)
 
     pieces = []
     for value in (held_ref[0] * LOG2E, held_ref[1]):
@@ -149,7 +145,7 @@
         row = places_ref[which:which + 1]
         for kind in range(2):
             for head in range(out_ref.shape[2]):
-                out_ref[which, kind, head] = pick_block([ref[kind, head] for ref in column], row)
+                out_ref[which, kind, head] = pick_block([ref[kind, head] for ref in column[::-1]], row)
 
 
 def far_blocks(places_ref, column, other_ref, head):
@@ -157,7 +153,7 @@
         jnp.concatenate(
             [
                 pick_block(
-                    [ref[kind, head] for ref in column] + [other_ref[which, kind, head]],
+                    [ref[kind, head] for ref in column[::-1]] + [other_ref[which, kind, head]],
                     places_ref[2 + which:3 + which],
                 )
                 for which in range(2)
@@ -277,12 +273,12 @@
     subs = lax.axis_size("sub")
     rows = min(ROWS, tokens * grouped)
     cols = tokens * grouped
-    parts = PARTS if kv_heads % PARTS == 0 else 1
+    parts = 1
     each = kv_heads // parts
     span_shape = (2, each, tokens, head_dim)
 
-    def shifted(array, shift):
-        return lax.ppermute(array, "ctx", [(i, (i + shift) % ring) for i in range(ring)])
+    def crossed(blocks):
+        return [lax.ppermute(blocks[e], "ctx", [(i, i ^ e) for i in range(ring)]) for e in range(ring - 1, 0, -1)]
 
     def swapped(array):
         return lax.ppermute(array, "sub", [(i, i ^ 1) for i in range(subs)])
@@ -300,7 +296,7 @@
         compiler_params=params,
         name="pack",
     )(*in_hbm(keys, values))
-    columns = [[block] + [shifted(block, shift) for shift in range(1, ring)] for block in kv]
+    columns = [[*crossed([block] * ring), block] for block in kv]
 
     norm, term, docs, doc_col, places = pl.pallas_call(
         functools.partial(spread_kernel, grouped, ring, subs),
@@ -374,7 +370,7 @@
             compiler_params=params,
             name="combine",
         )(places, far_kv, other_kv)
-        sums += [blocks[0]] + [shifted(blocks[shift], shift) for shift in range(1, ring)]
+        sums += [blocks[0], *crossed(blocks)]
         after = blocks[0]
 
     grad_queries = pl.pallas_call(

time: 37.8 us -> 38.7 us (1.024)
  waiting for transfers between devices: 7.72 us -> 11.6 us
  starting transfers between devices: 13.1 us -> 10.5 us
    ppermute x6, waiting for transfers between devices: 4.8 us -> 8.63 us  [crossed(): lax.ppermute(blocks[e], 'ctx', [(i, i ^ e) for i in range(ring)])]
    ppermute x6, starting transfers between devices: 12.8 us -> 10.2 us  [crossed(): lax.ppermute(blocks[e], 'ctx', [(i, i ^ e) for i in range(ring)])]
  transfers between devices with their start and end apart: 8 -> 8, of which waited for: 4 -> 4; matrix products, arithmetic and copies ran while one was open for 0% -> 0% of each run, Pallas kernels for 29% -> 28%
where the time goes in v5:
time: 38.7 us; the launch traced here: 38.4 us
  Pallas kernels  15.7 us (41%)
  waiting for transfers between devices  11.6 us (30%)
  starting transfers between devices  10.5 us (27%)
  between operations  0.69 us (2%)
    ppermute x6, starting transfers between devices, crossed(): lax.ppermute(blocks[e], 'ctx', [(i, i ^ e) for i in range(ring)])  10.2 us
    ppermute x6, waiting for transfers between devices, crossed(): lax.ppermute(blocks[e], 'ctx', [(i, i ^ e) for i in range(ring)])  8.63 us
    pallas_call x1, Pallas kernels, body(): pl.pallas_call(functools.partial(local_kernel, factor, rows), in_specs=[V...  4.93 us
    pallas_call x1, Pallas kernels, body(): pl.pallas_call(functools.partial(query_kernel, factor, rows, parts), in_s...  4.51 us
    ppermute x2, waiting for transfers between devices, swapped(): return lax.ppermute(array, 'sub', [(i, i ^ 1) for i in range(subs)])  2.92 us
    pallas_call x1, Pallas kernels, body(): pl.pallas_call(functools.partial(listed_kernel, factor, rows, part * each...  2.45 us
    pallas_call x1, Pallas kernels, body(): pl.pallas_call(pack_kernel, in_specs=[HBM_SPEC] * 2, out_specs=[VMEM_SPEC...  1.24 us
    pallas_call x1, Pallas kernels, body(): pl.pallas_call(functools.partial(spread_kernel, grouped, ring, subs), in_...  1.18 us
  transfers between devices with their start and end apart: 8, of which 4 were waited for; matrix products, arithmetic and copies ran while one was open for 0% of the time, Pallas kernels for 28%

profile of v5, /device:TPU:0, one launch (start us, length us, event | category | flops | bytes accessed | tf_op | source)
XLA Modules:
  0.0 38.4 jit_solution(18029135392853971975)
XLA Ops:
  0.6 1.2 %pack.1.refs_0_.refs_3_ = bf16[2,2,128,128]{3,2,1,0:T(8,128)(2,1)S(1)} custom-call(bf16[128,2,128]{2,1,0:T(2,128)(2,1)} %key_ref.1, bf16[128,2,128]{2,1,0:T(2,128)(2,1)} %value_ref.1), custom_call_target="tpu_custom_call" | custom-call | tf_op jit(solution)/shard_map/pack/pallas_call | solution.py:290
  1.9 5.1 %collective-permute-start = (bf16[2,2,128,128]{3,2,1,0:T(8,128)(2,1)S(1)}, bf16[2,2,128,128]{3,2,1,0:T(8,128)(2,1)S(1)}, u32[]{:S(2)}, u32[]{:S(2)}) collective-permute-start(bf16[2,2,128,128]{3,2,1,0:T(8,128)(2,1)S(1)} %pack.1.refs_0_.refs_3_), channel_id=1, source_target_pairs={{0,12},{4,8},{8,4},{12,0},{1,13},{5,9},{9,5},{13,1},{2,14},{6,10},... | collective-permute-start | bytes 393224 | tf_op jit(solution)/shard_map/ppermute | solution.py:281
  7.0 0.0 collective-permute-start.1
  7.0 0.6 %collective-permute-start.2 = (bf16[2,2,128,128]{3,2,1,0:T(8,128)(2,1)S(1)}, bf16[2,2,128,128]{3,2,1,0:T(8,128)(2,1)S(1)}, u32[]{:S(2)}, u32[]{:S(2)}) collective-permute-start(bf16[2,2,128,128]{3,2,1,0:T(8,128)(2,1)S(1)} %pack.1.refs_0_.refs_3_), channel_id=1, source_target_pairs={{0,4},{4,0},{8,12},{12,8},{1,5},{5,1},{9,13},{13,9},{2,6},{6,2},{1... | collective-permute-start | bytes 393224 | tf_op jit(solution)/shard_map/ppermute | solution.py:281
  7.6 1.2 %spread.1 = (f32[2,1,2048]{2,1,0:T(1,128)S(1)}, f32[2,1,2048]{2,1,0:T(1,128)S(1)}, f32[1,2048]{1,0:T(1,128)S(1)}, f32[128,128]{1,0:T(8,128)S(1)}, s32[8,128]{1,0:T(8,128)S(1)}) custom-call(f32[32,128]{1,0:T(8,128)} %bitcast.4, f32[32,128]{1,0:T(8,128)} %bitcast.5, s32[1,128]{1,0:T(1,128)} %bitcast.7, s32[2,8]{1,0:T(2,128)} %bitcast.6), custom_call_target="tpu_custom_call" | custom-call | tf_op jit(solution)/shard_map/spread/pallas_call | solution.py:301
  8.8 4.9 %local_block.1 = (f32[2,2,128,128]{3,2,1,0:T(8,128)S(1)}, f32[128,32,128]{2,1,0:T(8,128)S(1)}, bf16[2,2,128,16,128]{4,3,2,1,0:T(8,128)(2,1)S(1)}) custom-call(bf16[2,2,128,128]{3,2,1,0:T(8,128)(2,1)S(1)} %pack.1.refs_0_.refs_3_, bf16[128,32,128]{2,1,0:T(8,128)(2,1)} %refs_1_.1, bf16[128,32,128]{2,1,0:T(8,128)(2,1)} %refs_2_.1, ...), custom_call_target="tpu_custom_call" | custom-call | flops 671088640 | bytes 4194304 | tf_op jit(solution)/shard_map/local_block/pallas_call | solution.py:326
  13.8 0.0 collective-permute-done.refs_0_
  13.8 4.3 %collective-permute-done.1.refs_1_ = bf16[2,2,128,128]{3,2,1,0:T(8,128)(2,1)S(1)} collective-permute-done((bf16[2,2,128,128]{3,2,1,0:T(8,128)(2,1)S(1)}, bf16[2,2,128,128]{3,2,1,0:T(8,128)(2,1)S(1)}, u32[]{:S(2)}, u32[]{:S(2)}) %collective-permute-start.1) | collective-permute-done | bytes 131104 | tf_op jit(solution)/shard_map/ppermute | solution.py:281
  18.1 0.0 collective-permute-done.2.refs_2_
  18.1 0.1 choose.1
  18.2 0.1 collective-permute-start.3
  18.3 1.5 %collective-permute-done.3.refs_4_ = bf16[2,2,2,128,128]{4,3,2,1,0:T(8,128)(2,1)S(1)} collective-permute-done((bf16[2,2,2,128,128]{4,3,2,1,0:T(8,128)(2,1)S(1)}, bf16[2,2,2,128,128]{4,3,2,1,0:T(8,128)(2,1)S(1)}, u32[]{:S(2)}, u32[]{:S(2)}) %collective-permute-start.3) | collective-permute-done | bytes 262176 | tf_op jit(solution)/shard_map/ppermute | solution.py:284
  19.8 2.4 %listed_keys.1.mine_ref = bf16[2,2,2,128,128]{4,3,2,1,0:T(8,128)(2,1)S(1)} custom-call(s32[8,128]{1,0:T(8,128)S(1)} %get-tuple-element.17.places_ref, bf16[2,2,128,128]{3,2,1,0:T(8,128)(2,1)S(1)} %collective-permute-done.refs_0_, bf16[2,2,128,128]{3,2,1,0:T(8,128)(2,1)S(1)} %collective-permute-done.1.refs_1_, ...), custom_call_target="tpu_custom_call" | custom-call | flops 1073741824 | bytes 2097152 | tf_op jit(solution)/shard_map/listed_keys/pallas_call | solution.py:354
  22.3 0.2 collective-permute-start.4
  22.5 1.4 %collective-permute-done.4.other_ref = bf16[2,2,2,128,128]{4,3,2,1,0:T(8,128)(2,1)S(1)} collective-permute-done((bf16[2,2,2,128,128]{4,3,2,1,0:T(8,128)(2,1)S(1)}, bf16[2,2,2,128,128]{4,3,2,1,0:T(8,128)(2,1)S(1)}, u32[]{:S(2)}, u32[]{:S(2)}) %collective-permute-start.4) | collective-permute-done | bytes 262176 | tf_op jit(solution)/shard_map/ppermute | solution.py:284
  23.9 0.4 %combine.1 = (f32[2,2,128,128]{3,2,1,0:T(8,128)S(1)}, bf16[2,2,128,128]{3,2,1,0:T(8,128)(2,1)S(1)}, bf16[2,2,128,128]{3,2,1,0:T(8,128)(2,1)S(1)}, bf16[2,2,128,128]{3,2,1,0:T(8,128)(2,1)S(1)}) custom-call(s32[8,128]{1,0:T(8,128)S(1)} %get-tuple-element.17.places_ref, bf16[2,2,2,128,128]{4,3,2,1,0:T(8,128)(2,1)S(1)} %listed_keys.1.mine_ref, ...), custom_call_target="tpu_custom_call" | custom-call | tf_op jit(solution)/shard_map/combine/pallas_call | solution.py:364
  24.3 2.5 %collective-permute-start.5 = (bf16[2,2,128,128]{3,2,1,0:T(8,128)(2,1)S(1)}, bf16[2,2,128,128]{3,2,1,0:T(8,128)(2,1)S(1)}, u32[]{:S(2)}, u32[]{:S(2)}) collective-permute-start(bf16[2,2,128,128]{3,2,1,0:T(8,128)(2,1)S(1)} %get-tuple-element.26), channel_id=1, source_target_pairs={{0,12},{4,8},{8,4},{12,0},{1,13},{5,9},{9,5},{13,1},{2,14},{6,10},... | collective-permute-start | bytes 393224 | tf_op jit(solution)/shard_map/ppermute | solution.py:281
  26.8 0.0 collective-permute-start.6
  26.8 1.9 %collective-permute-start.7 = (bf16[2,2,128,128]{3,2,1,0:T(8,128)(2,1)S(1)}, bf16[2,2,128,128]{3,2,1,0:T(8,128)(2,1)S(1)}, u32[]{:S(2)}, u32[]{:S(2)}) collective-permute-start(bf16[2,2,128,128]{3,2,1,0:T(8,128)(2,1)S(1)} %get-tuple-element.28), channel_id=1, source_target_pairs={{0,4},{4,0},{8,12},{12,8},{1,5},{5,1},{9,13},{13,9},{2,6},{6,2},{1... | collective-permute-start | bytes 393224 | tf_op jit(solution)/shard_map/ppermute | solution.py:281
  28.7 4.5 %listed_queries.1 = f32[128,32,128]{2,1,0:T(8,128)} custom-call(s32[8,128]{1,0:T(8,128)S(1)} %get-tuple-element.17.places_ref, bf16[2,2,128,128]{3,2,1,0:T(8,128)(2,1)S(1)} %collective-permute-done.refs_0_, bf16[2,2,128,128]{3,2,1,0:T(8,128)(2,1)S(1)} %collective-permute-done.1.refs_1_, bf16[2,2,128,128]{3,2,1,0:T(8,128)(2,1)S(1)} %collective-permute-done.2.refs_2_, ...), custom_call_target="tpu_custom_call" | custom-call | flops 805306368 | bytes 6291456 | tf_op jit(solution)/shard_map/listed_queries/pallas_call | solution.py:376
  33.2 0.0 collective-permute-done.5.refs_1_
  33.2 4.3 %collective-permute-done.6.refs_2_ = bf16[2,2,128,128]{3,2,1,0:T(8,128)(2,1)S(1)} collective-permute-done((bf16[2,2,128,128]{3,2,1,0:T(8,128)(2,1)S(1)}, bf16[2,2,128,128]{3,2,1,0:T(8,128)(2,1)S(1)}, u32[]{:S(2)}, u32[]{:S(2)}) %collective-permute-start.6) | collective-permute-done | bytes 131104 | tf_op jit(solution)/shard_map/ppermute | solution.py:281
  37.6 0.0 collective-permute-done.7.refs_3_
  37.6 0.8 %total.1 = (f32[128,2,128]{2,1,0:T(2,128)}, f32[128,2,128]{2,1,0:T(2,128)}) custom-call(f32[2,2,128,128]{3,2,1,0:T(8,128)S(1)} %get-tuple-element.22.refs_4_.refs_5_.near_ref, f32[2,2,128,128]{3,2,1,0:T(8,128)S(1)} %get-tuple-element.25.refs_9_.refs_0_, bf16[2,2,128,128]{3,2,1,0:T(8,128)(2,1)S(1)} %collective-permute-done.5.refs_1_, ...), custom_call_target="tpu_custom_call" | custom-call | tf_op jit(solution)/shard_map/total/pallas_call | solution.py:386
Async XLA Ops:
  1.9 11.9 %collective-permute-start = (bf16[2,2,128,128]{3,2,1,0:T(8,128)(2,1)S(1)}, bf16[2,2,128,128]{3,2,1,0:T(8,128)(2,1)S(1)}, u32[]{:S(2)}, u32[]{:S(2)}) collective-permute-start(bf16[2,2,128,128]{3,2,1,0:T(8,128)(2,1)S(1)} %pack.1.refs_0_.refs_3_), channel_id=1, source_target_pairs={{0,12},{4,8},{8,4},{12,0},{1,13},{5,9},{9,5},{13,1},{2,14},{6,10},... | collective-permute-start | bytes 393224 | tf_op jit(solution)/shard_map/ppermute | solution.py:281
  7.0 11.1 %collective-permute-start.1 = (bf16[2,2,128,128]{3,2,1,0:T(8,128)(2,1)S(1)}, bf16[2,2,128,128]{3,2,1,0:T(8,128)(2,1)S(1)}, u32[]{:S(2)}, u32[]{:S(2)}) collective-permute-start(bf16[2,2,128,128]{3,2,1,0:T(8,128)(2,1)S(1)} %pack.1.refs_0_.refs_3_), channel_id=1, source_target_pairs={{0,8},{4,12},{8,0},{12,4},{1,9},{5,13},{9,1},{13,5},{2,10},{6,14},... | collective-permute-start | bytes 393224 | tf_op jit(solution)/shard_map/ppermute | solution.py:281
  7.0 11.1 %collective-permute-start.2 = (bf16[2,2,128,128]{3,2,1,0:T(8,128)(2,1)S(1)}, bf16[2,2,128,128]{3,2,1,0:T(8,128)(2,1)S(1)}, u32[]{:S(2)}, u32[]{:S(2)}) collective-permute-start(bf16[2,2,128,128]{3,2,1,0:T(8,128)(2,1)S(1)} %pack.1.refs_0_.refs_3_), channel_id=1, source_target_pairs={{0,4},{4,0},{8,12},{12,8},{1,5},{5,1},{9,13},{13,9},{2,6},{6,2},{1... | collective-permute-start | bytes 393224 | tf_op jit(solution)/shard_map/ppermute | solution.py:281
  18.2 1.6 %collective-permute-start.3 = (bf16[2,2,2,128,128]{4,3,2,1,0:T(8,128)(2,1)S(1)}, bf16[2,2,2,128,128]{4,3,2,1,0:T(8,128)(2,1)S(1)}, u32[]{:S(2)}, u32[]{:S(2)}) collective-permute-start(bf16[2,2,2,128,128]{4,3,2,1,0:T(8,128)(2,1)S(1)} %choose.1), channel_id=1, source_target_pairs={{0,1},{1,0},{2,3},{3,2},{4,5},{5,4},{6,7},{7,6},{8,9},{9,8},{10,11... | collective-permute-start | bytes 786440 | tf_op jit(solution)/shard_map/ppermute | solution.py:284
  22.3 1.6 %collective-permute-start.4 = (bf16[2,2,2,128,128]{4,3,2,1,0:T(8,128)(2,1)S(1)}, bf16[2,2,2,128,128]{4,3,2,1,0:T(8,128)(2,1)S(1)}, u32[]{:S(2)}, u32[]{:S(2)}) collective-permute-start(bf16[2,2,2,128,128]{4,3,2,1,0:T(8,128)(2,1)S(1)} %listed_keys.1.mine_ref), channel_id=1, source_target_pairs={{0,1},{1,0},{2,3},{3,2},{4,5},{5,4},{6,7},{7,6},{8,9},{9,8},{10,11... | collective-permute-start | bytes 786440 | tf_op jit(solution)/shard_map/ppermute | solution.py:284
  24.3 9.0 %collective-permute-start.5 = (bf16[2,2,128,128]{3,2,1,0:T(8,128)(2,1)S(1)}, bf16[2,2,128,128]{3,2,1,0:T(8,128)(2,1)S(1)}, u32[]{:S(2)}, u32[]{:S(2)}) collective-permute-start(bf16[2,2,128,128]{3,2,1,0:T(8,128)(2,1)S(1)} %get-tuple-element.26), channel_id=1, source_target_pairs={{0,12},{4,8},{8,4},{12,0},{1,13},{5,9},{9,5},{13,1},{2,14},{6,10},... | collective-permute-start | bytes 393224 | tf_op jit(solution)/shard_map/ppermute | solution.py:281
  26.8 10.8 %collective-permute-start.6 = (bf16[2,2,128,128]{3,2,1,0:T(8,128)(2,1)S(1)}, bf16[2,2,128,128]{3,2,1,0:T(8,128)(2,1)S(1)}, u32[]{:S(2)}, u32[]{:S(2)}) collective-permute-start(bf16[2,2,128,128]{3,2,1,0:T(8,128)(2,1)S(1)} %get-tuple-element.27), channel_id=1, source_target_pairs={{0,8},{4,12},{8,0},{12,4},{1,9},{5,13},{9,1},{13,5},{2,10},{6,14},... | collective-permute-start | bytes 393224 | tf_op jit(solution)/shard_map/ppermute | solution.py:281
  26.8 10.8 %collective-permute-start.7 = (bf16[2,2,128,128]{3,2,1,0:T(8,128)(2,1)S(1)}, bf16[2,2,128,128]{3,2,1,0:T(8,128)(2,1)S(1)}, u32[]{:S(2)}, u32[]{:S(2)}) collective-permute-start(bf16[2,2,128,128]{3,2,1,0:T(8,128)(2,1)S(1)} %get-tuple-element.28), channel_id=1, source_target_pairs={{0,4},{4,0},{8,12},{12,8},{1,5},{5,1},{9,13},{13,9},{2,6},{6,2},{1... | collective-permute-start | bytes 393224 | tf_op jit(solution)/shard_map/ppermute | solution.py:281

commit v6 on v5

--- a/solution.py
+++ b/solution.py
@@ -35,6 +35,15 @@
 def chunks(tokens, grouped, rows):
     step = rows // grouped
     return [(i, slice(i * step, (i + 1) * step), slice(i * rows, (i + 1) * rows)) for i in range(tokens // step)]
+
+
+def send_order(ring):
+    return sorted(range(ring), key=lambda e: (-e.bit_length(), e))
+
+
+def by_place(column):
+    order = send_order(len(column))
+    return [column[order.index(e)] for e in range(len(column))]
 
 
 def start_all(sources, targets, sems):
@@ -145,7 +154,7 @@
         row = places_ref[which:which + 1]
         for kind in range(2):
             for head in range(out_ref.shape[2]):
-                out_ref[which, kind, head] = pick_block([ref[kind, head] for ref in column[::-1]], row)
+                out_ref[which, kind, head] = pick_block([ref[kind, head] for ref in by_place(column)], row)
 
 
 def far_blocks(places_ref, column, other_ref, head):
@@ -153,7 +162,7 @@
         jnp.concatenate(
             [
                 pick_block(
-                    [ref[kind, head] for ref in column[::-1]] + [other_ref[which, kind, head]],
+                    [ref[kind, head] for ref in by_place(column)] + [other_ref[which, kind, head]],
                     places_ref[2 + which:3 + which],
                 )
                 for which in range(2)
@@ -278,7 +287,7 @@
     span_shape = (2, each, tokens, head_dim)
 
     def crossed(blocks):
-        return [lax.ppermute(blocks[e], "ctx", [(i, i ^ e) for i in range(ring)]) for e in range(ring - 1, 0, -1)]
+        return [lax.ppermute(blocks[e], "ctx", [(i, i ^ e) for i in range(ring)]) for e in send_order(ring)[:-1]]
 
     def swapped(array):
         return lax.ppermute(array, "sub", [(i, i ^ 1) for i in range(subs)])

time: 38.7 us -> 38.7 us (level)
  transfers between devices with their start and end apart: 8 -> 8, of which waited for: 4 -> 6; matrix products, arithmetic and copies ran while one was open for 0% -> 0% of each run, Pallas kernels for 28% -> 28%
where the time goes in v6:
time: 38.7 us; the launch traced here: 38.5 us
  Pallas kernels  15.7 us (41%)
  waiting for transfers between devices  11.3 us (29%)
  starting transfers between devices  10.8 us (28%)
  between operations  0.68 us (2%)
    ppermute x6, starting transfers between devices, crossed(): lax.ppermute(blocks[e], 'ctx', [(i, i ^ e) for i in range(ring)])  10.5 us
    ppermute x6, waiting for transfers between devices, crossed(): lax.ppermute(blocks[e], 'ctx', [(i, i ^ e) for i in range(ring)])  8.42 us
    pallas_call x1, Pallas kernels, body(): pl.pallas_call(functools.partial(local_kernel, factor, rows), in_specs=[V...  4.93 us
    pallas_call x1, Pallas kernels, body(): pl.pallas_call(functools.partial(query_kernel, factor, rows, parts), in_s...  4.51 us
    ppermute x2, waiting for transfers between devices, swapped(): return lax.ppermute(array, 'sub', [(i, i ^ 1) for i in range(subs)])  2.92 us
    pallas_call x1, Pallas kernels, body(): pl.pallas_call(functools.partial(listed_kernel, factor, rows, part * each...  2.45 us
    pallas_call x1, Pallas kernels, body(): pl.pallas_call(pack_kernel, in_specs=[HBM_SPEC] * 2, out_specs=[VMEM_SPEC...  1.24 us
    pallas_call x1, Pallas kernels, body(): pl.pallas_call(functools.partial(spread_kernel, grouped, ring, subs), in_...  1.18 us
  transfers between devices with their start and end apart: 8, of which 6 were waited for; matrix products, arithmetic and copies ran while one was open for 0% of the time, Pallas kernels for 28%

profile of v6, /device:TPU:0, one launch (start us, length us, event | category | flops | bytes accessed | tf_op | source)
XLA Modules:
  0.0 38.5 jit_solution(10827289095490605309)
XLA Ops:
  0.6 1.2 %pack.1.refs_0_.refs_3_ = bf16[2,2,128,128]{3,2,1,0:T(8,128)(2,1)S(1)} custom-call(bf16[128,2,128]{2,1,0:T(2,128)(2,1)} %key_ref.1, bf16[128,2,128]{2,1,0:T(2,128)(2,1)} %value_ref.1), custom_call_target="tpu_custom_call" | custom-call | tf_op jit(solution)/shard_map/pack/pallas_call | solution.py:299
  1.9 4.1 %collective-permute-start = (bf16[2,2,128,128]{3,2,1,0:T(8,128)(2,1)S(1)}, bf16[2,2,128,128]{3,2,1,0:T(8,128)(2,1)S(1)}, u32[]{:S(2)}, u32[]{:S(2)}) collective-permute-start(bf16[2,2,128,128]{3,2,1,0:T(8,128)(2,1)S(1)} %pack.1.refs_0_.refs_3_), channel_id=1, source_target_pairs={{0,8},{4,12},{8,0},{12,4},{1,9},{5,13},{9,1},{13,5},{2,10},{6,14},... | collective-permute-start | bytes 393224 | tf_op jit(solution)/shard_map/ppermute | solution.py:290
  6.0 1.3 %collective-permute-start.1 = (bf16[2,2,128,128]{3,2,1,0:T(8,128)(2,1)S(1)}, bf16[2,2,128,128]{3,2,1,0:T(8,128)(2,1)S(1)}, u32[]{:S(2)}, u32[]{:S(2)}) collective-permute-start(bf16[2,2,128,128]{3,2,1,0:T(8,128)(2,1)S(1)} %pack.1.refs_0_.refs_3_), channel_id=1, source_target_pairs={{0,12},{4,8},{8,4},{12,0},{1,13},{5,9},{9,5},{13,1},{2,14},{6,10},... | collective-permute-start | bytes 393224 | tf_op jit(solution)/shard_map/ppermute | solution.py:290
  7.3 0.2 collective-permute-start.2
  7.6 1.2 %spread.1 = (f32[2,1,2048]{2,1,0:T(1,128)S(1)}, f32[2,1,2048]{2,1,0:T(1,128)S(1)}, f32[1,2048]{1,0:T(1,128)S(1)}, f32[128,128]{1,0:T(8,128)S(1)}, s32[8,128]{1,0:T(8,128)S(1)}) custom-call(f32[32,128]{1,0:T(8,128)} %bitcast.4, f32[32,128]{1,0:T(8,128)} %bitcast.5, s32[1,128]{1,0:T(1,128)} %bitcast.7, s32[2,8]{1,0:T(2,128)} %bitcast.6), custom_call_target="tpu_custom_call" | custom-call | tf_op jit(solution)/shard_map/spread/pallas_call | solution.py:310
  8.7 4.9 %local_block.1 = (f32[2,2,128,128]{3,2,1,0:T(8,128)S(1)}, f32[128,32,128]{2,1,0:T(8,128)S(1)}, bf16[2,2,128,16,128]{4,3,2,1,0:T(8,128)(2,1)S(1)}) custom-call(bf16[2,2,128,128]{3,2,1,0:T(8,128)(2,1)S(1)} %pack.1.refs_0_.refs_3_, bf16[128,32,128]{2,1,0:T(8,128)(2,1)} %refs_1_.1, bf16[128,32,128]{2,1,0:T(8,128)(2,1)} %refs_2_.1, ...), custom_call_target="tpu_custom_call" | custom-call | flops 671088640 | bytes 4194304 | tf_op jit(solution)/shard_map/local_block/pallas_call | solution.py:335
  13.7 2.3 %collective-permute-done.refs_0_ = bf16[2,2,128,128]{3,2,1,0:T(8,128)(2,1)S(1)} collective-permute-done((bf16[2,2,128,128]{3,2,1,0:T(8,128)(2,1)S(1)}, bf16[2,2,128,128]{3,2,1,0:T(8,128)(2,1)S(1)}, u32[]{:S(2)}, u32[]{:S(2)}) %collective-permute-start) | collective-permute-done | bytes 131104 | tf_op jit(solution)/shard_map/ppermute | solution.py:290
  16.0 0.0 collective-permute-done.1.refs_1_
  16.0 0.5 %collective-permute-done.2.refs_2_ = bf16[2,2,128,128]{3,2,1,0:T(8,128)(2,1)S(1)} collective-permute-done((bf16[2,2,128,128]{3,2,1,0:T(8,128)(2,1)S(1)}, bf16[2,2,128,128]{3,2,1,0:T(8,128)(2,1)S(1)}, u32[]{:S(2)}, u32[]{:S(2)}) %collective-permute-start.2) | collective-permute-done | bytes 131104 | tf_op jit(solution)/shard_map/ppermute | solution.py:290
  16.5 0.1 choose.1
  16.6 0.1 collective-permute-start.3
  16.7 1.5 %collective-permute-done.3.refs_4_ = bf16[2,2,2,128,128]{4,3,2,1,0:T(8,128)(2,1)S(1)} collective-permute-done((bf16[2,2,2,128,128]{4,3,2,1,0:T(8,128)(2,1)S(1)}, bf16[2,2,2,128,128]{4,3,2,1,0:T(8,128)(2,1)S(1)}, u32[]{:S(2)}, u32[]{:S(2)}) %collective-permute-start.3) | collective-permute-done | bytes 262176 | tf_op jit(solution)/shard_map/ppermute | solution.py:293
  18.2 2.4 %listed_keys.1.mine_ref = bf16[2,2,2,128,128]{4,3,2,1,0:T(8,128)(2,1)S(1)} custom-call(s32[8,128]{1,0:T(8,128)S(1)} %get-tuple-element.17.places_ref, bf16[2,2,128,128]{3,2,1,0:T(8,128)(2,1)S(1)} %collective-permute-done.refs_0_, bf16[2,2,128,128]{3,2,1,0:T(8,128)(2,1)S(1)} %collective-permute-done.1.refs_1_, ...), custom_call_target="tpu_custom_call" | custom-call | flops 1073741824 | bytes 2097152 | tf_op jit(solution)/shard_map/listed_keys/pallas_call | solution.py:363
  20.7 0.2 collective-permute-start.4
  20.9 1.4 %collective-permute-done.4.other_ref = bf16[2,2,2,128,128]{4,3,2,1,0:T(8,128)(2,1)S(1)} collective-permute-done((bf16[2,2,2,128,128]{4,3,2,1,0:T(8,128)(2,1)S(1)}, bf16[2,2,2,128,128]{4,3,2,1,0:T(8,128)(2,1)S(1)}, u32[]{:S(2)}, u32[]{:S(2)}) %collective-permute-start.4) | collective-permute-done | bytes 262176 | tf_op jit(solution)/shard_map/ppermute | solution.py:293
  22.3 0.4 %combine.1 = (f32[2,2,128,128]{3,2,1,0:T(8,128)S(1)}, bf16[2,2,128,128]{3,2,1,0:T(8,128)(2,1)S(1)}, bf16[2,2,128,128]{3,2,1,0:T(8,128)(2,1)S(1)}, bf16[2,2,128,128]{3,2,1,0:T(8,128)(2,1)S(1)}) custom-call(s32[8,128]{1,0:T(8,128)S(1)} %get-tuple-element.17.places_ref, bf16[2,2,2,128,128]{4,3,2,1,0:T(8,128)(2,1)S(1)} %listed_keys.1.mine_ref, ...), custom_call_target="tpu_custom_call" | custom-call | tf_op jit(solution)/shard_map/combine/pallas_call | solution.py:373
  22.7 4.2 %collective-permute-start.5 = (bf16[2,2,128,128]{3,2,1,0:T(8,128)(2,1)S(1)}, bf16[2,2,128,128]{3,2,1,0:T(8,128)(2,1)S(1)}, u32[]{:S(2)}, u32[]{:S(2)}) collective-permute-start(bf16[2,2,128,128]{3,2,1,0:T(8,128)(2,1)S(1)} %get-tuple-element.26), channel_id=1, source_target_pairs={{0,8},{4,12},{8,0},{12,4},{1,9},{5,13},{9,1},{13,5},{2,10},{6,14},... | collective-permute-start | bytes 393224 | tf_op jit(solution)/shard_map/ppermute | solution.py:290
  26.9 0.4 %collective-permute-start.6 = (bf16[2,2,128,128]{3,2,1,0:T(8,128)(2,1)S(1)}, bf16[2,2,128,128]{3,2,1,0:T(8,128)(2,1)S(1)}, u32[]{:S(2)}, u32[]{:S(2)}) collective-permute-start(bf16[2,2,128,128]{3,2,1,0:T(8,128)(2,1)S(1)} %get-tuple-element.27), channel_id=1, source_target_pairs={{0,12},{4,8},{8,4},{12,0},{1,13},{5,9},{9,5},{13,1},{2,14},{6,10},... | collective-permute-start | bytes 393224 | tf_op jit(solution)/shard_map/ppermute | solution.py:290
  27.3 0.2 collective-permute-start.7
  27.5 4.5 %listed_queries.1 = f32[128,32,128]{2,1,0:T(8,128)} custom-call(s32[8,128]{1,0:T(8,128)S(1)} %get-tuple-element.17.places_ref, bf16[2,2,128,128]{3,2,1,0:T(8,128)(2,1)S(1)} %collective-permute-done.refs_0_, bf16[2,2,128,128]{3,2,1,0:T(8,128)(2,1)S(1)} %collective-permute-done.1.refs_1_, bf16[2,2,128,128]{3,2,1,0:T(8,128)(2,1)S(1)} %collective-permute-done.2.refs_2_, ...), custom_call_target="tpu_custom_call" | custom-call | flops 805306368 | bytes 6291456 | tf_op jit(solution)/shard_map/listed_queries/pallas_call | solution.py:385
  32.0 4.6 %collective-permute-done.5.refs_1_ = bf16[2,2,128,128]{3,2,1,0:T(8,128)(2,1)S(1)} collective-permute-done((bf16[2,2,128,128]{3,2,1,0:T(8,128)(2,1)S(1)}, bf16[2,2,128,128]{3,2,1,0:T(8,128)(2,1)S(1)}, u32[]{:S(2)}, u32[]{:S(2)}) %collective-permute-start.5) | collective-permute-done | bytes 131104 | tf_op jit(solution)/shard_map/ppermute | solution.py:290
  36.6 0.0 collective-permute-done.6.refs_2_
  36.6 1.1 %collective-permute-done.7.refs_3_ = bf16[2,2,128,128]{3,2,1,0:T(8,128)(2,1)S(1)} collective-permute-done((bf16[2,2,128,128]{3,2,1,0:T(8,128)(2,1)S(1)}, bf16[2,2,128,128]{3,2,1,0:T(8,128)(2,1)S(1)}, u32[]{:S(2)}, u32[]{:S(2)}) %collective-permute-start.7) | collective-permute-done | bytes 131104 | tf_op jit(solution)/shard_map/ppermute | solution.py:290
  37.6 0.8 %total.1 = (f32[128,2,128]{2,1,0:T(2,128)}, f32[128,2,128]{2,1,0:T(2,128)}) custom-call(f32[2,2,128,128]{3,2,1,0:T(8,128)S(1)} %get-tuple-element.22.refs_4_.refs_5_.near_ref, f32[2,2,128,128]{3,2,1,0:T(8,128)S(1)} %get-tuple-element.25.refs_9_.refs_0_, bf16[2,2,128,128]{3,2,1,0:T(8,128)(2,1)S(1)} %collective-permute-done.5.refs_1_, ...), custom_call_target="tpu_custom_call" | custom-call | tf_op jit(solution)/shard_map/total/pallas_call | solution.py:395
Async XLA Ops:
  1.9 14.1 %collective-permute-start = (bf16[2,2,128,128]{3,2,1,0:T(8,128)(2,1)S(1)}, bf16[2,2,128,128]{3,2,1,0:T(8,128)(2,1)S(1)}, u32[]{:S(2)}, u32[]{:S(2)}) collective-permute-start(bf16[2,2,128,128]{3,2,1,0:T(8,128)(2,1)S(1)} %pack.1.refs_0_.refs_3_), channel_id=1, source_target_pairs={{0,8},{4,12},{8,0},{12,4},{1,9},{5,13},{9,1},{13,5},{2,10},{6,14},... | collective-permute-start | bytes 393224 | tf_op jit(solution)/shard_map/ppermute | solution.py:290
  6.0 10.0 %collective-permute-start.1 = (bf16[2,2,128,128]{3,2,1,0:T(8,128)(2,1)S(1)}, bf16[2,2,128,128]{3,2,1,0:T(8,128)(2,1)S(1)}, u32[]{:S(2)}, u32[]{:S(2)}) collective-permute-start(bf16[2,2,128,128]{3,2,1,0:T(8,128)(2,1)S(1)} %pack.1.refs_0_.refs_3_), channel_id=1, source_target_pairs={{0,12},{4,8},{8,4},{12,0},{1,13},{5,9},{9,5},{13,1},{2,14},{6,10},... | collective-permute-start | bytes 393224 | tf_op jit(solution)/shard_map/ppermute | solution.py:290
  7.3 9.2 %collective-permute-start.2 = (bf16[2,2,128,128]{3,2,1,0:T(8,128)(2,1)S(1)}, bf16[2,2,128,128]{3,2,1,0:T(8,128)(2,1)S(1)}, u32[]{:S(2)}, u32[]{:S(2)}) collective-permute-start(bf16[2,2,128,128]{3,2,1,0:T(8,128)(2,1)S(1)} %pack.1.refs_0_.refs_3_), channel_id=1, source_target_pairs={{0,4},{4,0},{8,12},{12,8},{1,5},{5,1},{9,13},{13,9},{2,6},{6,2},{1... | collective-permute-start | bytes 393224 | tf_op jit(solution)/shard_map/ppermute | solution.py:290
  16.6 1.6 %collective-permute-start.3 = (bf16[2,2,2,128,128]{4,3,2,1,0:T(8,128)(2,1)S(1)}, bf16[2,2,2,128,128]{4,3,2,1,0:T(8,128)(2,1)S(1)}, u32[]{:S(2)}, u32[]{:S(2)}) collective-permute-start(bf16[2,2,2,128,128]{4,3,2,1,0:T(8,128)(2,1)S(1)} %choose.1), channel_id=1, source_target_pairs={{0,1},{1,0},{2,3},{3,2},{4,5},{5,4},{6,7},{7,6},{8,9},{9,8},{10,11... | collective-permute-start | bytes 786440 | tf_op jit(solution)/shard_map/ppermute | solution.py:293
  20.7 1.6 %collective-permute-start.4 = (bf16[2,2,2,128,128]{4,3,2,1,0:T(8,128)(2,1)S(1)}, bf16[2,2,2,128,128]{4,3,2,1,0:T(8,128)(2,1)S(1)}, u32[]{:S(2)}, u32[]{:S(2)}) collective-permute-start(bf16[2,2,2,128,128]{4,3,2,1,0:T(8,128)(2,1)S(1)} %listed_keys.1.mine_ref), channel_id=1, source_target_pairs={{0,1},{1,0},{2,3},{3,2},{4,5},{5,4},{6,7},{7,6},{8,9},{9,8},{10,11... | collective-permute-start | bytes 786440 | tf_op jit(solution)/shard_map/ppermute | solution.py:293
  22.7 13.9 %collective-permute-start.5 = (bf16[2,2,128,128]{3,2,1,0:T(8,128)(2,1)S(1)}, bf16[2,2,128,128]{3,2,1,0:T(8,128)(2,1)S(1)}, u32[]{:S(2)}, u32[]{:S(2)}) collective-permute-start(bf16[2,2,128,128]{3,2,1,0:T(8,128)(2,1)S(1)} %get-tuple-element.26), channel_id=1, source_target_pairs={{0,8},{4,12},{8,0},{12,4},{1,9},{5,13},{9,1},{13,5},{2,10},{6,14},... | collective-permute-start | bytes 393224 | tf_op jit(solution)/shard_map/ppermute | solution.py:290
  26.9 9.7 %collective-permute-start.6 = (bf16[2,2,128,128]{3,2,1,0:T(8,128)(2,1)S(1)}, bf16[2,2,128,128]{3,2,1,0:T(8,128)(2,1)S(1)}, u32[]{:S(2)}, u32[]{:S(2)}) collective-permute-start(bf16[2,2,128,128]{3,2,1,0:T(8,128)(2,1)S(1)} %get-tuple-element.27), channel_id=1, source_target_pairs={{0,12},{4,8},{8,4},{12,0},{1,13},{5,9},{9,5},{13,1},{2,14},{6,10},... | collective-permute-start | bytes 393224 | tf_op jit(solution)/shard_map/ppermute | solution.py:290
  27.3 10.3 %collective-permute-start.7 = (bf16[2,2,128,128]{3,2,1,0:T(8,128)(2,1)S(1)}, bf16[2,2,128,128]{3,2,1,0:T(8,128)(2,1)S(1)}, u32[]{:S(2)}, u32[]{:S(2)}) collective-permute-start(bf16[2,2,128,128]{3,2,1,0:T(8,128)(2,1)S(1)} %get-tuple-element.28), channel_id=1, source_target_pairs={{0,4},{4,0},{8,12},{12,8},{1,5},{5,1},{9,13},{13,9},{2,6},{6,2},{1... | collective-permute-start | bytes 393224 | tf_op jit(solution)/shard_map/ppermute | solution.py:290

commit v7 on v6

--- a/solution.py
+++ b/solution.py
@@ -286,8 +286,8 @@
     each = kv_heads // parts
     span_shape = (2, each, tokens, head_dim)
 
-    def crossed(blocks):
-        return [lax.ppermute(blocks[e], "ctx", [(i, i ^ e) for i in range(ring)]) for e in send_order(ring)[:-1]]
+    def crossed(blocks, order):
+        return [lax.ppermute(blocks[e], "ctx", [(i, i ^ e) for i in range(ring)]) for e in order if e]
 
     def swapped(array):
         return lax.ppermute(array, "sub", [(i, i ^ 1) for i in range(subs)])
@@ -305,7 +305,7 @@
         compiler_params=params,
         name="pack",
     )(*in_hbm(keys, values))
-    columns = [[*crossed([block] * ring), block] for block in kv]
+    columns = [[*crossed([block] * ring, send_order(ring)), block] for block in kv]
 
     norm, term, docs, doc_col, places = pl.pallas_call(
         functools.partial(spread_kernel, grouped, ring, subs),
@@ -379,7 +379,7 @@
             compiler_params=params,
             name="combine",
         )(places, far_kv, other_kv)
-        sums += [blocks[0], *crossed(blocks)]
+        sums += [blocks[0], *crossed(blocks, range(ring - 1, 0, -1))]
         after = blocks[0]
 
     grad_queries = pl.pallas_call(

time: 38.7 us -> 39.6 us (1.023)
  waiting for transfers between devices: 11.3 us -> 12.3 us
    ppermute x6, waiting for transfers between devices: 8.42 us -> 9.37 us  [crossed(): lax.ppermute(blocks[e], 'ctx', [(i, i ^ e) for i in range(ring)])]
  transfers between devices with their start and end apart: 8 -> 8, of which waited for: 6 -> 5; matrix products, arithmetic and copies ran while one was open for 0% -> 0% of each run, Pallas kernels for 28% -> 27%
where the time goes in v7:
time: 39.6 us; the launch traced here: 39.4 us
  Pallas kernels  15.7 us (40%)
  waiting for transfers between devices  12.3 us (31%)
  starting transfers between devices  10.7 us (27%)
  between operations  0.68 us (2%)
    ppermute x6, starting transfers between devices, crossed(): lax.ppermute(blocks[e], 'ctx', [(i, i ^ e) for i in range(ring)])  10.4 us
    ppermute x6, waiting for transfers between devices, crossed(): lax.ppermute(blocks[e], 'ctx', [(i, i ^ e) for i in range(ring)])  9.37 us
    pallas_call x1, Pallas kernels, body(): pl.pallas_call(functools.partial(local_kernel, factor, rows), in_specs=[V...  4.93 us
    pallas_call x1, Pallas kernels, body(): pl.pallas_call(functools.partial(query_kernel, factor, rows, parts), in_s...  4.51 us
    ppermute x2, waiting for transfers between devices, swapped(): return lax.ppermute(array, 'sub', [(i, i ^ 1) for i in range(subs)])  2.92 us
    pallas_call x1, Pallas kernels, body(): pl.pallas_call(functools.partial(listed_kernel, factor, rows, part * each...  2.45 us
    pallas_call x1, Pallas kernels, body(): pl.pallas_call(pack_kernel, in_specs=[HBM_SPEC] * 2, out_specs=[VMEM_SPEC...  1.24 us
    pallas_call x1, Pallas kernels, body(): pl.pallas_call(functools.partial(spread_kernel, grouped, ring, subs), in_...  1.18 us
  transfers between devices with their start and end apart: 8, of which 5 were waited for; matrix products, arithmetic and copies ran while one was open for 0% of the time, Pallas kernels for 27%

profile of v7, /device:TPU:0, one launch (start us, length us, event | category | flops | bytes accessed | tf_op | source)
XLA Modules:
  0.0 39.4 jit_solution(12533514148181774829)
XLA Ops:
  0.6 1.2 %pack.1.refs_0_.refs_3_ = bf16[2,2,128,128]{3,2,1,0:T(8,128)(2,1)S(1)} custom-call(bf16[128,2,128]{2,1,0:T(2,128)(2,1)} %key_ref.1, bf16[128,2,128]{2,1,0:T(2,128)(2,1)} %value_ref.1), custom_call_target="tpu_custom_call" | custom-call | tf_op jit(solution)/shard_map/pack/pallas_call | solution.py:299
  1.9 4.1 %collective-permute-start = (bf16[2,2,128,128]{3,2,1,0:T(8,128)(2,1)S(1)}, bf16[2,2,128,128]{3,2,1,0:T(8,128)(2,1)S(1)}, u32[]{:S(2)}, u32[]{:S(2)}) collective-permute-start(bf16[2,2,128,128]{3,2,1,0:T(8,128)(2,1)S(1)} %pack.1.refs_0_.refs_3_), channel_id=1, source_target_pairs={{0,8},{4,12},{8,0},{12,4},{1,9},{5,13},{9,1},{13,5},{2,10},{6,14},... | collective-permute-start | bytes 393224 | tf_op jit(solution)/shard_map/ppermute | solution.py:290
  6.0 1.3 %collective-permute-start.1 = (bf16[2,2,128,128]{3,2,1,0:T(8,128)(2,1)S(1)}, bf16[2,2,128,128]{3,2,1,0:T(8,128)(2,1)S(1)}, u32[]{:S(2)}, u32[]{:S(2)}) collective-permute-start(bf16[2,2,128,128]{3,2,1,0:T(8,128)(2,1)S(1)} %pack.1.refs_0_.refs_3_), channel_id=1, source_target_pairs={{0,12},{4,8},{8,4},{12,0},{1,13},{5,9},{9,5},{13,1},{2,14},{6,10},... | collective-permute-start | bytes 393224 | tf_op jit(solution)/shard_map/ppermute | solution.py:290
  7.3 0.2 collective-permute-start.2
  7.6 1.2 %spread.1 = (f32[2,1,2048]{2,1,0:T(1,128)S(1)}, f32[2,1,2048]{2,1,0:T(1,128)S(1)}, f32[1,2048]{1,0:T(1,128)S(1)}, f32[128,128]{1,0:T(8,128)S(1)}, s32[8,128]{1,0:T(8,128)S(1)}) custom-call(f32[32,128]{1,0:T(8,128)} %bitcast.4, f32[32,128]{1,0:T(8,128)} %bitcast.5, s32[1,128]{1,0:T(1,128)} %bitcast.7, s32[2,8]{1,0:T(2,128)} %bitcast.6), custom_call_target="tpu_custom_call" | custom-call | tf_op jit(solution)/shard_map/spread/pallas_call | solution.py:310
  8.7 4.9 %local_block.1 = (f32[2,2,128,128]{3,2,1,0:T(8,128)S(1)}, f32[128,32,128]{2,1,0:T(8,128)S(1)}, bf16[2,2,128,16,128]{4,3,2,1,0:T(8,128)(2,1)S(1)}) custom-call(bf16[2,2,128,128]{3,2,1,0:T(8,128)(2,1)S(1)} %pack.1.refs_0_.refs_3_, bf16[128,32,128]{2,1,0:T(8,128)(2,1)} %refs_1_.1, bf16[128,32,128]{2,1,0:T(8,128)(2,1)} %refs_2_.1, ...), custom_call_target="tpu_custom_call" | custom-call | flops 671088640 | bytes 4194304 | tf_op jit(solution)/shard_map/local_block/pallas_call | solution.py:335
  13.7 2.3 %collective-permute-done.refs_0_ = bf16[2,2,128,128]{3,2,1,0:T(8,128)(2,1)S(1)} collective-permute-done((bf16[2,2,128,128]{3,2,1,0:T(8,128)(2,1)S(1)}, bf16[2,2,128,128]{3,2,1,0:T(8,128)(2,1)S(1)}, u32[]{:S(2)}, u32[]{:S(2)}) %collective-permute-start) | collective-permute-done | bytes 131104 | tf_op jit(solution)/shard_map/ppermute | solution.py:290
  16.0 0.0 collective-permute-done.1.refs_1_
  16.0 0.5 %collective-permute-done.2.refs_2_ = bf16[2,2,128,128]{3,2,1,0:T(8,128)(2,1)S(1)} collective-permute-done((bf16[2,2,128,128]{3,2,1,0:T(8,128)(2,1)S(1)}, bf16[2,2,128,128]{3,2,1,0:T(8,128)(2,1)S(1)}, u32[]{:S(2)}, u32[]{:S(2)}) %collective-permute-start.2) | collective-permute-done | bytes 131104 | tf_op jit(solution)/shard_map/ppermute | solution.py:290
  16.5 0.1 choose.1
  16.6 0.1 collective-permute-start.3
  16.7 1.5 %collective-permute-done.3.refs_4_ = bf16[2,2,2,128,128]{4,3,2,1,0:T(8,128)(2,1)S(1)} collective-permute-done((bf16[2,2,2,128,128]{4,3,2,1,0:T(8,128)(2,1)S(1)}, bf16[2,2,2,128,128]{4,3,2,1,0:T(8,128)(2,1)S(1)}, u32[]{:S(2)}, u32[]{:S(2)}) %collective-permute-start.3) | collective-permute-done | bytes 262176 | tf_op jit(solution)/shard_map/ppermute | solution.py:293
  18.2 2.4 %listed_keys.1.mine_ref = bf16[2,2,2,128,128]{4,3,2,1,0:T(8,128)(2,1)S(1)} custom-call(s32[8,128]{1,0:T(8,128)S(1)} %get-tuple-element.17.places_ref, bf16[2,2,128,128]{3,2,1,0:T(8,128)(2,1)S(1)} %collective-permute-done.refs_0_, bf16[2,2,128,128]{3,2,1,0:T(8,128)(2,1)S(1)} %collective-permute-done.1.refs_1_, ...), custom_call_target="tpu_custom_call" | custom-call | flops 1073741824 | bytes 2097152 | tf_op jit(solution)/shard_map/listed_keys/pallas_call | solution.py:363
  20.7 0.2 collective-permute-start.4
  20.9 1.4 %collective-permute-done.4.other_ref = bf16[2,2,2,128,128]{4,3,2,1,0:T(8,128)(2,1)S(1)} collective-permute-done((bf16[2,2,2,128,128]{4,3,2,1,0:T(8,128)(2,1)S(1)}, bf16[2,2,2,128,128]{4,3,2,1,0:T(8,128)(2,1)S(1)}, u32[]{:S(2)}, u32[]{:S(2)}) %collective-permute-start.4) | collective-permute-done | bytes 262176 | tf_op jit(solution)/shard_map/ppermute | solution.py:293
  22.3 0.4 %combine.1 = (f32[2,2,128,128]{3,2,1,0:T(8,128)S(1)}, bf16[2,2,128,128]{3,2,1,0:T(8,128)(2,1)S(1)}, bf16[2,2,128,128]{3,2,1,0:T(8,128)(2,1)S(1)}, bf16[2,2,128,128]{3,2,1,0:T(8,128)(2,1)S(1)}) custom-call(s32[8,128]{1,0:T(8,128)S(1)} %get-tuple-element.17.places_ref, bf16[2,2,2,128,128]{4,3,2,1,0:T(8,128)(2,1)S(1)} %listed_keys.1.mine_ref, ...), custom_call_target="tpu_custom_call" | custom-call | tf_op jit(solution)/shard_map/combine/pallas_call | solution.py:373
  22.7 3.6 %collective-permute-start.5 = (bf16[2,2,128,128]{3,2,1,0:T(8,128)(2,1)S(1)}, bf16[2,2,128,128]{3,2,1,0:T(8,128)(2,1)S(1)}, u32[]{:S(2)}, u32[]{:S(2)}) collective-permute-start(bf16[2,2,128,128]{3,2,1,0:T(8,128)(2,1)S(1)} %get-tuple-element.26), channel_id=1, source_target_pairs={{0,12},{4,8},{8,4},{12,0},{1,13},{5,9},{9,5},{13,1},{2,14},{6,10},... | collective-permute-start | bytes 393224 | tf_op jit(solution)/shard_map/ppermute | solution.py:290
  26.3 0.7 %collective-permute-start.6 = (bf16[2,2,128,128]{3,2,1,0:T(8,128)(2,1)S(1)}, bf16[2,2,128,128]{3,2,1,0:T(8,128)(2,1)S(1)}, u32[]{:S(2)}, u32[]{:S(2)}) collective-permute-start(bf16[2,2,128,128]{3,2,1,0:T(8,128)(2,1)S(1)} %get-tuple-element.27), channel_id=1, source_target_pairs={{0,8},{4,12},{8,0},{12,4},{1,9},{5,13},{9,1},{13,5},{2,10},{6,14},... | collective-permute-start | bytes 393224 | tf_op jit(solution)/shard_map/ppermute | solution.py:290
  26.9 0.5 %collective-permute-start.7 = (bf16[2,2,128,128]{3,2,1,0:T(8,128)(2,1)S(1)}, bf16[2,2,128,128]{3,2,1,0:T(8,128)(2,1)S(1)}, u32[]{:S(2)}, u32[]{:S(2)}) collective-permute-start(bf16[2,2,128,128]{3,2,1,0:T(8,128)(2,1)S(1)} %get-tuple-element.28), channel_id=1, source_target_pairs={{0,4},{4,0},{8,12},{12,8},{1,5},{5,1},{9,13},{13,9},{2,6},{6,2},{1... | collective-permute-start | bytes 393224 | tf_op jit(solution)/shard_map/ppermute | solution.py:290
  27.4 4.5 %listed_queries.1 = f32[128,32,128]{2,1,0:T(8,128)} custom-call(s32[8,128]{1,0:T(8,128)S(1)} %get-tuple-element.17.places_ref, bf16[2,2,128,128]{3,2,1,0:T(8,128)(2,1)S(1)} %collective-permute-done.refs_0_, bf16[2,2,128,128]{3,2,1,0:T(8,128)(2,1)S(1)} %collective-permute-done.1.refs_1_, bf16[2,2,128,128]{3,2,1,0:T(8,128)(2,1)S(1)} %collective-permute-done.2.refs_2_, ...), custom_call_target="tpu_custom_call" | custom-call | flops 805306368 | bytes 6291456 | tf_op jit(solution)/shard_map/listed_queries/pallas_call | solution.py:385
  31.9 0.0 collective-permute-done.5.refs_1_
  31.9 6.6 %collective-permute-done.6.refs_2_ = bf16[2,2,128,128]{3,2,1,0:T(8,128)(2,1)S(1)} collective-permute-done((bf16[2,2,128,128]{3,2,1,0:T(8,128)(2,1)S(1)}, bf16[2,2,128,128]{3,2,1,0:T(8,128)(2,1)S(1)}, u32[]{:S(2)}, u32[]{:S(2)}) %collective-permute-start.6) | collective-permute-done | bytes 131104 | tf_op jit(solution)/shard_map/ppermute | solution.py:290
  38.5 0.0 collective-permute-done.7.refs_3_
  38.5 0.8 %total.1 = (f32[128,2,128]{2,1,0:T(2,128)}, f32[128,2,128]{2,1,0:T(2,128)}) custom-call(f32[2,2,128,128]{3,2,1,0:T(8,128)S(1)} %get-tuple-element.22.refs_4_.refs_5_.near_ref, f32[2,2,128,128]{3,2,1,0:T(8,128)S(1)} %get-tuple-element.25.refs_9_.refs_0_, bf16[2,2,128,128]{3,2,1,0:T(8,128)(2,1)S(1)} %collective-permute-done.5.refs_1_, ...), custom_call_target="tpu_custom_call" | custom-call | tf_op jit(solution)/shard_map/total/pallas_call | solution.py:395
Async XLA Ops:
  1.9 14.1 %collective-permute-start = (bf16[2,2,128,128]{3,2,1,0:T(8,128)(2,1)S(1)}, bf16[2,2,128,128]{3,2,1,0:T(8,128)(2,1)S(1)}, u32[]{:S(2)}, u32[]{:S(2)}) collective-permute-start(bf16[2,2,128,128]{3,2,1,0:T(8,128)(2,1)S(1)} %pack.1.refs_0_.refs_3_), channel_id=1, source_target_pairs={{0,8},{4,12},{8,0},{12,4},{1,9},{5,13},{9,1},{13,5},{2,10},{6,14},... | collective-permute-start | bytes 393224 | tf_op jit(solution)/shard_map/ppermute | solution.py:290
  6.0 10.0 %collective-permute-start.1 = (bf16[2,2,128,128]{3,2,1,0:T(8,128)(2,1)S(1)}, bf16[2,2,128,128]{3,2,1,0:T(8,128)(2,1)S(1)}, u32[]{:S(2)}, u32[]{:S(2)}) collective-permute-start(bf16[2,2,128,128]{3,2,1,0:T(8,128)(2,1)S(1)} %pack.1.refs_0_.refs_3_), channel_id=1, source_target_pairs={{0,12},{4,8},{8,4},{12,0},{1,13},{5,9},{9,5},{13,1},{2,14},{6,10},... | collective-permute-start | bytes 393224 | tf_op jit(solution)/shard_map/ppermute | solution.py:290
  7.3 9.2 %collective-permute-start.2 = (bf16[2,2,128,128]{3,2,1,0:T(8,128)(2,1)S(1)}, bf16[2,2,128,128]{3,2,1,0:T(8,128)(2,1)S(1)}, u32[]{:S(2)}, u32[]{:S(2)}) collective-permute-start(bf16[2,2,128,128]{3,2,1,0:T(8,128)(2,1)S(1)} %pack.1.refs_0_.refs_3_), channel_id=1, source_target_pairs={{0,4},{4,0},{8,12},{12,8},{1,5},{5,1},{9,13},{13,9},{2,6},{6,2},{1... | collective-permute-start | bytes 393224 | tf_op jit(solution)/shard_map/ppermute | solution.py:290
  16.6 1.6 %collective-permute-start.3 = (bf16[2,2,2,128,128]{4,3,2,1,0:T(8,128)(2,1)S(1)}, bf16[2,2,2,128,128]{4,3,2,1,0:T(8,128)(2,1)S(1)}, u32[]{:S(2)}, u32[]{:S(2)}) collective-permute-start(bf16[2,2,2,128,128]{4,3,2,1,0:T(8,128)(2,1)S(1)} %choose.1), channel_id=1, source_target_pairs={{0,1},{1,0},{2,3},{3,2},{4,5},{5,4},{6,7},{7,6},{8,9},{9,8},{10,11... | collective-permute-start | bytes 786440 | tf_op jit(solution)/shard_map/ppermute | solution.py:293
  20.7 1.6 %collective-permute-start.4 = (bf16[2,2,2,128,128]{4,3,2,1,0:T(8,128)(2,1)S(1)}, bf16[2,2,2,128,128]{4,3,2,1,0:T(8,128)(2,1)S(1)}, u32[]{:S(2)}, u32[]{:S(2)}) collective-permute-start(bf16[2,2,2,128,128]{4,3,2,1,0:T(8,128)(2,1)S(1)} %listed_keys.1.mine_ref), channel_id=1, source_target_pairs={{0,1},{1,0},{2,3},{3,2},{4,5},{5,4},{6,7},{7,6},{8,9},{9,8},{10,11... | collective-permute-start | bytes 786440 | tf_op jit(solution)/shard_map/ppermute | solution.py:293
  22.7 9.3 %collective-permute-start.5 = (bf16[2,2,128,128]{3,2,1,0:T(8,128)(2,1)S(1)}, bf16[2,2,128,128]{3,2,1,0:T(8,128)(2,1)S(1)}, u32[]{:S(2)}, u32[]{:S(2)}) collective-permute-start(bf16[2,2,128,128]{3,2,1,0:T(8,128)(2,1)S(1)} %get-tuple-element.26), channel_id=1, source_target_pairs={{0,12},{4,8},{8,4},{12,0},{1,13},{5,9},{9,5},{13,1},{2,14},{6,10},... | collective-permute-start | bytes 393224 | tf_op jit(solution)/shard_map/ppermute | solution.py:290
  26.3 12.2 %collective-permute-start.6 = (bf16[2,2,128,128]{3,2,1,0:T(8,128)(2,1)S(1)}, bf16[2,2,128,128]{3,2,1,0:T(8,128)(2,1)S(1)}, u32[]{:S(2)}, u32[]{:S(2)}) collective-permute-start(bf16[2,2,128,128]{3,2,1,0:T(8,128)(2,1)S(1)} %get-tuple-element.27), channel_id=1, source_target_pairs={{0,8},{4,12},{8,0},{12,4},{1,9},{5,13},{9,1},{13,5},{2,10},{6,14},... | collective-permute-start | bytes 393224 | tf_op jit(solution)/shard_map/ppermute | solution.py:290
  26.9 11.6 %collective-permute-start.7 = (bf16[2,2,128,128]{3,2,1,0:T(8,128)(2,1)S(1)}, bf16[2,2,128,128]{3,2,1,0:T(8,128)(2,1)S(1)}, u32[]{:S(2)}, u32[]{:S(2)}) collective-permute-start(bf16[2,2,128,128]{3,2,1,0:T(8,128)(2,1)S(1)} %get-tuple-element.28), channel_id=1, source_target_pairs={{0,4},{4,0},{8,12},{12,8},{1,5},{5,1},{9,13},{13,9},{2,6},{6,2},{1... | collective-permute-start | bytes 393224 | tf_op jit(solution)/shard_map/ppermute | solution.py:290

commit v8 on v1

--- a/solution.py
+++ b/solution.py
@@ -11,7 +11,7 @@
 KVH = 4
 LOG2E = 1.4426950408889634
 ROWS = 512
-PARTS = 1
+PARTS = 2
 VMEM_LIMIT = 24 * 1024 * 1024
 
 VMEM_SPEC = pl.BlockSpec(memory_space=pltpu.VMEM)
@@ -68,14 +68,12 @@
         yield toks, cols, *(held_ref[kind, head, toks].reshape(rows, head_dim) for kind in range(2))
 
 
-def pack_kernel(key_ref, value_ref, *refs):
-    *kv_refs, held_ref, sems = refs
-    each = kv_refs[0].shape[1]
+def pack_kernel(key_ref, value_ref, kv_ref, held_ref, sems):
     copies = start_all((key_ref, value_ref), (held_ref.at[0], held_ref.at[1]), sems)
     for kind, copy in enumerate(copies):
         copy.wait()
         for head in range(held_ref.shape[2]):
-            kv_refs[head // each][kind, head % each] = held_ref[kind, :, head, :]
+            kv_ref[kind, head] = held_ref[kind, :, head, :]
 
 
 def spread_kernel(
@@ -144,7 +142,7 @@
 
 
 def choose_kernel(places_ref, *refs):
-    *column, _, _, out_ref = refs
+    *column, _, out_ref = refs
     for which in range(2):
         row = places_ref[which:which + 1]
         for kind in range(2):
@@ -169,13 +167,12 @@
 
 
 def local_kernel(factor, rows, *refs):
-    *kv_refs, query_ref, up_ref, norm_ref, term_ref, docs_ref, doc_col_ref, dkv_ref, dq_ref, held_ref, sems = refs
+    kv_ref, query_ref, up_ref, norm_ref, term_ref, docs_ref, doc_col_ref, dkv_ref, dq_ref, held_ref, sems = refs
     copies = bring_rows(query_ref, up_ref, held_ref, sems, rows)
     tokens, grouped, head_dim = held_ref.shape[2:]
-    each = kv_refs[0].shape[1]
     doc_col = jnp.concatenate([doc_col_ref[...]] * (rows // tokens), axis=1)
     for head in range(held_ref.shape[1]):
-        key_blk, value_blk = kv_refs[head // each][0, head % each], kv_refs[head // each][1, head % each]
+        key_blk, value_blk = kv_ref[0, head], kv_ref[1, head]
         grad_key = jnp.zeros((tokens, head_dim), jnp.float32)
         grad_val = jnp.zeros((tokens, head_dim), jnp.float32)
         for toks, cols, query_blk, upstream in row_blocks(held_ref, head, rows, copies):
@@ -200,10 +197,10 @@
 
 
 def listed_kernel(factor, rows, first, places_ref, *refs):
-    *column, other_ref, held_ref, norm_ref, term_ref, dkv_ref = refs
+    *column, other_ref, held_ref, norm_ref, term_ref, _, dkv_ref = refs
     tokens, grouped, head_dim = held_ref.shape[2:]
-    for head in range(other_ref.shape[2]):
-        key_blk, value_blk = far_blocks(places_ref, column, other_ref, head)
+    for head in range(dkv_ref.shape[2]):
+        key_blk, value_blk = far_blocks(places_ref, column, other_ref, first + head)
         grad_key = jnp.zeros((2 * tokens, head_dim), jnp.float32)
         grad_val = jnp.zeros((2 * tokens, head_dim), jnp.float32)
         for toks, cols, query_blk, upstream in row_blocks(held_ref, first + head, rows):
@@ -220,14 +217,11 @@
             dkv_ref[which, 1, head] = grad_val[which * tokens:(which + 1) * tokens]
 
 
-def query_kernel(factor, rows, parts, places_ref, *refs):
-    *inputs, held_ref, norm_ref, term_ref, near_ref, _, dq_ref = refs
+def query_kernel(factor, rows, places_ref, *refs):
+    *column, other_ref, held_ref, norm_ref, term_ref, near_ref, _, dq_ref = refs
     tokens, grouped, head_dim = held_ref.shape[2:]
-    size = len(inputs) // parts
-    each = held_ref.shape[1] // parts
     for head in range(held_ref.shape[1]):
-        *column, other_ref = inputs[head // each * size:(head // each + 1) * size]
-        key_blk, value_blk = far_blocks(places_ref, column, other_ref, head % each)
+        key_blk, value_blk = far_blocks(places_ref, column, other_ref, head)
         for toks, cols, query_blk, upstream in row_blocks(held_ref, head, rows):
             _, grads = tile_terms(
                 key_blk, value_blk, query_blk, upstream, norm_ref[head, :, cols], term_ref[head, :, cols],
@@ -279,7 +273,8 @@
     cols = tokens * grouped
     parts = PARTS if kv_heads % PARTS == 0 else 1
     each = kv_heads // parts
-    span_shape = (2, each, tokens, head_dim)
+    span_shape = (2, kv_heads, tokens, head_dim)
+    part_shape = (2, each, tokens, head_dim)
 
     def shifted(array, shift):
         return lax.ppermute(array, "ctx", [(i, (i + shift) % ring) for i in range(ring)])
@@ -294,13 +289,13 @@
     kv = pl.pallas_call(
         pack_kernel,
         in_specs=[HBM_SPEC] * 2,
-        out_specs=[VMEM_SPEC] * parts,
-        out_shape=[jax.ShapeDtypeStruct(span_shape, jnp.bfloat16)] * parts,
+        out_specs=VMEM_SPEC,
+        out_shape=jax.ShapeDtypeStruct(span_shape, jnp.bfloat16),
         scratch_shapes=[pltpu.VMEM((2, *keys.shape), jnp.bfloat16), pltpu.SemaphoreType.DMA((2,))],
         compiler_params=params,
         name="pack",
     )(*in_hbm(keys, values))
-    columns = [[block] + [shifted(block, shift) for shift in range(1, ring)] for block in kv]
+    column = [kv] + [shifted(kv, shift) for shift in range(1, ring)]
 
     norm, term, docs, doc_col, places = pl.pallas_call(
         functools.partial(spread_kernel, grouped, ring, subs),
@@ -329,7 +324,7 @@
     row_specs = [VMEM_SPEC] * 3
     near_kv, near_query, held = pl.pallas_call(
         functools.partial(local_kernel, factor, rows),
-        in_specs=[VMEM_SPEC] * parts + [HBM_SPEC] * 2 + [VMEM_SPEC] * 4,
+        in_specs=[VMEM_SPEC] + [HBM_SPEC] * 2 + [VMEM_SPEC] * 4,
         out_specs=[VMEM_SPEC] * 3,
         out_shape=[
             jax.ShapeDtypeStruct((2, kv_heads, tokens, head_dim), jnp.float32),
@@ -340,52 +335,56 @@
         compiler_params=params,
         cost_estimate=pl.CostEstimate(flops=5 * work, bytes_accessed=2 * moved, transcendentals=0),
         name="local_block",
-    )(*kv, *in_hbm(queries, grad_out), norm, term, docs, doc_col)
-
-    inputs, sums = [], []
-    after = near_kv
-    for part, column in enumerate(columns):
-        chosen = pl.pallas_call(
-            choose_kernel,
-            in_specs=[VMEM_SPEC] * (ring + 1) + [ANY_SPEC] * 2,
-            out_specs=VMEM_SPEC,
-            out_shape=jax.ShapeDtypeStruct((2, *span_shape), jnp.bfloat16),
-            compiler_params=params,
-            name="choose",
-        )(places, *column, near_kv, after)
-        other = swapped(chosen)
-        inputs += [*column, other]
-        far_kv = pl.pallas_call(
-            functools.partial(listed_kernel, factor, rows, part * each),
-            in_specs=[VMEM_SPEC] * (ring + 2) + row_specs,
-            out_specs=VMEM_SPEC,
-            out_shape=jax.ShapeDtypeStruct((2, *span_shape), jnp.bfloat16),
-            compiler_params=params,
-            cost_estimate=pl.CostEstimate(flops=8 * work // parts, bytes_accessed=moved // parts, transcendentals=0),
-            name="listed_keys",
-        )(places, *column, other, held, norm, term)
-        other_kv = swapped(far_kv)
+    )(kv, *in_hbm(queries, grad_out), norm, term, docs, doc_col)
+
+    chosen = pl.pallas_call(
+        choose_kernel,
+        in_specs=[VMEM_SPEC] * (ring + 1) + [ANY_SPEC],
+        out_specs=VMEM_SPEC,
+        out_shape=jax.ShapeDtypeStruct((2, *span_shape), jnp.bfloat16),
+        compiler_params=params,
+        name="choose",
+    )(places, *column, near_kv)
+    other = swapped(chosen)
+
+    sums = []
+    far_kv = [near_kv]
+    for part in range(parts):
+        far_kv.append(
+            pl.pallas_call(
+                functools.partial(listed_kernel, factor, rows, part * each),
+                in_specs=[VMEM_SPEC] * (ring + 2) + row_specs + [ANY_SPEC],
+                out_specs=VMEM_SPEC,
+                out_shape=jax.ShapeDtypeStruct((2, *part_shape), jnp.bfloat16),
+                compiler_params=params,
+                cost_estimate=pl.CostEstimate(
+                    flops=8 * work // parts, bytes_accessed=moved // parts, transcendentals=0
+                ),
+                name="listed_keys",
+            )(places, *column, other, held, norm, term, far_kv[-1])
+        )
+    for mine in far_kv[1:]:
         blocks = pl.pallas_call(
             combine_kernel,
             in_specs=[VMEM_SPEC] * 3,
             out_specs=[VMEM_SPEC] * ring,
-            out_shape=[jax.ShapeDtypeStruct(span_shape, jnp.float32)]
-            + [jax.ShapeDtypeStruct(span_shape, jnp.bfloat16)] * (ring - 1),
+            out_shape=[jax.ShapeDtypeStruct(part_shape, jnp.float32)]
+            + [jax.ShapeDtypeStruct(part_shape, jnp.bfloat16)] * (ring - 1),
             compiler_params=params,
             name="combine",
-        )(places, far_kv, other_kv)
+        )(places, mine, swapped(mine))
         sums += [blocks[0]] + [shifted(blocks[shift], shift) for shift in range(1, ring)]
         after = blocks[0]
 
     grad_queries = pl.pallas_call(
-        functools.partial(query_kernel, factor, rows, parts),
-        in_specs=[VMEM_SPEC] * (1 + len(inputs)) + row_specs + [VMEM_SPEC, ANY_SPEC],
+        functools.partial(query_kernel, factor, rows),
+        in_specs=[VMEM_SPEC] * (2 + ring) + row_specs + [VMEM_SPEC, ANY_SPEC],
         out_specs=VMEM_SPEC,
         out_shape=jax.ShapeDtypeStruct((tokens, heads, head_dim), jnp.float32),
         compiler_params=params,
         cost_estimate=pl.CostEstimate(flops=6 * work, bytes_accessed=3 * moved, transcendentals=0),
         name="listed_queries",
-    )(places, *inputs, held, norm, term, near_query, after)
+    )(places, *column, other, held, norm, term, near_query, after)
 
     grad_keys, grad_values = pl.pallas_call(
         functools.partial(total_kernel, parts),

time: 37.8 us -> 38.3 us (1.013)
  starting transfers between devices: 13.1 us -> 17.1 us
  waiting for transfers between devices: 7.72 us -> 4.34 us
    ppermute x6 -> x9, starting transfers between devices: 12.8 us -> 16.4 us  [shifted(): lax.ppermute(array, 'ctx', [(i, (i + shift) % ring) for i in range(ring)])]
    ppermute x6 -> x9, waiting for transfers between devices: 4.8 us -> 2.82 us  [shifted(): lax.ppermute(array, 'ctx', [(i, (i + shift) % ring) for i in range(ring)])]
    ppermute x2 -> x3, waiting for transfers between devices: 2.92 us -> 1.53 us  [swapped(): return lax.ppermute(array, 'sub', [(i, i ^ 1) for i in range(subs)])]
    ppermute x2 -> x3, starting transfers between devices: 0.27 us -> 0.71 us  [swapped(): return lax.ppermute(array, 'sub', [(i, i ^ 1) for i in range(subs)])]
    pallas_call x1 -> x2, Pallas kernels: 2.45 us -> 2.58 us  [body(): pl.pallas_call(functools.partial(listed_kernel, factor, rows, part * each...]
  transfers between devices with their start and end apart: 8 -> 12, of which waited for: 4 -> 4; matrix products, arithmetic and copies ran while one was open for 0% -> 0% of each run, Pallas kernels for 29% -> 32%
where the time goes in v8:
time: 38.3 us; the launch traced here: 38 us
  starting transfers between devices  17.1 us (45%)
  Pallas kernels  15.8 us (41%)
  waiting for transfers between devices  4.34 us (11%)
  between operations  0.7 us (2%)
    ppermute x9, starting transfers between devices, shifted(): lax.ppermute(array, 'ctx', [(i, (i + shift) % ring) for i in range(ring)])  16.4 us
    pallas_call x1, Pallas kernels, body(): pl.pallas_call(functools.partial(local_kernel, factor, rows), in_specs=[V...  4.93 us
    pallas_call x1, Pallas kernels, body(): pl.pallas_call(functools.partial(query_kernel, factor, rows), in_specs=[V...  4.52 us
    ppermute x9, waiting for transfers between devices, shifted(): lax.ppermute(array, 'ctx', [(i, (i + shift) % ring) for i in range(ring)])  2.82 us
    pallas_call x2, Pallas kernels, body(): pl.pallas_call(functools.partial(listed_kernel, factor, rows, part * each...  2.58 us
    ppermute x3, waiting for transfers between devices, swapped(): return lax.ppermute(array, 'sub', [(i, i ^ 1) for i in range(subs)])  1.53 us
    pallas_call x1, Pallas kernels, body(): pl.pallas_call(pack_kernel, in_specs=[HBM_SPEC] * 2, out_specs=VMEM_SPEC,...  1.24 us
    pallas_call x1, Pallas kernels, body(): pl.pallas_call(functools.partial(spread_kernel, grouped, ring, subs), in_...  1.18 us
  transfers between devices with their start and end apart: 12, of which 4 were waited for; matrix products, arithmetic and copies ran while one was open for 0% of the time, Pallas kernels for 32%

profile of v8, /device:TPU:0, one launch (start us, length us, event | category | flops | bytes accessed | tf_op | source)
XLA Modules:
  0.0 38.0 jit_solution(12062445172865249893)
XLA Ops:
  0.6 1.2 %pack.1.refs_0_ = bf16[2,2,128,128]{3,2,1,0:T(8,128)(2,1)S(1)} custom-call(bf16[128,2,128]{2,1,0:T(2,128)(2,1)} %key_ref.1, bf16[128,2,128]{2,1,0:T(2,128)(2,1)} %value_ref.1), custom_call_target="tpu_custom_call" | custom-call | tf_op jit(solution)/shard_map/pack/pallas_call | solution.py:289
  1.9 3.1 %collective-permute-start = (bf16[2,2,128,128]{3,2,1,0:T(8,128)(2,1)S(1)}, bf16[2,2,128,128]{3,2,1,0:T(8,128)(2,1)S(1)}, u32[]{:S(2)}, u32[]{:S(2)}) collective-permute-start(bf16[2,2,128,128]{3,2,1,0:T(8,128)(2,1)S(1)} %pack.1.refs_0_), channel_id=1, source_target_pairs={{0,4},{4,8},{8,12},{12,0},{1,5},{5,9},{9,13},{13,1},{2,6},{6,10},{... | collective-permute-start | bytes 393224 | tf_op jit(solution)/shard_map/ppermute | solution.py:280
  5.0 2.6 %collective-permute-start.1 = (bf16[2,2,128,128]{3,2,1,0:T(8,128)(2,1)S(1)}, bf16[2,2,128,128]{3,2,1,0:T(8,128)(2,1)S(1)}, u32[]{:S(2)}, u32[]{:S(2)}) collective-permute-start(bf16[2,2,128,128]{3,2,1,0:T(8,128)(2,1)S(1)} %pack.1.refs_0_), channel_id=1, source_target_pairs={{0,8},{4,12},{8,0},{12,4},{1,9},{5,13},{9,1},{13,5},{2,10},{6,14},... | collective-permute-start | bytes 393224 | tf_op jit(solution)/shard_map/ppermute | solution.py:280
  7.5 1.3 %collective-permute-start.2 = (bf16[2,2,128,128]{3,2,1,0:T(8,128)(2,1)S(1)}, bf16[2,2,128,128]{3,2,1,0:T(8,128)(2,1)S(1)}, u32[]{:S(2)}, u32[]{:S(2)}) collective-permute-start(bf16[2,2,128,128]{3,2,1,0:T(8,128)(2,1)S(1)} %pack.1.refs_0_), channel_id=1, source_target_pairs={{0,12},{4,0},{8,4},{12,8},{1,13},{5,1},{9,5},{13,9},{2,14},{6,2},{... | collective-permute-start | bytes 393224 | tf_op jit(solution)/shard_map/ppermute | solution.py:280
  8.9 1.2 %spread.1 = (f32[2,1,2048]{2,1,0:T(1,128)S(1)}, f32[2,1,2048]{2,1,0:T(1,128)S(1)}, f32[1,2048]{1,0:T(1,128)S(1)}, f32[128,128]{1,0:T(8,128)S(1)}, s32[8,128]{1,0:T(8,128)S(1)}) custom-call(f32[32,128]{1,0:T(8,128)} %bitcast.4, f32[32,128]{1,0:T(8,128)} %bitcast.5, s32[1,128]{1,0:T(1,128)} %bitcast.7, s32[2,8]{1,0:T(2,128)} %bitcast.6), custom_call_target="tpu_custom_call" | custom-call | tf_op jit(solution)/shard_map/spread/pallas_call | solution.py:300
  10.1 4.9 %local_block.1 = (f32[2,2,128,128]{3,2,1,0:T(8,128)S(1)}, f32[128,32,128]{2,1,0:T(8,128)S(1)}, bf16[2,2,128,16,128]{4,3,2,1,0:T(8,128)(2,1)S(1)}) custom-call(bf16[2,2,128,128]{3,2,1,0:T(8,128)(2,1)S(1)} %pack.1.refs_0_, bf16[128,32,128]{2,1,0:T(8,128)(2,1)} %refs_1_.1, bf16[128,32,128]{2,1,0:T(8,128)(2,1)} %refs_2_.1, ...), custom_call_target="tpu_custom_call" | custom-call | flops 671088640 | bytes 4194304 | tf_op jit(solution)/shard_map/local_block/pallas_call | solution.py:325
  15.0 0.0 collective-permute-done.refs_1_
  15.0 1.2 %collective-permute-done.1.refs_2_ = bf16[2,2,128,128]{3,2,1,0:T(8,128)(2,1)S(1)} collective-permute-done((bf16[2,2,128,128]{3,2,1,0:T(8,128)(2,1)S(1)}, bf16[2,2,128,128]{3,2,1,0:T(8,128)(2,1)S(1)}, u32[]{:S(2)}, u32[]{:S(2)}) %collective-permute-start.1) | collective-permute-done | bytes 131104 | tf_op jit(solution)/shard_map/ppermute | solution.py:280
  16.2 0.0 collective-permute-done.2.refs_3_
  16.2 0.1 choose.1
  16.3 0.1 collective-permute-start.3
  16.4 1.5 %collective-permute-done.3.refs_4_ = bf16[2,2,2,128,128]{4,3,2,1,0:T(8,128)(2,1)S(1)} collective-permute-done((bf16[2,2,2,128,128]{4,3,2,1,0:T(8,128)(2,1)S(1)}, bf16[2,2,2,128,128]{4,3,2,1,0:T(8,128)(2,1)S(1)}, u32[]{:S(2)}, u32[]{:S(2)}) %collective-permute-start.3) | collective-permute-done | bytes 262176 | tf_op jit(solution)/shard_map/ppermute | solution.py:283
  17.9 1.3 %listed_keys.2.refs_8_.mine_ref = bf16[2,2,1,128,128]{4,3,2,1,0:T(8,128)(2,1)S(1)} custom-call(s32[8,128]{1,0:T(8,128)S(1)} %get-tuple-element.21.places_ref, bf16[2,2,128,128]{3,2,1,0:T(8,128)(2,1)S(1)} %pack.1.refs_0_, bf16[2,2,128,128]{3,2,1,0:T(8,128)(2,1)S(1)} %collective-permute-done.refs_1_, ...), custom_call_target="tpu_custom_call" | custom-call | flops 536870912 | bytes 1048576 | tf_op jit(solution)/shard_map/listed_keys/pallas_call | solution.py:354
  19.2 0.2 collective-permute-start.5
  19.4 1.3 %listed_keys.3.mine_ref = bf16[2,2,1,128,128]{4,3,2,1,0:T(8,128)(2,1)S(1)} custom-call(s32[8,128]{1,0:T(8,128)S(1)} %get-tuple-element.21.places_ref, bf16[2,2,128,128]{3,2,1,0:T(8,128)(2,1)S(1)} %pack.1.refs_0_, bf16[2,2,128,128]{3,2,1,0:T(8,128)(2,1)S(1)} %collective-permute-done.refs_1_, bf16[2,2,128,128]{3,2,1,0:T(8,128)(2,1)S(1)} %collective-permute-done.1.refs_2_, ...), custom_call_target="tpu_custom_call" | custom-call | flops 536870912 | bytes 1048576 | tf_op jit(solution)/shard_map/listed_keys/pallas_call | solution.py:354
  20.7 0.4 %collective-permute-start.4 = (bf16[2,2,1,128,128]{4,3,2,1,0:T(8,128)(2,1)S(1)}, bf16[2,2,1,128,128]{4,3,2,1,0:T(8,128)(2,1)S(1)}, u32[]{:S(2)}, u32[]{:S(2)}) collective-permute-start(bf16[2,2,1,128,128]{4,3,2,1,0:T(8,128)(2,1)S(1)} %listed_keys.3.mine_ref), channel_id=1, source_target_pairs={{0,1},{1,0},{2,3},{3,2},{4,5},{5,4},{6,7},{7,6},{8,9},{9,8},{10,11... | collective-permute-start | bytes 393224 | tf_op jit(solution)/shard_map/ppermute | solution.py:283
  21.2 0.0 collective-permute-done.5.other_ref
  21.2 0.2 combine.3
  21.4 3.3 %collective-permute-start.6 = (bf16[2,1,128,128]{3,2,1,0:T(8,128)(2,1)S(1)}, bf16[2,1,128,128]{3,2,1,0:T(8,128)(2,1)S(1)}, u32[]{:S(2)}, u32[]{:S(2)}) collective-permute-start(bf16[2,1,128,128]{3,2,1,0:T(8,128)(2,1)S(1)} %get-tuple-element.31), channel_id=1, source_target_pairs={{0,4},{4,8},{8,12},{12,0},{1,5},{5,9},{9,13},{13,1},{2,6},{6,10},{... | collective-permute-start | bytes 196616 | tf_op jit(solution)/shard_map/ppermute | solution.py:280
  24.7 1.6 %collective-permute-start.7 = (bf16[2,1,128,128]{3,2,1,0:T(8,128)(2,1)S(1)}, bf16[2,1,128,128]{3,2,1,0:T(8,128)(2,1)S(1)}, u32[]{:S(2)}, u32[]{:S(2)}) collective-permute-start(bf16[2,1,128,128]{3,2,1,0:T(8,128)(2,1)S(1)} %get-tuple-element.32), channel_id=1, source_target_pairs={{0,8},{4,12},{8,0},{12,4},{1,9},{5,13},{9,1},{13,5},{2,10},{6,14},... | collective-permute-start | bytes 196616 | tf_op jit(solution)/shard_map/ppermute | solution.py:280
  26.3 0.8 %collective-permute-start.8 = (bf16[2,1,128,128]{3,2,1,0:T(8,128)(2,1)S(1)}, bf16[2,1,128,128]{3,2,1,0:T(8,128)(2,1)S(1)}, u32[]{:S(2)}, u32[]{:S(2)}) collective-permute-start(bf16[2,1,128,128]{3,2,1,0:T(8,128)(2,1)S(1)} %get-tuple-element.33), channel_id=1, source_target_pairs={{0,12},{4,0},{8,4},{12,8},{1,13},{5,1},{9,5},{13,9},{2,14},{6,2},{... | collective-permute-start | bytes 196616 | tf_op jit(solution)/shard_map/ppermute | solution.py:280
  27.1 0.0 collective-permute-done.4.other_ref
  27.1 0.2 combine.2
  27.4 0.8 %collective-permute-start.10 = (bf16[2,1,128,128]{3,2,1,0:T(8,128)(2,1)S(1)}, bf16[2,1,128,128]{3,2,1,0:T(8,128)(2,1)S(1)}, u32[]{:S(2)}, u32[]{:S(2)}) collective-permute-start(bf16[2,1,128,128]{3,2,1,0:T(8,128)(2,1)S(1)} %get-tuple-element.35), channel_id=1, source_target_pairs={{0,8},{4,12},{8,0},{12,4},{1,9},{5,13},{9,1},{13,5},{2,10},{6,14},... | collective-permute-start | bytes 196616 | tf_op jit(solution)/shard_map/ppermute | solution.py:280
  28.1 2.8 %collective-permute-start.11 = (bf16[2,1,128,128]{3,2,1,0:T(8,128)(2,1)S(1)}, bf16[2,1,128,128]{3,2,1,0:T(8,128)(2,1)S(1)}, u32[]{:S(2)}, u32[]{:S(2)}) collective-permute-start(bf16[2,1,128,128]{3,2,1,0:T(8,128)(2,1)S(1)} %get-tuple-element.36), channel_id=1, source_target_pairs={{0,12},{4,0},{8,4},{12,8},{1,13},{5,1},{9,5},{13,9},{2,14},{6,2},{... | collective-permute-start | bytes 196616 | tf_op jit(solution)/shard_map/ppermute | solution.py:280
  31.0 0.0 collective-permute-done.6.refs_1_
  31.0 0.0 collective-permute-start.9
  31.0 4.5 %listed_queries.1 = f32[128,32,128]{2,1,0:T(8,128)} custom-call(s32[8,128]{1,0:T(8,128)S(1)} %get-tuple-element.21.places_ref, bf16[2,2,128,128]{3,2,1,0:T(8,128)(2,1)S(1)} %pack.1.refs_0_, bf16[2,2,128,128]{3,2,1,0:T(8,128)(2,1)S(1)} %collective-permute-done.refs_1_, bf16[2,2,128,128]{3,2,1,0:T(8,128)(2,1)S(1)} %collective-permute-done.1.refs_2_, ...), custom_call_target="tpu_custom_call" | custom-call | flops 805306368 | bytes 6291456 | tf_op jit(solution)/shard_map/listed_queries/pallas_call | solution.py:379
  35.5 0.0 collective-permute-done.7.refs_2_
  35.5 0.0 collective-permute-done.8.refs_3_
  35.5 0.5 %collective-permute-done.10.refs_6_ = bf16[2,1,128,128]{3,2,1,0:T(8,128)(2,1)S(1)} collective-permute-done((bf16[2,1,128,128]{3,2,1,0:T(8,128)(2,1)S(1)}, bf16[2,1,128,128]{3,2,1,0:T(8,128)(2,1)S(1)}, u32[]{:S(2)}, u32[]{:S(2)}) %collective-permute-start.10) | collective-permute-done | bytes 65568 | tf_op jit(solution)/shard_map/ppermute | solution.py:280
  36.0 0.0 collective-permute-done.11.refs_7_
  36.0 1.2 %collective-permute-done.9.refs_5_ = bf16[2,1,128,128]{3,2,1,0:T(8,128)(2,1)S(1)} collective-permute-done((bf16[2,1,128,128]{3,2,1,0:T(8,128)(2,1)S(1)}, bf16[2,1,128,128]{3,2,1,0:T(8,128)(2,1)S(1)}, u32[]{:S(2)}, u32[]{:S(2)}) %collective-permute-start.9) | collective-permute-done | bytes 65568 | tf_op jit(solution)/shard_map/ppermute | solution.py:280
  37.2 0.8 %total.1 = (f32[128,2,128]{2,1,0:T(2,128)}, f32[128,2,128]{2,1,0:T(2,128)}) custom-call(f32[2,2,128,128]{3,2,1,0:T(8,128)S(1)} %get-tuple-element.26.refs_4_.refs_8_.near_ref, f32[2,1,128,128]{3,2,1,0:T(8,128)S(1)} %get-tuple-element.30.refs_0_, bf16[2,1,128,128]{3,2,1,0:T(8,128)(2,1)S(1)} %collective-permute-done.6.refs_1_, ...), custom_call_target="tpu_custom_call" | custom-call | tf_op jit(solution)/shard_map/total/pallas_call | solution.py:389
Async XLA Ops:
  1.9 13.1 %collective-permute-start = (bf16[2,2,128,128]{3,2,1,0:T(8,128)(2,1)S(1)}, bf16[2,2,128,128]{3,2,1,0:T(8,128)(2,1)S(1)}, u32[]{:S(2)}, u32[]{:S(2)}) collective-permute-start(bf16[2,2,128,128]{3,2,1,0:T(8,128)(2,1)S(1)} %pack.1.refs_0_), channel_id=1, source_target_pairs={{0,4},{4,8},{8,12},{12,0},{1,5},{5,9},{9,13},{13,1},{2,6},{6,10},{... | collective-permute-start | bytes 393224 | tf_op jit(solution)/shard_map/ppermute | solution.py:280
  5.0 11.2 %collective-permute-start.1 = (bf16[2,2,128,128]{3,2,1,0:T(8,128)(2,1)S(1)}, bf16[2,2,128,128]{3,2,1,0:T(8,128)(2,1)S(1)}, u32[]{:S(2)}, u32[]{:S(2)}) collective-permute-start(bf16[2,2,128,128]{3,2,1,0:T(8,128)(2,1)S(1)} %pack.1.refs_0_), channel_id=1, source_target_pairs={{0,8},{4,12},{8,0},{12,4},{1,9},{5,13},{9,1},{13,5},{2,10},{6,14},... | collective-permute-start | bytes 393224 | tf_op jit(solution)/shard_map/ppermute | solution.py:280
  7.5 8.6 %collective-permute-start.2 = (bf16[2,2,128,128]{3,2,1,0:T(8,128)(2,1)S(1)}, bf16[2,2,128,128]{3,2,1,0:T(8,128)(2,1)S(1)}, u32[]{:S(2)}, u32[]{:S(2)}) collective-permute-start(bf16[2,2,128,128]{3,2,1,0:T(8,128)(2,1)S(1)} %pack.1.refs_0_), channel_id=1, source_target_pairs={{0,12},{4,0},{8,4},{12,8},{1,13},{5,1},{9,5},{13,9},{2,14},{6,2},{... | collective-permute-start | bytes 393224 | tf_op jit(solution)/shard_map/ppermute | solution.py:280
  16.3 1.6 %collective-permute-start.3 = (bf16[2,2,2,128,128]{4,3,2,1,0:T(8,128)(2,1)S(1)}, bf16[2,2,2,128,128]{4,3,2,1,0:T(8,128)(2,1)S(1)}, u32[]{:S(2)}, u32[]{:S(2)}) collective-permute-start(bf16[2,2,2,128,128]{4,3,2,1,0:T(8,128)(2,1)S(1)} %choose.1), channel_id=1, source_target_pairs={{0,1},{1,0},{2,3},{3,2},{4,5},{5,4},{6,7},{7,6},{8,9},{9,8},{10,11... | collective-permute-start | bytes 786440 | tf_op jit(solution)/shard_map/ppermute | solution.py:283
  19.2 1.9 %collective-permute-start.5 = (bf16[2,2,1,128,128]{4,3,2,1,0:T(8,128)(2,1)S(1)}, bf16[2,2,1,128,128]{4,3,2,1,0:T(8,128)(2,1)S(1)}, u32[]{:S(2)}, u32[]{:S(2)}) collective-permute-start(bf16[2,2,1,128,128]{4,3,2,1,0:T(8,128)(2,1)S(1)} %listed_keys.2.refs_8_.mine_ref), channel_id=1, source_target_pairs={{0,1},{1,0},{2,3},{3,2},{4,5},{5,4},{6,7},{7,6},{8,9},{9,8},{10,11... | collective-permute-start | bytes 393224 | tf_op jit(solution)/shard_map/ppermute | solution.py:283
  20.7 6.4 %collective-permute-start.4 = (bf16[2,2,1,128,128]{4,3,2,1,0:T(8,128)(2,1)S(1)}, bf16[2,2,1,128,128]{4,3,2,1,0:T(8,128)(2,1)S(1)}, u32[]{:S(2)}, u32[]{:S(2)}) collective-permute-start(bf16[2,2,1,128,128]{4,3,2,1,0:T(8,128)(2,1)S(1)} %listed_keys.3.mine_ref), channel_id=1, source_target_pairs={{0,1},{1,0},{2,3},{3,2},{4,5},{5,4},{6,7},{7,6},{8,9},{9,8},{10,11... | collective-permute-start | bytes 393224 | tf_op jit(solution)/shard_map/ppermute | solution.py:283
  21.4 9.6 %collective-permute-start.6 = (bf16[2,1,128,128]{3,2,1,0:T(8,128)(2,1)S(1)}, bf16[2,1,128,128]{3,2,1,0:T(8,128)(2,1)S(1)}, u32[]{:S(2)}, u32[]{:S(2)}) collective-permute-start(bf16[2,1,128,128]{3,2,1,0:T(8,128)(2,1)S(1)} %get-tuple-element.31), channel_id=1, source_target_pairs={{0,4},{4,8},{8,12},{12,0},{1,5},{5,9},{9,13},{13,1},{2,6},{6,10},{... | collective-permute-start | bytes 196616 | tf_op jit(solution)/shard_map/ppermute | solution.py:280
  24.7 10.8 %collective-permute-start.7 = (bf16[2,1,128,128]{3,2,1,0:T(8,128)(2,1)S(1)}, bf16[2,1,128,128]{3,2,1,0:T(8,128)(2,1)S(1)}, u32[]{:S(2)}, u32[]{:S(2)}) collective-permute-start(bf16[2,1,128,128]{3,2,1,0:T(8,128)(2,1)S(1)} %get-tuple-element.32), channel_id=1, source_target_pairs={{0,8},{4,12},{8,0},{12,4},{1,9},{5,13},{9,1},{13,5},{2,10},{6,14},... | collective-permute-start | bytes 196616 | tf_op jit(solution)/shard_map/ppermute | solution.py:280
  26.3 9.2 %collective-permute-start.8 = (bf16[2,1,128,128]{3,2,1,0:T(8,128)(2,1)S(1)}, bf16[2,1,128,128]{3,2,1,0:T(8,128)(2,1)S(1)}, u32[]{:S(2)}, u32[]{:S(2)}) collective-permute-start(bf16[2,1,128,128]{3,2,1,0:T(8,128)(2,1)S(1)} %get-tuple-element.33), channel_id=1, source_target_pairs={{0,12},{4,0},{8,4},{12,8},{1,13},{5,1},{9,5},{13,9},{2,14},{6,2},{... | collective-permute-start | bytes 196616 | tf_op jit(solution)/shard_map/ppermute | solution.py:280
  27.4 8.6 %collective-permute-start.10 = (bf16[2,1,128,128]{3,2,1,0:T(8,128)(2,1)S(1)}, bf16[2,1,128,128]{3,2,1,0:T(8,128)(2,1)S(1)}, u32[]{:S(2)}, u32[]{:S(2)}) collective-permute-start(bf16[2,1,128,128]{3,2,1,0:T(8,128)(2,1)S(1)} %get-tuple-element.35), channel_id=1, source_target_pairs={{0,8},{4,12},{8,0},{12,4},{1,9},{5,13},{9,1},{13,5},{2,10},{6,14},... | collective-permute-start | bytes 196616 | tf_op jit(solution)/shard_map/ppermute | solution.py:280
  28.1 7.8 %collective-permute-start.11 = (bf16[2,1,128,128]{3,2,1,0:T(8,128)(2,1)S(1)}, bf16[2,1,128,128]{3,2,1,0:T(8,128)(2,1)S(1)}, u32[]{:S(2)}, u32[]{:S(2)}) collective-permute-start(bf16[2,1,128,128]{3,2,1,0:T(8,128)(2,1)S(1)} %get-tuple-element.36), channel_id=1, source_target_pairs={{0,12},{4,0},{8,4},{12,8},{1,13},{5,1},{9,5},{13,9},{2,14},{6,2},{... | collective-permute-start | bytes 196616 | tf_op jit(solution)/shard_map/ppermute | solution.py:280
  31.0 6.2 %collective-permute-start.9 = (bf16[2,1,128,128]{3,2,1,0:T(8,128)(2,1)S(1)}, bf16[2,1,128,128]{3,2,1,0:T(8,128)(2,1)S(1)}, u32[]{:S(2)}, u32[]{:S(2)}) collective-permute-start(bf16[2,1,128,128]{3,2,1,0:T(8,128)(2,1)S(1)} %get-tuple-element.34), channel_id=1, source_target_pairs={{0,4},{4,8},{8,12},{12,0},{1,5},{5,9},{9,13},{13,1},{2,6},{6,10},{... | collective-permute-start | bytes 196616 | tf_op jit(solution)/shard_map/ppermute | solution.py:280

commit v9 on v8

--- a/solution.py
+++ b/solution.py
@@ -373,7 +373,8 @@
             compiler_params=params,
             name="combine",
         )(places, mine, swapped(mine))
-        sums += [blocks[0]] + [shifted(blocks[shift], shift) for shift in range(1, ring)]
+        order = [*range(1, ring)] if mine is far_kv[1] else [ring - 1, *range(1, ring - 1)]
+        sums += [blocks[0]] + [shifted(blocks[shift], shift) for shift in order]
         after = blocks[0]
 
     grad_queries = pl.pallas_call(

time: 38.3 us -> 37.8 us (0.987)
  waiting for transfers between devices: 4.34 us -> 3.62 us
    ppermute x9, waiting for transfers between devices: 2.82 us -> 2.1 us  [shifted(): lax.ppermute(array, 'ctx', [(i, (i + shift) % ring) for i in range(ring)])]
  transfers between devices with their start and end apart: 12 -> 12, of which waited for: 4 -> 3; matrix products, arithmetic and copies ran while one was open for 0% -> 0% of each run, Pallas kernels for 32% -> 33%
where the time goes in v9:
time: 37.8 us; the launch traced here: 37.5 us
  starting transfers between devices  17.4 us (46%)
  Pallas kernels  15.8 us (42%)
  waiting for transfers between devices  3.62 us (10%)
  between operations  0.71 us (2%)
    ppermute x9, starting transfers between devices, shifted(): lax.ppermute(array, 'ctx', [(i, (i + shift) % ring) for i in range(ring)])  16.7 us
    pallas_call x1, Pallas kernels, body(): pl.pallas_call(functools.partial(local_kernel, factor, rows), in_specs=[V...  4.93 us
    pallas_call x1, Pallas kernels, body(): pl.pallas_call(functools.partial(query_kernel, factor, rows), in_specs=[V...  4.52 us
    pallas_call x2, Pallas kernels, body(): pl.pallas_call(functools.partial(listed_kernel, factor, rows, part * each...  2.58 us
    ppermute x9, waiting for transfers between devices, shifted(): lax.ppermute(array, 'ctx', [(i, (i + shift) % ring) for i in range(ring)])  2.1 us
    ppermute x3, waiting for transfers between devices, swapped(): return lax.ppermute(array, 'sub', [(i, i ^ 1) for i in range(subs)])  1.53 us
    pallas_call x1, Pallas kernels, body(): pl.pallas_call(pack_kernel, in_specs=[HBM_SPEC] * 2, out_specs=VMEM_SPEC,...  1.24 us
    pallas_call x1, Pallas kernels, body(): pl.pallas_call(functools.partial(spread_kernel, grouped, ring, subs), in_...  1.18 us
  transfers between devices with their start and end apart: 12, of which 3 were waited for; matrix products, arithmetic and copies ran while one was open for 0% of the time, Pallas kernels for 33%

profile of v9, /device:TPU:0, one launch (start us, length us, event | category | flops | bytes accessed | tf_op | source)
XLA Modules:
  0.0 37.5 jit_solution(12786630646347929313)
XLA Ops:
  0.6 1.2 %pack.1.refs_0_ = bf16[2,2,128,128]{3,2,1,0:T(8,128)(2,1)S(1)} custom-call(bf16[128,2,128]{2,1,0:T(2,128)(2,1)} %key_ref.1, bf16[128,2,128]{2,1,0:T(2,128)(2,1)} %value_ref.1), custom_call_target="tpu_custom_call" | custom-call | tf_op jit(solution)/shard_map/pack/pallas_call | solution.py:289
  1.9 3.1 %collective-permute-start = (bf16[2,2,128,128]{3,2,1,0:T(8,128)(2,1)S(1)}, bf16[2,2,128,128]{3,2,1,0:T(8,128)(2,1)S(1)}, u32[]{:S(2)}, u32[]{:S(2)}) collective-permute-start(bf16[2,2,128,128]{3,2,1,0:T(8,128)(2,1)S(1)} %pack.1.refs_0_), channel_id=1, source_target_pairs={{0,4},{4,8},{8,12},{12,0},{1,5},{5,9},{9,13},{13,1},{2,6},{6,10},{... | collective-permute-start | bytes 393224 | tf_op jit(solution)/shard_map/ppermute | solution.py:280
  5.0 2.6 %collective-permute-start.1 = (bf16[2,2,128,128]{3,2,1,0:T(8,128)(2,1)S(1)}, bf16[2,2,128,128]{3,2,1,0:T(8,128)(2,1)S(1)}, u32[]{:S(2)}, u32[]{:S(2)}) collective-permute-start(bf16[2,2,128,128]{3,2,1,0:T(8,128)(2,1)S(1)} %pack.1.refs_0_), channel_id=1, source_target_pairs={{0,8},{4,12},{8,0},{12,4},{1,9},{5,13},{9,1},{13,5},{2,10},{6,14},... | collective-permute-start | bytes 393224 | tf_op jit(solution)/shard_map/ppermute | solution.py:280
  7.5 1.3 %collective-permute-start.2 = (bf16[2,2,128,128]{3,2,1,0:T(8,128)(2,1)S(1)}, bf16[2,2,128,128]{3,2,1,0:T(8,128)(2,1)S(1)}, u32[]{:S(2)}, u32[]{:S(2)}) collective-permute-start(bf16[2,2,128,128]{3,2,1,0:T(8,128)(2,1)S(1)} %pack.1.refs_0_), channel_id=1, source_target_pairs={{0,12},{4,0},{8,4},{12,8},{1,13},{5,1},{9,5},{13,9},{2,14},{6,2},{... | collective-permute-start | bytes 393224 | tf_op jit(solution)/shard_map/ppermute | solution.py:280
  8.9 1.2 %spread.1 = (f32[2,1,2048]{2,1,0:T(1,128)S(1)}, f32[2,1,2048]{2,1,0:T(1,128)S(1)}, f32[1,2048]{1,0:T(1,128)S(1)}, f32[128,128]{1,0:T(8,128)S(1)}, s32[8,128]{1,0:T(8,128)S(1)}) custom-call(f32[32,128]{1,0:T(8,128)} %bitcast.4, f32[32,128]{1,0:T(8,128)} %bitcast.5, s32[1,128]{1,0:T(1,128)} %bitcast.7, s32[2,8]{1,0:T(2,128)} %bitcast.6), custom_call_target="tpu_custom_call" | custom-call | tf_op jit(solution)/shard_map/spread/pallas_call | solution.py:300
  10.1 4.9 %local_block.1 = (f32[2,2,128,128]{3,2,1,0:T(8,128)S(1)}, f32[128,32,128]{2,1,0:T(8,128)S(1)}, bf16[2,2,128,16,128]{4,3,2,1,0:T(8,128)(2,1)S(1)}) custom-call(bf16[2,2,128,128]{3,2,1,0:T(8,128)(2,1)S(1)} %pack.1.refs_0_, bf16[128,32,128]{2,1,0:T(8,128)(2,1)} %refs_1_.1, bf16[128,32,128]{2,1,0:T(8,128)(2,1)} %refs_2_.1, ...), custom_call_target="tpu_custom_call" | custom-call | flops 671088640 | bytes 4194304 | tf_op jit(solution)/shard_map/local_block/pallas_call | solution.py:325
  15.0 0.0 collective-permute-done.refs_1_
  15.0 1.2 %collective-permute-done.1.refs_2_ = bf16[2,2,128,128]{3,2,1,0:T(8,128)(2,1)S(1)} collective-permute-done((bf16[2,2,128,128]{3,2,1,0:T(8,128)(2,1)S(1)}, bf16[2,2,128,128]{3,2,1,0:T(8,128)(2,1)S(1)}, u32[]{:S(2)}, u32[]{:S(2)}) %collective-permute-start.1) | collective-permute-done | bytes 131104 | tf_op jit(solution)/shard_map/ppermute | solution.py:280
  16.2 0.0 collective-permute-done.2.refs_3_
  16.2 0.1 choose.1
  16.3 0.1 collective-permute-start.3
  16.4 1.5 %collective-permute-done.3.refs_4_ = bf16[2,2,2,128,128]{4,3,2,1,0:T(8,128)(2,1)S(1)} collective-permute-done((bf16[2,2,2,128,128]{4,3,2,1,0:T(8,128)(2,1)S(1)}, bf16[2,2,2,128,128]{4,3,2,1,0:T(8,128)(2,1)S(1)}, u32[]{:S(2)}, u32[]{:S(2)}) %collective-permute-start.3) | collective-permute-done | bytes 262176 | tf_op jit(solution)/shard_map/ppermute | solution.py:283
  17.9 1.3 %listed_keys.2.refs_8_.mine_ref = bf16[2,2,1,128,128]{4,3,2,1,0:T(8,128)(2,1)S(1)} custom-call(s32[8,128]{1,0:T(8,128)S(1)} %get-tuple-element.21.places_ref, bf16[2,2,128,128]{3,2,1,0:T(8,128)(2,1)S(1)} %pack.1.refs_0_, bf16[2,2,128,128]{3,2,1,0:T(8,128)(2,1)S(1)} %collective-permute-done.refs_1_, ...), custom_call_target="tpu_custom_call" | custom-call | flops 536870912 | bytes 1048576 | tf_op jit(solution)/shard_map/listed_keys/pallas_call | solution.py:354
  19.2 0.2 collective-permute-start.5
  19.4 1.3 %listed_keys.3.mine_ref = bf16[2,2,1,128,128]{4,3,2,1,0:T(8,128)(2,1)S(1)} custom-call(s32[8,128]{1,0:T(8,128)S(1)} %get-tuple-element.21.places_ref, bf16[2,2,128,128]{3,2,1,0:T(8,128)(2,1)S(1)} %pack.1.refs_0_, bf16[2,2,128,128]{3,2,1,0:T(8,128)(2,1)S(1)} %collective-permute-done.refs_1_, bf16[2,2,128,128]{3,2,1,0:T(8,128)(2,1)S(1)} %collective-permute-done.1.refs_2_, ...), custom_call_target="tpu_custom_call" | custom-call | flops 536870912 | bytes 1048576 | tf_op jit(solution)/shard_map/listed_keys/pallas_call | solution.py:354
  20.7 0.4 %collective-permute-start.4 = (bf16[2,2,1,128,128]{4,3,2,1,0:T(8,128)(2,1)S(1)}, bf16[2,2,1,128,128]{4,3,2,1,0:T(8,128)(2,1)S(1)}, u32[]{:S(2)}, u32[]{:S(2)}) collective-permute-start(bf16[2,2,1,128,128]{4,3,2,1,0:T(8,128)(2,1)S(1)} %listed_keys.3.mine_ref), channel_id=1, source_target_pairs={{0,1},{1,0},{2,3},{3,2},{4,5},{5,4},{6,7},{7,6},{8,9},{9,8},{10,11... | collective-permute-start | bytes 393224 | tf_op jit(solution)/shard_map/ppermute | solution.py:283
  21.2 0.0 collective-permute-done.5.other_ref
  21.2 0.2 combine.3
  21.4 3.3 %collective-permute-start.6 = (bf16[2,1,128,128]{3,2,1,0:T(8,128)(2,1)S(1)}, bf16[2,1,128,128]{3,2,1,0:T(8,128)(2,1)S(1)}, u32[]{:S(2)}, u32[]{:S(2)}) collective-permute-start(bf16[2,1,128,128]{3,2,1,0:T(8,128)(2,1)S(1)} %get-tuple-element.31), channel_id=1, source_target_pairs={{0,4},{4,8},{8,12},{12,0},{1,5},{5,9},{9,13},{13,1},{2,6},{6,10},{... | collective-permute-start | bytes 196616 | tf_op jit(solution)/shard_map/ppermute | solution.py:280
  24.7 1.6 %collective-permute-start.7 = (bf16[2,1,128,128]{3,2,1,0:T(8,128)(2,1)S(1)}, bf16[2,1,128,128]{3,2,1,0:T(8,128)(2,1)S(1)}, u32[]{:S(2)}, u32[]{:S(2)}) collective-permute-start(bf16[2,1,128,128]{3,2,1,0:T(8,128)(2,1)S(1)} %get-tuple-element.32), channel_id=1, source_target_pairs={{0,8},{4,12},{8,0},{12,4},{1,9},{5,13},{9,1},{13,5},{2,10},{6,14},... | collective-permute-start | bytes 196616 | tf_op jit(solution)/shard_map/ppermute | solution.py:280
  26.3 0.8 %collective-permute-start.8 = (bf16[2,1,128,128]{3,2,1,0:T(8,128)(2,1)S(1)}, bf16[2,1,128,128]{3,2,1,0:T(8,128)(2,1)S(1)}, u32[]{:S(2)}, u32[]{:S(2)}) collective-permute-start(bf16[2,1,128,128]{3,2,1,0:T(8,128)(2,1)S(1)} %get-tuple-element.33), channel_id=1, source_target_pairs={{0,12},{4,0},{8,4},{12,8},{1,13},{5,1},{9,5},{13,9},{2,14},{6,2},{... | collective-permute-start | bytes 196616 | tf_op jit(solution)/shard_map/ppermute | solution.py:280
  27.1 0.0 collective-permute-done.4.other_ref
  27.1 0.2 combine.2
  27.4 1.3 %collective-permute-start.10 = (bf16[2,1,128,128]{3,2,1,0:T(8,128)(2,1)S(1)}, bf16[2,1,128,128]{3,2,1,0:T(8,128)(2,1)S(1)}, u32[]{:S(2)}, u32[]{:S(2)}) collective-permute-start(bf16[2,1,128,128]{3,2,1,0:T(8,128)(2,1)S(1)} %get-tuple-element.35), channel_id=1, source_target_pairs={{0,4},{4,8},{8,12},{12,0},{1,5},{5,9},{9,13},{13,1},{2,6},{6,10},{... | collective-permute-start | bytes 196616 | tf_op jit(solution)/shard_map/ppermute | solution.py:280
  28.6 1.3 %collective-permute-start.11 = (bf16[2,1,128,128]{3,2,1,0:T(8,128)(2,1)S(1)}, bf16[2,1,128,128]{3,2,1,0:T(8,128)(2,1)S(1)}, u32[]{:S(2)}, u32[]{:S(2)}) collective-permute-start(bf16[2,1,128,128]{3,2,1,0:T(8,128)(2,1)S(1)} %get-tuple-element.36), channel_id=1, source_target_pairs={{0,8},{4,12},{8,0},{12,4},{1,9},{5,13},{9,1},{13,5},{2,10},{6,14},... | collective-permute-start | bytes 196616 | tf_op jit(solution)/shard_map/ppermute | solution.py:280
  29.9 0.0 collective-permute-done.6.refs_1_
  29.9 1.3 %collective-permute-start.9 = (bf16[2,1,128,128]{3,2,1,0:T(8,128)(2,1)S(1)}, bf16[2,1,128,128]{3,2,1,0:T(8,128)(2,1)S(1)}, u32[]{:S(2)}, u32[]{:S(2)}) collective-permute-start(bf16[2,1,128,128]{3,2,1,0:T(8,128)(2,1)S(1)} %get-tuple-element.34), channel_id=1, source_target_pairs={{0,12},{4,0},{8,4},{12,8},{1,13},{5,1},{9,5},{13,9},{2,14},{6,2},{... | collective-permute-start | bytes 196616 | tf_op jit(solution)/shard_map/ppermute | solution.py:280
  31.2 4.5 %listed_queries.1 = f32[128,32,128]{2,1,0:T(8,128)} custom-call(s32[8,128]{1,0:T(8,128)S(1)} %get-tuple-element.21.places_ref, bf16[2,2,128,128]{3,2,1,0:T(8,128)(2,1)S(1)} %pack.1.refs_0_, bf16[2,2,128,128]{3,2,1,0:T(8,128)(2,1)S(1)} %collective-permute-done.refs_1_, bf16[2,2,128,128]{3,2,1,0:T(8,128)(2,1)S(1)} %collective-permute-done.1.refs_2_, ...), custom_call_target="tpu_custom_call" | custom-call | flops 805306368 | bytes 6291456 | tf_op jit(solution)/shard_map/listed_queries/pallas_call | solution.py:380
  35.8 0.0 collective-permute-done.7.refs_2_
  35.8 0.0 collective-permute-done.8.refs_3_
  35.8 0.0 collective-permute-done.10.refs_6_
  35.8 0.9 %collective-permute-done.11.refs_7_ = bf16[2,1,128,128]{3,2,1,0:T(8,128)(2,1)S(1)} collective-permute-done((bf16[2,1,128,128]{3,2,1,0:T(8,128)(2,1)S(1)}, bf16[2,1,128,128]{3,2,1,0:T(8,128)(2,1)S(1)}, u32[]{:S(2)}, u32[]{:S(2)}) %collective-permute-start.11) | collective-permute-done | bytes 65568 | tf_op jit(solution)/shard_map/ppermute | solution.py:280
  36.7 0.0 collective-permute-done.9.refs_5_
  36.7 0.8 %total.1 = (f32[128,2,128]{2,1,0:T(2,128)}, f32[128,2,128]{2,1,0:T(2,128)}) custom-call(f32[2,2,128,128]{3,2,1,0:T(8,128)S(1)} %get-tuple-element.26.refs_4_.refs_8_.near_ref, f32[2,1,128,128]{3,2,1,0:T(8,128)S(1)} %get-tuple-element.30.refs_0_, bf16[2,1,128,128]{3,2,1,0:T(8,128)(2,1)S(1)} %collective-permute-done.6.refs_1_, ...), custom_call_target="tpu_custom_call" | custom-call | tf_op jit(solution)/shard_map/total/pallas_call | solution.py:390
Async XLA Ops:
  1.9 13.1 %collective-permute-start = (bf16[2,2,128,128]{3,2,1,0:T(8,128)(2,1)S(1)}, bf16[2,2,128,128]{3,2,1,0:T(8,128)(2,1)S(1)}, u32[]{:S(2)}, u32[]{:S(2)}) collective-permute-start(bf16[2,2,128,128]{3,2,1,0:T(8,128)(2,1)S(1)} %pack.1.refs_0_), channel_id=1, source_target_pairs={{0,4},{4,8},{8,12},{12,0},{1,5},{5,9},{9,13},{13,1},{2,6},{6,10},{... | collective-permute-start | bytes 393224 | tf_op jit(solution)/shard_map/ppermute | solution.py:280
  5.0 11.2 %collective-permute-start.1 = (bf16[2,2,128,128]{3,2,1,0:T(8,128)(2,1)S(1)}, bf16[2,2,128,128]{3,2,1,0:T(8,128)(2,1)S(1)}, u32[]{:S(2)}, u32[]{:S(2)}) collective-permute-start(bf16[2,2,128,128]{3,2,1,0:T(8,128)(2,1)S(1)} %pack.1.refs_0_), channel_id=1, source_target_pairs={{0,8},{4,12},{8,0},{12,4},{1,9},{5,13},{9,1},{13,5},{2,10},{6,14},... | collective-permute-start | bytes 393224 | tf_op jit(solution)/shard_map/ppermute | solution.py:280
  7.5 8.6 %collective-permute-start.2 = (bf16[2,2,128,128]{3,2,1,0:T(8,128)(2,1)S(1)}, bf16[2,2,128,128]{3,2,1,0:T(8,128)(2,1)S(1)}, u32[]{:S(2)}, u32[]{:S(2)}) collective-permute-start(bf16[2,2,128,128]{3,2,1,0:T(8,128)(2,1)S(1)} %pack.1.refs_0_), channel_id=1, source_target_pairs={{0,12},{4,0},{8,4},{12,8},{1,13},{5,1},{9,5},{13,9},{2,14},{6,2},{... | collective-permute-start | bytes 393224 | tf_op jit(solution)/shard_map/ppermute | solution.py:280
  16.3 1.6 %collective-permute-start.3 = (bf16[2,2,2,128,128]{4,3,2,1,0:T(8,128)(2,1)S(1)}, bf16[2,2,2,128,128]{4,3,2,1,0:T(8,128)(2,1)S(1)}, u32[]{:S(2)}, u32[]{:S(2)}) collective-permute-start(bf16[2,2,2,128,128]{4,3,2,1,0:T(8,128)(2,1)S(1)} %choose.1), channel_id=1, source_target_pairs={{0,1},{1,0},{2,3},{3,2},{4,5},{5,4},{6,7},{7,6},{8,9},{9,8},{10,11... | collective-permute-start | bytes 786440 | tf_op jit(solution)/shard_map/ppermute | solution.py:283
  19.2 1.9 %collective-permute-start.5 = (bf16[2,2,1,128,128]{4,3,2,1,0:T(8,128)(2,1)S(1)}, bf16[2,2,1,128,128]{4,3,2,1,0:T(8,128)(2,1)S(1)}, u32[]{:S(2)}, u32[]{:S(2)}) collective-permute-start(bf16[2,2,1,128,128]{4,3,2,1,0:T(8,128)(2,1)S(1)} %listed_keys.2.refs_8_.mine_ref), channel_id=1, source_target_pairs={{0,1},{1,0},{2,3},{3,2},{4,5},{5,4},{6,7},{7,6},{8,9},{9,8},{10,11... | collective-permute-start | bytes 393224 | tf_op jit(solution)/shard_map/ppermute | solution.py:283
  20.7 6.4 %collective-permute-start.4 = (bf16[2,2,1,128,128]{4,3,2,1,0:T(8,128)(2,1)S(1)}, bf16[2,2,1,128,128]{4,3,2,1,0:T(8,128)(2,1)S(1)}, u32[]{:S(2)}, u32[]{:S(2)}) collective-permute-start(bf16[2,2,1,128,128]{4,3,2,1,0:T(8,128)(2,1)S(1)} %listed_keys.3.mine_ref), channel_id=1, source_target_pairs={{0,1},{1,0},{2,3},{3,2},{4,5},{5,4},{6,7},{7,6},{8,9},{9,8},{10,11... | collective-permute-start | bytes 393224 | tf_op jit(solution)/shard_map/ppermute | solution.py:283
  21.4 8.6 %collective-permute-start.6 = (bf16[2,1,128,128]{3,2,1,0:T(8,128)(2,1)S(1)}, bf16[2,1,128,128]{3,2,1,0:T(8,128)(2,1)S(1)}, u32[]{:S(2)}, u32[]{:S(2)}) collective-permute-start(bf16[2,1,128,128]{3,2,1,0:T(8,128)(2,1)S(1)} %get-tuple-element.31), channel_id=1, source_target_pairs={{0,4},{4,8},{8,12},{12,0},{1,5},{5,9},{9,13},{13,1},{2,6},{6,10},{... | collective-permute-start | bytes 196616 | tf_op jit(solution)/shard_map/ppermute | solution.py:280
  24.7 11.1 %collective-permute-start.7 = (bf16[2,1,128,128]{3,2,1,0:T(8,128)(2,1)S(1)}, bf16[2,1,128,128]{3,2,1,0:T(8,128)(2,1)S(1)}, u32[]{:S(2)}, u32[]{:S(2)}) collective-permute-start(bf16[2,1,128,128]{3,2,1,0:T(8,128)(2,1)S(1)} %get-tuple-element.32), channel_id=1, source_target_pairs={{0,8},{4,12},{8,0},{12,4},{1,9},{5,13},{9,1},{13,5},{2,10},{6,14},... | collective-permute-start | bytes 196616 | tf_op jit(solution)/shard_map/ppermute | solution.py:280
  26.3 9.4 %collective-permute-start.8 = (bf16[2,1,128,128]{3,2,1,0:T(8,128)(2,1)S(1)}, bf16[2,1,128,128]{3,2,1,0:T(8,128)(2,1)S(1)}, u32[]{:S(2)}, u32[]{:S(2)}) collective-permute-start(bf16[2,1,128,128]{3,2,1,0:T(8,128)(2,1)S(1)} %get-tuple-element.33), channel_id=1, source_target_pairs={{0,12},{4,0},{8,4},{12,8},{1,13},{5,1},{9,5},{13,9},{2,14},{6,2},{... | collective-permute-start | bytes 196616 | tf_op jit(solution)/shard_map/ppermute | solution.py:280
  27.4 8.4 %collective-permute-start.10 = (bf16[2,1,128,128]{3,2,1,0:T(8,128)(2,1)S(1)}, bf16[2,1,128,128]{3,2,1,0:T(8,128)(2,1)S(1)}, u32[]{:S(2)}, u32[]{:S(2)}) collective-permute-start(bf16[2,1,128,128]{3,2,1,0:T(8,128)(2,1)S(1)} %get-tuple-element.35), channel_id=1, source_target_pairs={{0,4},{4,8},{8,12},{12,0},{1,5},{5,9},{9,13},{13,1},{2,6},{6,10},{... | collective-permute-start | bytes 196616 | tf_op jit(solution)/shard_map/ppermute | solution.py:280
  28.6 8.1 %collective-permute-start.11 = (bf16[2,1,128,128]{3,2,1,0:T(8,128)(2,1)S(1)}, bf16[2,1,128,128]{3,2,1,0:T(8,128)(2,1)S(1)}, u32[]{:S(2)}, u32[]{:S(2)}) collective-permute-start(bf16[2,1,128,128]{3,2,1,0:T(8,128)(2,1)S(1)} %get-tuple-element.36), channel_id=1, source_target_pairs={{0,8},{4,12},{8,0},{12,4},{1,9},{5,13},{9,1},{13,5},{2,10},{6,14},... | collective-permute-start | bytes 196616 | tf_op jit(solution)/shard_map/ppermute | solution.py:280
  29.9 6.8 %collective-permute-start.9 = (bf16[2,1,128,128]{3,2,1,0:T(8,128)(2,1)S(1)}, bf16[2,1,128,128]{3,2,1,0:T(8,128)(2,1)S(1)}, u32[]{:S(2)}, u32[]{:S(2)}) collective-permute-start(bf16[2,1,128,128]{3,2,1,0:T(8,128)(2,1)S(1)} %get-tuple-element.34), channel_id=1, source_target_pairs={{0,12},{4,0},{8,4},{12,8},{1,13},{5,1},{9,5},{13,9},{2,14},{6,2},{... | collective-permute-start | bytes 196616 | tf_op jit(solution)/shard_map/ppermute | solution.py:280

commit v10 on v9

--- a/solution.py
+++ b/solution.py
@@ -10,7 +10,7 @@
 QH = 64
 KVH = 4
 LOG2E = 1.4426950408889634
-ROWS = 512
+ROWS = 1024
 PARTS = 2
 VMEM_LIMIT = 24 * 1024 * 1024
 

time: 37.8 us -> 37.8 us (level)
  waiting for transfers between devices: 3.62 us -> 5.5 us
  Pallas kernels: 15.8 us -> 14 us
    ppermute x9, waiting for transfers between devices: 2.1 us -> 3.98 us  [shifted(): lax.ppermute(array, 'ctx', [(i, (i + shift) % ring) for i in range(ring)])]
    pallas_call x1, Pallas kernels: 4.93 us -> 3.76 us  [body(): pl.pallas_call(functools.partial(local_kernel, factor, rows), in_specs=[V...]
    pallas_call x1, Pallas kernels: 4.52 us -> 3.8 us  [body(): pl.pallas_call(functools.partial(query_kernel, factor, rows), in_specs=[V...]
  transfers between devices with their start and end apart: 12 -> 12, of which waited for: 3 -> 3; matrix products, arithmetic and copies ran while one was open for 0% -> 0% of each run, Pallas kernels for 33% -> 28%
where the time goes in v10:
time: 37.8 us; the launch traced here: 37.6 us
  starting transfers between devices  17.4 us (46%)
  Pallas kernels  14 us (37%)
  waiting for transfers between devices  5.5 us (15%)
  between operations  0.7 us (2%)
    ppermute x9, starting transfers between devices, shifted(): lax.ppermute(array, 'ctx', [(i, (i + shift) % ring) for i in range(ring)])  16.7 us
    ppermute x9, waiting for transfers between devices, shifted(): lax.ppermute(array, 'ctx', [(i, (i + shift) % ring) for i in range(ring)])  3.98 us
    pallas_call x1, Pallas kernels, body(): pl.pallas_call(functools.partial(query_kernel, factor, rows), in_specs=[V...  3.8 us
    pallas_call x1, Pallas kernels, body(): pl.pallas_call(functools.partial(local_kernel, factor, rows), in_specs=[V...  3.76 us
    pallas_call x2, Pallas kernels, body(): pl.pallas_call(functools.partial(listed_kernel, factor, rows, part * each...  2.64 us
    ppermute x3, waiting for transfers between devices, swapped(): return lax.ppermute(array, 'sub', [(i, i ^ 1) for i in range(subs)])  1.53 us
    pallas_call x1, Pallas kernels, body(): pl.pallas_call(pack_kernel, in_specs=[HBM_SPEC] * 2, out_specs=VMEM_SPEC,...  1.24 us
    pallas_call x1, Pallas kernels, body(): pl.pallas_call(functools.partial(spread_kernel, grouped, ring, subs), in_...  1.18 us
  transfers between devices with their start and end apart: 12, of which 3 were waited for; matrix products, arithmetic and copies ran while one was open for 0% of the time, Pallas kernels for 28%

profile of v10, /device:TPU:0, one launch (start us, length us, event | category | flops | bytes accessed | tf_op | source)
XLA Modules:
  0.0 37.6 jit_solution(15034328532505606657)
XLA Ops:
  0.6 1.2 %pack.1.refs_0_ = bf16[2,2,128,128]{3,2,1,0:T(8,128)(2,1)S(1)} custom-call(bf16[128,2,128]{2,1,0:T(2,128)(2,1)} %key_ref.1, bf16[128,2,128]{2,1,0:T(2,128)(2,1)} %value_ref.1), custom_call_target="tpu_custom_call" | custom-call | tf_op jit(solution)/shard_map/pack/pallas_call | solution.py:289
  1.9 3.1 %collective-permute-start = (bf16[2,2,128,128]{3,2,1,0:T(8,128)(2,1)S(1)}, bf16[2,2,128,128]{3,2,1,0:T(8,128)(2,1)S(1)}, u32[]{:S(2)}, u32[]{:S(2)}) collective-permute-start(bf16[2,2,128,128]{3,2,1,0:T(8,128)(2,1)S(1)} %pack.1.refs_0_), channel_id=1, source_target_pairs={{0,4},{4,8},{8,12},{12,0},{1,5},{5,9},{9,13},{13,1},{2,6},{6,10},{... | collective-permute-start | bytes 393224 | tf_op jit(solution)/shard_map/ppermute | solution.py:280
  5.0 2.6 %collective-permute-start.1 = (bf16[2,2,128,128]{3,2,1,0:T(8,128)(2,1)S(1)}, bf16[2,2,128,128]{3,2,1,0:T(8,128)(2,1)S(1)}, u32[]{:S(2)}, u32[]{:S(2)}) collective-permute-start(bf16[2,2,128,128]{3,2,1,0:T(8,128)(2,1)S(1)} %pack.1.refs_0_), channel_id=1, source_target_pairs={{0,8},{4,12},{8,0},{12,4},{1,9},{5,13},{9,1},{13,5},{2,10},{6,14},... | collective-permute-start | bytes 393224 | tf_op jit(solution)/shard_map/ppermute | solution.py:280
  7.5 1.3 %collective-permute-start.2 = (bf16[2,2,128,128]{3,2,1,0:T(8,128)(2,1)S(1)}, bf16[2,2,128,128]{3,2,1,0:T(8,128)(2,1)S(1)}, u32[]{:S(2)}, u32[]{:S(2)}) collective-permute-start(bf16[2,2,128,128]{3,2,1,0:T(8,128)(2,1)S(1)} %pack.1.refs_0_), channel_id=1, source_target_pairs={{0,12},{4,0},{8,4},{12,8},{1,13},{5,1},{9,5},{13,9},{2,14},{6,2},{... | collective-permute-start | bytes 393224 | tf_op jit(solution)/shard_map/ppermute | solution.py:280
  8.9 1.2 %spread.1 = (f32[2,1,2048]{2,1,0:T(1,128)S(1)}, f32[2,1,2048]{2,1,0:T(1,128)S(1)}, f32[1,2048]{1,0:T(1,128)S(1)}, f32[128,128]{1,0:T(8,128)S(1)}, s32[8,128]{1,0:T(8,128)S(1)}) custom-call(f32[32,128]{1,0:T(8,128)} %bitcast.4, f32[32,128]{1,0:T(8,128)} %bitcast.5, s32[1,128]{1,0:T(1,128)} %bitcast.7, s32[2,8]{1,0:T(2,128)} %bitcast.6), custom_call_target="tpu_custom_call" | custom-call | tf_op jit(solution)/shard_map/spread/pallas_call | solution.py:300
  10.1 3.8 %local_block.1 = (f32[2,2,128,128]{3,2,1,0:T(8,128)S(1)}, f32[128,32,128]{2,1,0:T(8,128)S(1)}, bf16[2,2,128,16,128]{4,3,2,1,0:T(8,128)(2,1)S(1)}) custom-call(bf16[2,2,128,128]{3,2,1,0:T(8,128)(2,1)S(1)} %pack.1.refs_0_, bf16[128,32,128]{2,1,0:T(8,128)(2,1)} %refs_1_.1, bf16[128,32,128]{2,1,0:T(8,128)(2,1)} %refs_2_.1, ...), custom_call_target="tpu_custom_call" | custom-call | flops 671088640 | bytes 4194304 | tf_op jit(solution)/shard_map/local_block/pallas_call | solution.py:325
  13.8 0.0 collective-permute-done.refs_1_
  13.9 2.3 %collective-permute-done.1.refs_2_ = bf16[2,2,128,128]{3,2,1,0:T(8,128)(2,1)S(1)} collective-permute-done((bf16[2,2,128,128]{3,2,1,0:T(8,128)(2,1)S(1)}, bf16[2,2,128,128]{3,2,1,0:T(8,128)(2,1)S(1)}, u32[]{:S(2)}, u32[]{:S(2)}) %collective-permute-start.1) | collective-permute-done | bytes 131104 | tf_op jit(solution)/shard_map/ppermute | solution.py:280
  16.2 0.0 collective-permute-done.2.refs_3_
  16.2 0.1 choose.1
  16.3 0.1 collective-permute-start.3
  16.4 1.5 %collective-permute-done.3.refs_4_ = bf16[2,2,2,128,128]{4,3,2,1,0:T(8,128)(2,1)S(1)} collective-permute-done((bf16[2,2,2,128,128]{4,3,2,1,0:T(8,128)(2,1)S(1)}, bf16[2,2,2,128,128]{4,3,2,1,0:T(8,128)(2,1)S(1)}, u32[]{:S(2)}, u32[]{:S(2)}) %collective-permute-start.3) | collective-permute-done | bytes 262176 | tf_op jit(solution)/shard_map/ppermute | solution.py:283
  17.9 1.3 %listed_keys.2.refs_8_.mine_ref = bf16[2,2,1,128,128]{4,3,2,1,0:T(8,128)(2,1)S(1)} custom-call(s32[8,128]{1,0:T(8,128)S(1)} %get-tuple-element.21.places_ref, bf16[2,2,128,128]{3,2,1,0:T(8,128)(2,1)S(1)} %pack.1.refs_0_, bf16[2,2,128,128]{3,2,1,0:T(8,128)(2,1)S(1)} %collective-permute-done.refs_1_, ...), custom_call_target="tpu_custom_call" | custom-call | flops 536870912 | bytes 1048576 | tf_op jit(solution)/shard_map/listed_keys/pallas_call | solution.py:354
  19.2 0.2 collective-permute-start.5
  19.4 1.3 %listed_keys.3.mine_ref = bf16[2,2,1,128,128]{4,3,2,1,0:T(8,128)(2,1)S(1)} custom-call(s32[8,128]{1,0:T(8,128)S(1)} %get-tuple-element.21.places_ref, bf16[2,2,128,128]{3,2,1,0:T(8,128)(2,1)S(1)} %pack.1.refs_0_, bf16[2,2,128,128]{3,2,1,0:T(8,128)(2,1)S(1)} %collective-permute-done.refs_1_, bf16[2,2,128,128]{3,2,1,0:T(8,128)(2,1)S(1)} %collective-permute-done.1.refs_2_, ...), custom_call_target="tpu_custom_call" | custom-call | flops 536870912 | bytes 1048576 | tf_op jit(solution)/shard_map/listed_keys/pallas_call | solution.py:354
  20.8 0.4 %collective-permute-start.4 = (bf16[2,2,1,128,128]{4,3,2,1,0:T(8,128)(2,1)S(1)}, bf16[2,2,1,128,128]{4,3,2,1,0:T(8,128)(2,1)S(1)}, u32[]{:S(2)}, u32[]{:S(2)}) collective-permute-start(bf16[2,2,1,128,128]{4,3,2,1,0:T(8,128)(2,1)S(1)} %listed_keys.3.mine_ref), channel_id=1, source_target_pairs={{0,1},{1,0},{2,3},{3,2},{4,5},{5,4},{6,7},{7,6},{8,9},{9,8},{10,11... | collective-permute-start | bytes 393224 | tf_op jit(solution)/shard_map/ppermute | solution.py:283
  21.2 0.0 collective-permute-done.5.other_ref
  21.2 0.2 combine.3
  21.4 3.3 %collective-permute-start.6 = (bf16[2,1,128,128]{3,2,1,0:T(8,128)(2,1)S(1)}, bf16[2,1,128,128]{3,2,1,0:T(8,128)(2,1)S(1)}, u32[]{:S(2)}, u32[]{:S(2)}) collective-permute-start(bf16[2,1,128,128]{3,2,1,0:T(8,128)(2,1)S(1)} %get-tuple-element.31), channel_id=1, source_target_pairs={{0,4},{4,8},{8,12},{12,0},{1,5},{5,9},{9,13},{13,1},{2,6},{6,10},{... | collective-permute-start | bytes 196616 | tf_op jit(solution)/shard_map/ppermute | solution.py:280
  24.8 1.6 %collective-permute-start.7 = (bf16[2,1,128,128]{3,2,1,0:T(8,128)(2,1)S(1)}, bf16[2,1,128,128]{3,2,1,0:T(8,128)(2,1)S(1)}, u32[]{:S(2)}, u32[]{:S(2)}) collective-permute-start(bf16[2,1,128,128]{3,2,1,0:T(8,128)(2,1)S(1)} %get-tuple-element.32), channel_id=1, source_target_pairs={{0,8},{4,12},{8,0},{12,4},{1,9},{5,13},{9,1},{13,5},{2,10},{6,14},... | collective-permute-start | bytes 196616 | tf_op jit(solution)/shard_map/ppermute | solution.py:280
  26.4 0.8 %collective-permute-start.8 = (bf16[2,1,128,128]{3,2,1,0:T(8,128)(2,1)S(1)}, bf16[2,1,128,128]{3,2,1,0:T(8,128)(2,1)S(1)}, u32[]{:S(2)}, u32[]{:S(2)}) collective-permute-start(bf16[2,1,128,128]{3,2,1,0:T(8,128)(2,1)S(1)} %get-tuple-element.33), channel_id=1, source_target_pairs={{0,12},{4,0},{8,4},{12,8},{1,13},{5,1},{9,5},{13,9},{2,14},{6,2},{... | collective-permute-start | bytes 196616 | tf_op jit(solution)/shard_map/ppermute | solution.py:280
  27.2 0.0 collective-permute-done.4.other_ref
  27.2 0.2 combine.2
  27.4 1.3 %collective-permute-start.10 = (bf16[2,1,128,128]{3,2,1,0:T(8,128)(2,1)S(1)}, bf16[2,1,128,128]{3,2,1,0:T(8,128)(2,1)S(1)}, u32[]{:S(2)}, u32[]{:S(2)}) collective-permute-start(bf16[2,1,128,128]{3,2,1,0:T(8,128)(2,1)S(1)} %get-tuple-element.35), channel_id=1, source_target_pairs={{0,4},{4,8},{8,12},{12,0},{1,5},{5,9},{9,13},{13,1},{2,6},{6,10},{... | collective-permute-start | bytes 196616 | tf_op jit(solution)/shard_map/ppermute | solution.py:280
  28.7 1.3 %collective-permute-start.11 = (bf16[2,1,128,128]{3,2,1,0:T(8,128)(2,1)S(1)}, bf16[2,1,128,128]{3,2,1,0:T(8,128)(2,1)S(1)}, u32[]{:S(2)}, u32[]{:S(2)}) collective-permute-start(bf16[2,1,128,128]{3,2,1,0:T(8,128)(2,1)S(1)} %get-tuple-element.36), channel_id=1, source_target_pairs={{0,8},{4,12},{8,0},{12,4},{1,9},{5,13},{9,1},{13,5},{2,10},{6,14},... | collective-permute-start | bytes 196616 | tf_op jit(solution)/shard_map/ppermute | solution.py:280
  30.0 0.0 collective-permute-done.6.refs_1_
  30.0 1.3 %collective-permute-start.9 = (bf16[2,1,128,128]{3,2,1,0:T(8,128)(2,1)S(1)}, bf16[2,1,128,128]{3,2,1,0:T(8,128)(2,1)S(1)}, u32[]{:S(2)}, u32[]{:S(2)}) collective-permute-start(bf16[2,1,128,128]{3,2,1,0:T(8,128)(2,1)S(1)} %get-tuple-element.34), channel_id=1, source_target_pairs={{0,12},{4,0},{8,4},{12,8},{1,13},{5,1},{9,5},{13,9},{2,14},{6,2},{... | collective-permute-start | bytes 196616 | tf_op jit(solution)/shard_map/ppermute | solution.py:280
  31.3 3.8 %listed_queries.1 = f32[128,32,128]{2,1,0:T(8,128)} custom-call(s32[8,128]{1,0:T(8,128)S(1)} %get-tuple-element.21.places_ref, bf16[2,2,128,128]{3,2,1,0:T(8,128)(2,1)S(1)} %pack.1.refs_0_, bf16[2,2,128,128]{3,2,1,0:T(8,128)(2,1)S(1)} %collective-permute-done.refs_1_, bf16[2,2,128,128]{3,2,1,0:T(8,128)(2,1)S(1)} %collective-permute-done.1.refs_2_, ...), custom_call_target="tpu_custom_call" | custom-call | flops 805306368 | bytes 6291456 | tf_op jit(solution)/shard_map/listed_queries/pallas_call | solution.py:380
  35.1 0.0 collective-permute-done.7.refs_2_
  35.1 0.0 collective-permute-done.8.refs_3_
  35.1 0.0 collective-permute-done.10.refs_6_
  35.1 1.6 %collective-permute-done.11.refs_7_ = bf16[2,1,128,128]{3,2,1,0:T(8,128)(2,1)S(1)} collective-permute-done((bf16[2,1,128,128]{3,2,1,0:T(8,128)(2,1)S(1)}, bf16[2,1,128,128]{3,2,1,0:T(8,128)(2,1)S(1)}, u32[]{:S(2)}, u32[]{:S(2)}) %collective-permute-start.11) | collective-permute-done | bytes 65568 | tf_op jit(solution)/shard_map/ppermute | solution.py:280
  36.7 0.0 collective-permute-done.9.refs_5_
  36.7 0.8 %total.1 = (f32[128,2,128]{2,1,0:T(2,128)}, f32[128,2,128]{2,1,0:T(2,128)}) custom-call(f32[2,2,128,128]{3,2,1,0:T(8,128)S(1)} %get-tuple-element.26.refs_4_.refs_8_.near_ref, f32[2,1,128,128]{3,2,1,0:T(8,128)S(1)} %get-tuple-element.30.refs_0_, bf16[2,1,128,128]{3,2,1,0:T(8,128)(2,1)S(1)} %collective-permute-done.6.refs_1_, ...), custom_call_target="tpu_custom_call" | custom-call | tf_op jit(solution)/shard_map/total/pallas_call | solution.py:390
Async XLA Ops:
  1.9 12.0 %collective-permute-start = (bf16[2,2,128,128]{3,2,1,0:T(8,128)(2,1)S(1)}, bf16[2,2,128,128]{3,2,1,0:T(8,128)(2,1)S(1)}, u32[]{:S(2)}, u32[]{:S(2)}) collective-permute-start(bf16[2,2,128,128]{3,2,1,0:T(8,128)(2,1)S(1)} %pack.1.refs_0_), channel_id=1, source_target_pairs={{0,4},{4,8},{8,12},{12,0},{1,5},{5,9},{9,13},{13,1},{2,6},{6,10},{... | collective-permute-start | bytes 393224 | tf_op jit(solution)/shard_map/ppermute | solution.py:280
  5.0 11.2 %collective-permute-start.1 = (bf16[2,2,128,128]{3,2,1,0:T(8,128)(2,1)S(1)}, bf16[2,2,128,128]{3,2,1,0:T(8,128)(2,1)S(1)}, u32[]{:S(2)}, u32[]{:S(2)}) collective-permute-start(bf16[2,2,128,128]{3,2,1,0:T(8,128)(2,1)S(1)} %pack.1.refs_0_), channel_id=1, source_target_pairs={{0,8},{4,12},{8,0},{12,4},{1,9},{5,13},{9,1},{13,5},{2,10},{6,14},... | collective-permute-start | bytes 393224 | tf_op jit(solution)/shard_map/ppermute | solution.py:280
  7.5 8.6 %collective-permute-start.2 = (bf16[2,2,128,128]{3,2,1,0:T(8,128)(2,1)S(1)}, bf16[2,2,128,128]{3,2,1,0:T(8,128)(2,1)S(1)}, u32[]{:S(2)}, u32[]{:S(2)}) collective-permute-start(bf16[2,2,128,128]{3,2,1,0:T(8,128)(2,1)S(1)} %pack.1.refs_0_), channel_id=1, source_target_pairs={{0,12},{4,0},{8,4},{12,8},{1,13},{5,1},{9,5},{13,9},{2,14},{6,2},{... | collective-permute-start | bytes 393224 | tf_op jit(solution)/shard_map/ppermute | solution.py:280
  16.3 1.6 %collective-permute-start.3 = (bf16[2,2,2,128,128]{4,3,2,1,0:T(8,128)(2,1)S(1)}, bf16[2,2,2,128,128]{4,3,2,1,0:T(8,128)(2,1)S(1)}, u32[]{:S(2)}, u32[]{:S(2)}) collective-permute-start(bf16[2,2,2,128,128]{4,3,2,1,0:T(8,128)(2,1)S(1)} %choose.1), channel_id=1, source_target_pairs={{0,1},{1,0},{2,3},{3,2},{4,5},{5,4},{6,7},{7,6},{8,9},{9,8},{10,11... | collective-permute-start | bytes 786440 | tf_op jit(solution)/shard_map/ppermute | solution.py:283
  19.2 2.0 %collective-permute-start.5 = (bf16[2,2,1,128,128]{4,3,2,1,0:T(8,128)(2,1)S(1)}, bf16[2,2,1,128,128]{4,3,2,1,0:T(8,128)(2,1)S(1)}, u32[]{:S(2)}, u32[]{:S(2)}) collective-permute-start(bf16[2,2,1,128,128]{4,3,2,1,0:T(8,128)(2,1)S(1)} %listed_keys.2.refs_8_.mine_ref), channel_id=1, source_target_pairs={{0,1},{1,0},{2,3},{3,2},{4,5},{5,4},{6,7},{7,6},{8,9},{9,8},{10,11... | collective-permute-start | bytes 393224 | tf_op jit(solution)/shard_map/ppermute | solution.py:283
  20.8 6.4 %collective-permute-start.4 = (bf16[2,2,1,128,128]{4,3,2,1,0:T(8,128)(2,1)S(1)}, bf16[2,2,1,128,128]{4,3,2,1,0:T(8,128)(2,1)S(1)}, u32[]{:S(2)}, u32[]{:S(2)}) collective-permute-start(bf16[2,2,1,128,128]{4,3,2,1,0:T(8,128)(2,1)S(1)} %listed_keys.3.mine_ref), channel_id=1, source_target_pairs={{0,1},{1,0},{2,3},{3,2},{4,5},{5,4},{6,7},{7,6},{8,9},{9,8},{10,11... | collective-permute-start | bytes 393224 | tf_op jit(solution)/shard_map/ppermute | solution.py:283
  21.4 8.5 %collective-permute-start.6 = (bf16[2,1,128,128]{3,2,1,0:T(8,128)(2,1)S(1)}, bf16[2,1,128,128]{3,2,1,0:T(8,128)(2,1)S(1)}, u32[]{:S(2)}, u32[]{:S(2)}) collective-permute-start(bf16[2,1,128,128]{3,2,1,0:T(8,128)(2,1)S(1)} %get-tuple-element.31), channel_id=1, source_target_pairs={{0,4},{4,8},{8,12},{12,0},{1,5},{5,9},{9,13},{13,1},{2,6},{6,10},{... | collective-permute-start | bytes 196616 | tf_op jit(solution)/shard_map/ppermute | solution.py:280
  24.8 10.3 %collective-permute-start.7 = (bf16[2,1,128,128]{3,2,1,0:T(8,128)(2,1)S(1)}, bf16[2,1,128,128]{3,2,1,0:T(8,128)(2,1)S(1)}, u32[]{:S(2)}, u32[]{:S(2)}) collective-permute-start(bf16[2,1,128,128]{3,2,1,0:T(8,128)(2,1)S(1)} %get-tuple-element.32), channel_id=1, source_target_pairs={{0,8},{4,12},{8,0},{12,4},{1,9},{5,13},{9,1},{13,5},{2,10},{6,14},... | collective-permute-start | bytes 196616 | tf_op jit(solution)/shard_map/ppermute | solution.py:280
  26.4 8.7 %collective-permute-start.8 = (bf16[2,1,128,128]{3,2,1,0:T(8,128)(2,1)S(1)}, bf16[2,1,128,128]{3,2,1,0:T(8,128)(2,1)S(1)}, u32[]{:S(2)}, u32[]{:S(2)}) collective-permute-start(bf16[2,1,128,128]{3,2,1,0:T(8,128)(2,1)S(1)} %get-tuple-element.33), channel_id=1, source_target_pairs={{0,12},{4,0},{8,4},{12,8},{1,13},{5,1},{9,5},{13,9},{2,14},{6,2},{... | collective-permute-start | bytes 196616 | tf_op jit(solution)/shard_map/ppermute | solution.py:280
  27.4 7.7 %collective-permute-start.10 = (bf16[2,1,128,128]{3,2,1,0:T(8,128)(2,1)S(1)}, bf16[2,1,128,128]{3,2,1,0:T(8,128)(2,1)S(1)}, u32[]{:S(2)}, u32[]{:S(2)}) collective-permute-start(bf16[2,1,128,128]{3,2,1,0:T(8,128)(2,1)S(1)} %get-tuple-element.35), channel_id=1, source_target_pairs={{0,4},{4,8},{8,12},{12,0},{1,5},{5,9},{9,13},{13,1},{2,6},{6,10},{... | collective-permute-start | bytes 196616 | tf_op jit(solution)/shard_map/ppermute | solution.py:280
  28.7 8.1 %collective-permute-start.11 = (bf16[2,1,128,128]{3,2,1,0:T(8,128)(2,1)S(1)}, bf16[2,1,128,128]{3,2,1,0:T(8,128)(2,1)S(1)}, u32[]{:S(2)}, u32[]{:S(2)}) collective-permute-start(bf16[2,1,128,128]{3,2,1,0:T(8,128)(2,1)S(1)} %get-tuple-element.36), channel_id=1, source_target_pairs={{0,8},{4,12},{8,0},{12,4},{1,9},{5,13},{9,1},{13,5},{2,10},{6,14},... | collective-permute-start | bytes 196616 | tf_op jit(solution)/shard_map/ppermute | solution.py:280
  30.0 6.8 %collective-permute-start.9 = (bf16[2,1,128,128]{3,2,1,0:T(8,128)(2,1)S(1)}, bf16[2,1,128,128]{3,2,1,0:T(8,128)(2,1)S(1)}, u32[]{:S(2)}, u32[]{:S(2)}) collective-permute-start(bf16[2,1,128,128]{3,2,1,0:T(8,128)(2,1)S(1)} %get-tuple-element.34), channel_id=1, source_target_pairs={{0,12},{4,0},{8,4},{12,8},{1,13},{5,1},{9,5},{13,9},{2,14},{6,2},{... | collective-permute-start | bytes 196616 | tf_op jit(solution)/shard_map/ppermute | solution.py:280

commit v11 on v10

--- a/solution.py
+++ b/solution.py
@@ -10,7 +10,7 @@
 QH = 64
 KVH = 4
 LOG2E = 1.4426950408889634
-ROWS = 1024
+ROWS = 2048
 PARTS = 2
 VMEM_LIMIT = 24 * 1024 * 1024
 

time: 37.8 us -> 38 us (level)
  waiting for transfers between devices: 5.5 us -> 6.25 us
  Pallas kernels: 14 us -> 13.4 us
    ppermute x9, waiting for transfers between devices: 3.98 us -> 4.72 us  [shifted(): lax.ppermute(array, 'ctx', [(i, (i + shift) % ring) for i in range(ring)])]
    pallas_call x1, Pallas kernels: 3.76 us -> 3.12 us  [body(): pl.pallas_call(functools.partial(local_kernel, factor, rows), in_specs=[V...]
  transfers between devices with their start and end apart: 12 -> 12, of which waited for: 3 -> 3; matrix products, arithmetic and copies ran while one was open for 0% -> 0% of each run, Pallas kernels for 28% -> 26%
where the time goes in v11:
time: 38 us; the launch traced here: 37.7 us
  starting transfers between devices  17.4 us (46%)
  Pallas kernels  13.4 us (35%)
  waiting for transfers between devices  6.25 us (16%)
  between operations  0.7 us (2%)
    ppermute x9, starting transfers between devices, shifted(): lax.ppermute(array, 'ctx', [(i, (i + shift) % ring) for i in range(ring)])  16.6 us
    ppermute x9, waiting for transfers between devices, shifted(): lax.ppermute(array, 'ctx', [(i, (i + shift) % ring) for i in range(ring)])  4.72 us
    pallas_call x1, Pallas kernels, body(): pl.pallas_call(functools.partial(query_kernel, factor, rows), in_specs=[V...  3.7 us
    pallas_call x1, Pallas kernels, body(): pl.pallas_call(functools.partial(local_kernel, factor, rows), in_specs=[V...  3.12 us
    pallas_call x2, Pallas kernels, body(): pl.pallas_call(functools.partial(listed_kernel, factor, rows, part * each...  2.78 us
    ppermute x3, waiting for transfers between devices, swapped(): return lax.ppermute(array, 'sub', [(i, i ^ 1) for i in range(subs)])  1.53 us
    pallas_call x1, Pallas kernels, body(): pl.pallas_call(pack_kernel, in_specs=[HBM_SPEC] * 2, out_specs=VMEM_SPEC,...  1.24 us
    pallas_call x1, Pallas kernels, body(): pl.pallas_call(functools.partial(spread_kernel, grouped, ring, subs), in_...  1.18 us
  transfers between devices with their start and end apart: 12, of which 3 were waited for; matrix products, arithmetic and copies ran while one was open for 0% of the time, Pallas kernels for 26%

profile of v11, /device:TPU:0, one launch (start us, length us, event | category | flops | bytes accessed | tf_op | source)
XLA Modules:
  0.0 37.7 jit_solution(1019772016898221563)
XLA Ops:
  0.6 1.2 %pack.1.refs_0_ = bf16[2,2,128,128]{3,2,1,0:T(8,128)(2,1)S(1)} custom-call(bf16[128,2,128]{2,1,0:T(2,128)(2,1)} %key_ref.1, bf16[128,2,128]{2,1,0:T(2,128)(2,1)} %value_ref.1), custom_call_target="tpu_custom_call" | custom-call | tf_op jit(solution)/shard_map/pack/pallas_call | solution.py:289
  1.9 3.1 %collective-permute-start = (bf16[2,2,128,128]{3,2,1,0:T(8,128)(2,1)S(1)}, bf16[2,2,128,128]{3,2,1,0:T(8,128)(2,1)S(1)}, u32[]{:S(2)}, u32[]{:S(2)}) collective-permute-start(bf16[2,2,128,128]{3,2,1,0:T(8,128)(2,1)S(1)} %pack.1.refs_0_), channel_id=1, source_target_pairs={{0,4},{4,8},{8,12},{12,0},{1,5},{5,9},{9,13},{13,1},{2,6},{6,10},{... | collective-permute-start | bytes 393224 | tf_op jit(solution)/shard_map/ppermute | solution.py:280
  5.0 2.6 %collective-permute-start.1 = (bf16[2,2,128,128]{3,2,1,0:T(8,128)(2,1)S(1)}, bf16[2,2,128,128]{3,2,1,0:T(8,128)(2,1)S(1)}, u32[]{:S(2)}, u32[]{:S(2)}) collective-permute-start(bf16[2,2,128,128]{3,2,1,0:T(8,128)(2,1)S(1)} %pack.1.refs_0_), channel_id=1, source_target_pairs={{0,8},{4,12},{8,0},{12,4},{1,9},{5,13},{9,1},{13,5},{2,10},{6,14},... | collective-permute-start | bytes 393224 | tf_op jit(solution)/shard_map/ppermute | solution.py:280
  7.5 1.3 %collective-permute-start.2 = (bf16[2,2,128,128]{3,2,1,0:T(8,128)(2,1)S(1)}, bf16[2,2,128,128]{3,2,1,0:T(8,128)(2,1)S(1)}, u32[]{:S(2)}, u32[]{:S(2)}) collective-permute-start(bf16[2,2,128,128]{3,2,1,0:T(8,128)(2,1)S(1)} %pack.1.refs_0_), channel_id=1, source_target_pairs={{0,12},{4,0},{8,4},{12,8},{1,13},{5,1},{9,5},{13,9},{2,14},{6,2},{... | collective-permute-start | bytes 393224 | tf_op jit(solution)/shard_map/ppermute | solution.py:280
  8.9 1.2 %spread.1 = (f32[2,1,2048]{2,1,0:T(1,128)S(1)}, f32[2,1,2048]{2,1,0:T(1,128)S(1)}, f32[1,2048]{1,0:T(1,128)S(1)}, f32[128,128]{1,0:T(8,128)S(1)}, s32[8,128]{1,0:T(8,128)S(1)}) custom-call(f32[32,128]{1,0:T(8,128)} %bitcast.4, f32[32,128]{1,0:T(8,128)} %bitcast.5, s32[1,128]{1,0:T(1,128)} %bitcast.7, s32[2,8]{1,0:T(2,128)} %bitcast.6), custom_call_target="tpu_custom_call" | custom-call | tf_op jit(solution)/shard_map/spread/pallas_call | solution.py:300
  10.1 3.1 %local_block.1 = (f32[2,2,128,128]{3,2,1,0:T(8,128)S(1)}, f32[128,32,128]{2,1,0:T(8,128)S(1)}, bf16[2,2,128,16,128]{4,3,2,1,0:T(8,128)(2,1)S(1)}) custom-call(bf16[2,2,128,128]{3,2,1,0:T(8,128)(2,1)S(1)} %pack.1.refs_0_, bf16[128,32,128]{2,1,0:T(8,128)(2,1)} %refs_1_.1, bf16[128,32,128]{2,1,0:T(8,128)(2,1)} %refs_2_.1, ...), custom_call_target="tpu_custom_call" | custom-call | flops 671088640 | bytes 4194304 | tf_op jit(solution)/shard_map/local_block/pallas_call | solution.py:325
  13.2 0.0 collective-permute-done.refs_1_
  13.2 3.0 %collective-permute-done.1.refs_2_ = bf16[2,2,128,128]{3,2,1,0:T(8,128)(2,1)S(1)} collective-permute-done((bf16[2,2,128,128]{3,2,1,0:T(8,128)(2,1)S(1)}, bf16[2,2,128,128]{3,2,1,0:T(8,128)(2,1)S(1)}, u32[]{:S(2)}, u32[]{:S(2)}) %collective-permute-start.1) | collective-permute-done | bytes 131104 | tf_op jit(solution)/shard_map/ppermute | solution.py:280
  16.2 0.0 collective-permute-done.2.refs_3_
  16.2 0.1 choose.1
  16.3 0.1 collective-permute-start.3
  16.4 1.5 %collective-permute-done.3.refs_4_ = bf16[2,2,2,128,128]{4,3,2,1,0:T(8,128)(2,1)S(1)} collective-permute-done((bf16[2,2,2,128,128]{4,3,2,1,0:T(8,128)(2,1)S(1)}, bf16[2,2,2,128,128]{4,3,2,1,0:T(8,128)(2,1)S(1)}, u32[]{:S(2)}, u32[]{:S(2)}) %collective-permute-start.3) | collective-permute-done | bytes 262176 | tf_op jit(solution)/shard_map/ppermute | solution.py:283
  17.9 1.4 %listed_keys.2.refs_8_.mine_ref = bf16[2,2,1,128,128]{4,3,2,1,0:T(8,128)(2,1)S(1)} custom-call(s32[8,128]{1,0:T(8,128)S(1)} %get-tuple-element.21.places_ref, bf16[2,2,128,128]{3,2,1,0:T(8,128)(2,1)S(1)} %pack.1.refs_0_, bf16[2,2,128,128]{3,2,1,0:T(8,128)(2,1)S(1)} %collective-permute-done.refs_1_, ...), custom_call_target="tpu_custom_call" | custom-call | flops 536870912 | bytes 1048576 | tf_op jit(solution)/shard_map/listed_keys/pallas_call | solution.py:354
  19.3 0.2 collective-permute-start.5
  19.5 1.4 %listed_keys.3.mine_ref = bf16[2,2,1,128,128]{4,3,2,1,0:T(8,128)(2,1)S(1)} custom-call(s32[8,128]{1,0:T(8,128)S(1)} %get-tuple-element.21.places_ref, bf16[2,2,128,128]{3,2,1,0:T(8,128)(2,1)S(1)} %pack.1.refs_0_, bf16[2,2,128,128]{3,2,1,0:T(8,128)(2,1)S(1)} %collective-permute-done.refs_1_, bf16[2,2,128,128]{3,2,1,0:T(8,128)(2,1)S(1)} %collective-permute-done.1.refs_2_, ...), custom_call_target="tpu_custom_call" | custom-call | flops 536870912 | bytes 1048576 | tf_op jit(solution)/shard_map/listed_keys/pallas_call | solution.py:354
  20.9 0.4 %collective-permute-start.4 = (bf16[2,2,1,128,128]{4,3,2,1,0:T(8,128)(2,1)S(1)}, bf16[2,2,1,128,128]{4,3,2,1,0:T(8,128)(2,1)S(1)}, u32[]{:S(2)}, u32[]{:S(2)}) collective-permute-start(bf16[2,2,1,128,128]{4,3,2,1,0:T(8,128)(2,1)S(1)} %listed_keys.3.mine_ref), channel_id=1, source_target_pairs={{0,1},{1,0},{2,3},{3,2},{4,5},{5,4},{6,7},{7,6},{8,9},{9,8},{10,11... | collective-permute-start | bytes 393224 | tf_op jit(solution)/shard_map/ppermute | solution.py:283
  21.4 0.0 collective-permute-done.5.other_ref
  21.4 0.2 combine.3
  21.6 3.3 %collective-permute-start.6 = (bf16[2,1,128,128]{3,2,1,0:T(8,128)(2,1)S(1)}, bf16[2,1,128,128]{3,2,1,0:T(8,128)(2,1)S(1)}, u32[]{:S(2)}, u32[]{:S(2)}) collective-permute-start(bf16[2,1,128,128]{3,2,1,0:T(8,128)(2,1)S(1)} %get-tuple-element.31), channel_id=1, source_target_pairs={{0,4},{4,8},{8,12},{12,0},{1,5},{5,9},{9,13},{13,1},{2,6},{6,10},{... | collective-permute-start | bytes 196616 | tf_op jit(solution)/shard_map/ppermute | solution.py:280
  24.9 1.6 %collective-permute-start.7 = (bf16[2,1,128,128]{3,2,1,0:T(8,128)(2,1)S(1)}, bf16[2,1,128,128]{3,2,1,0:T(8,128)(2,1)S(1)}, u32[]{:S(2)}, u32[]{:S(2)}) collective-permute-start(bf16[2,1,128,128]{3,2,1,0:T(8,128)(2,1)S(1)} %get-tuple-element.32), channel_id=1, source_target_pairs={{0,8},{4,12},{8,0},{12,4},{1,9},{5,13},{9,1},{13,5},{2,10},{6,14},... | collective-permute-start | bytes 196616 | tf_op jit(solution)/shard_map/ppermute | solution.py:280
  26.5 0.8 %collective-permute-start.8 = (bf16[2,1,128,128]{3,2,1,0:T(8,128)(2,1)S(1)}, bf16[2,1,128,128]{3,2,1,0:T(8,128)(2,1)S(1)}, u32[]{:S(2)}, u32[]{:S(2)}) collective-permute-start(bf16[2,1,128,128]{3,2,1,0:T(8,128)(2,1)S(1)} %get-tuple-element.33), channel_id=1, source_target_pairs={{0,12},{4,0},{8,4},{12,8},{1,13},{5,1},{9,5},{13,9},{2,14},{6,2},{... | collective-permute-start | bytes 196616 | tf_op jit(solution)/shard_map/ppermute | solution.py:280
  27.3 0.0 collective-permute-done.4.other_ref
  27.3 0.2 combine.2
  27.5 1.3 %collective-permute-start.10 = (bf16[2,1,128,128]{3,2,1,0:T(8,128)(2,1)S(1)}, bf16[2,1,128,128]{3,2,1,0:T(8,128)(2,1)S(1)}, u32[]{:S(2)}, u32[]{:S(2)}) collective-permute-start(bf16[2,1,128,128]{3,2,1,0:T(8,128)(2,1)S(1)} %get-tuple-element.35), channel_id=1, source_target_pairs={{0,4},{4,8},{8,12},{12,0},{1,5},{5,9},{9,13},{13,1},{2,6},{6,10},{... | collective-permute-start | bytes 196616 | tf_op jit(solution)/shard_map/ppermute | solution.py:280
  28.8 1.3 %collective-permute-start.11 = (bf16[2,1,128,128]{3,2,1,0:T(8,128)(2,1)S(1)}, bf16[2,1,128,128]{3,2,1,0:T(8,128)(2,1)S(1)}, u32[]{:S(2)}, u32[]{:S(2)}) collective-permute-start(bf16[2,1,128,128]{3,2,1,0:T(8,128)(2,1)S(1)} %get-tuple-element.36), channel_id=1, source_target_pairs={{0,8},{4,12},{8,0},{12,4},{1,9},{5,13},{9,1},{13,5},{2,10},{6,14},... | collective-permute-start | bytes 196616 | tf_op jit(solution)/shard_map/ppermute | solution.py:280
  30.1 0.0 collective-permute-done.6.refs_1_
  30.1 1.3 %collective-permute-start.9 = (bf16[2,1,128,128]{3,2,1,0:T(8,128)(2,1)S(1)}, bf16[2,1,128,128]{3,2,1,0:T(8,128)(2,1)S(1)}, u32[]{:S(2)}, u32[]{:S(2)}) collective-permute-start(bf16[2,1,128,128]{3,2,1,0:T(8,128)(2,1)S(1)} %get-tuple-element.34), channel_id=1, source_target_pairs={{0,12},{4,0},{8,4},{12,8},{1,13},{5,1},{9,5},{13,9},{2,14},{6,2},{... | collective-permute-start | bytes 196616 | tf_op jit(solution)/shard_map/ppermute | solution.py:280
  31.4 3.7 %listed_queries.1 = f32[128,32,128]{2,1,0:T(8,128)} custom-call(s32[8,128]{1,0:T(8,128)S(1)} %get-tuple-element.21.places_ref, bf16[2,2,128,128]{3,2,1,0:T(8,128)(2,1)S(1)} %pack.1.refs_0_, bf16[2,2,128,128]{3,2,1,0:T(8,128)(2,1)S(1)} %collective-permute-done.refs_1_, bf16[2,2,128,128]{3,2,1,0:T(8,128)(2,1)S(1)} %collective-permute-done.1.refs_2_, ...), custom_call_target="tpu_custom_call" | custom-call | flops 805306368 | bytes 6291456 | tf_op jit(solution)/shard_map/listed_queries/pallas_call | solution.py:380
  35.1 0.0 collective-permute-done.7.refs_2_
  35.1 0.0 collective-permute-done.8.refs_3_
  35.1 0.0 collective-permute-done.10.refs_6_
  35.1 1.7 %collective-permute-done.11.refs_7_ = bf16[2,1,128,128]{3,2,1,0:T(8,128)(2,1)S(1)} collective-permute-done((bf16[2,1,128,128]{3,2,1,0:T(8,128)(2,1)S(1)}, bf16[2,1,128,128]{3,2,1,0:T(8,128)(2,1)S(1)}, u32[]{:S(2)}, u32[]{:S(2)}) %collective-permute-start.11) | collective-permute-done | bytes 65568 | tf_op jit(solution)/shard_map/ppermute | solution.py:280
  36.9 0.0 collective-permute-done.9.refs_5_
  36.9 0.8 %total.1 = (f32[128,2,128]{2,1,0:T(2,128)}, f32[128,2,128]{2,1,0:T(2,128)}) custom-call(f32[2,2,128,128]{3,2,1,0:T(8,128)S(1)} %get-tuple-element.26.refs_4_.refs_8_.near_ref, f32[2,1,128,128]{3,2,1,0:T(8,128)S(1)} %get-tuple-element.30.refs_0_, bf16[2,1,128,128]{3,2,1,0:T(8,128)(2,1)S(1)} %collective-permute-done.6.refs_1_, ...), custom_call_target="tpu_custom_call" | custom-call | tf_op jit(solution)/shard_map/total/pallas_call | solution.py:390
Async XLA Ops:
  1.9 11.3 %collective-permute-start = (bf16[2,2,128,128]{3,2,1,0:T(8,128)(2,1)S(1)}, bf16[2,2,128,128]{3,2,1,0:T(8,128)(2,1)S(1)}, u32[]{:S(2)}, u32[]{:S(2)}) collective-permute-start(bf16[2,2,128,128]{3,2,1,0:T(8,128)(2,1)S(1)} %pack.1.refs_0_), channel_id=1, source_target_pairs={{0,4},{4,8},{8,12},{12,0},{1,5},{5,9},{9,13},{13,1},{2,6},{6,10},{... | collective-permute-start | bytes 393224 | tf_op jit(solution)/shard_map/ppermute | solution.py:280
  5.0 11.2 %collective-permute-start.1 = (bf16[2,2,128,128]{3,2,1,0:T(8,128)(2,1)S(1)}, bf16[2,2,128,128]{3,2,1,0:T(8,128)(2,1)S(1)}, u32[]{:S(2)}, u32[]{:S(2)}) collective-permute-start(bf16[2,2,128,128]{3,2,1,0:T(8,128)(2,1)S(1)} %pack.1.refs_0_), channel_id=1, source_target_pairs={{0,8},{4,12},{8,0},{12,4},{1,9},{5,13},{9,1},{13,5},{2,10},{6,14},... | collective-permute-start | bytes 393224 | tf_op jit(solution)/shard_map/ppermute | solution.py:280
  7.5 8.6 %collective-permute-start.2 = (bf16[2,2,128,128]{3,2,1,0:T(8,128)(2,1)S(1)}, bf16[2,2,128,128]{3,2,1,0:T(8,128)(2,1)S(1)}, u32[]{:S(2)}, u32[]{:S(2)}) collective-permute-start(bf16[2,2,128,128]{3,2,1,0:T(8,128)(2,1)S(1)} %pack.1.refs_0_), channel_id=1, source_target_pairs={{0,12},{4,0},{8,4},{12,8},{1,13},{5,1},{9,5},{13,9},{2,14},{6,2},{... | collective-permute-start | bytes 393224 | tf_op jit(solution)/shard_map/ppermute | solution.py:280
  16.3 1.6 %collective-permute-start.3 = (bf16[2,2,2,128,128]{4,3,2,1,0:T(8,128)(2,1)S(1)}, bf16[2,2,2,128,128]{4,3,2,1,0:T(8,128)(2,1)S(1)}, u32[]{:S(2)}, u32[]{:S(2)}) collective-permute-start(bf16[2,2,2,128,128]{4,3,2,1,0:T(8,128)(2,1)S(1)} %choose.1), channel_id=1, source_target_pairs={{0,1},{1,0},{2,3},{3,2},{4,5},{5,4},{6,7},{7,6},{8,9},{9,8},{10,11... | collective-permute-start | bytes 786440 | tf_op jit(solution)/shard_map/ppermute | solution.py:283
  19.3 2.0 %collective-permute-start.5 = (bf16[2,2,1,128,128]{4,3,2,1,0:T(8,128)(2,1)S(1)}, bf16[2,2,1,128,128]{4,3,2,1,0:T(8,128)(2,1)S(1)}, u32[]{:S(2)}, u32[]{:S(2)}) collective-permute-start(bf16[2,2,1,128,128]{4,3,2,1,0:T(8,128)(2,1)S(1)} %listed_keys.2.refs_8_.mine_ref), channel_id=1, source_target_pairs={{0,1},{1,0},{2,3},{3,2},{4,5},{5,4},{6,7},{7,6},{8,9},{9,8},{10,11... | collective-permute-start | bytes 393224 | tf_op jit(solution)/shard_map/ppermute | solution.py:283
  20.9 6.4 %collective-permute-start.4 = (bf16[2,2,1,128,128]{4,3,2,1,0:T(8,128)(2,1)S(1)}, bf16[2,2,1,128,128]{4,3,2,1,0:T(8,128)(2,1)S(1)}, u32[]{:S(2)}, u32[]{:S(2)}) collective-permute-start(bf16[2,2,1,128,128]{4,3,2,1,0:T(8,128)(2,1)S(1)} %listed_keys.3.mine_ref), channel_id=1, source_target_pairs={{0,1},{1,0},{2,3},{3,2},{4,5},{5,4},{6,7},{7,6},{8,9},{9,8},{10,11... | collective-permute-start | bytes 393224 | tf_op jit(solution)/shard_map/ppermute | solution.py:283
  21.6 8.5 %collective-permute-start.6 = (bf16[2,1,128,128]{3,2,1,0:T(8,128)(2,1)S(1)}, bf16[2,1,128,128]{3,2,1,0:T(8,128)(2,1)S(1)}, u32[]{:S(2)}, u32[]{:S(2)}) collective-permute-start(bf16[2,1,128,128]{3,2,1,0:T(8,128)(2,1)S(1)} %get-tuple-element.31), channel_id=1, source_target_pairs={{0,4},{4,8},{8,12},{12,0},{1,5},{5,9},{9,13},{13,1},{2,6},{6,10},{... | collective-permute-start | bytes 196616 | tf_op jit(solution)/shard_map/ppermute | solution.py:280
  24.9 10.2 %collective-permute-start.7 = (bf16[2,1,128,128]{3,2,1,0:T(8,128)(2,1)S(1)}, bf16[2,1,128,128]{3,2,1,0:T(8,128)(2,1)S(1)}, u32[]{:S(2)}, u32[]{:S(2)}) collective-permute-start(bf16[2,1,128,128]{3,2,1,0:T(8,128)(2,1)S(1)} %get-tuple-element.32), channel_id=1, source_target_pairs={{0,8},{4,12},{8,0},{12,4},{1,9},{5,13},{9,1},{13,5},{2,10},{6,14},... | collective-permute-start | bytes 196616 | tf_op jit(solution)/shard_map/ppermute | solution.py:280
  26.5 8.6 %collective-permute-start.8 = (bf16[2,1,128,128]{3,2,1,0:T(8,128)(2,1)S(1)}, bf16[2,1,128,128]{3,2,1,0:T(8,128)(2,1)S(1)}, u32[]{:S(2)}, u32[]{:S(2)}) collective-permute-start(bf16[2,1,128,128]{3,2,1,0:T(8,128)(2,1)S(1)} %get-tuple-element.33), channel_id=1, source_target_pairs={{0,12},{4,0},{8,4},{12,8},{1,13},{5,1},{9,5},{13,9},{2,14},{6,2},{... | collective-permute-start | bytes 196616 | tf_op jit(solution)/shard_map/ppermute | solution.py:280
  27.5 7.6 %collective-permute-start.10 = (bf16[2,1,128,128]{3,2,1,0:T(8,128)(2,1)S(1)}, bf16[2,1,128,128]{3,2,1,0:T(8,128)(2,1)S(1)}, u32[]{:S(2)}, u32[]{:S(2)}) collective-permute-start(bf16[2,1,128,128]{3,2,1,0:T(8,128)(2,1)S(1)} %get-tuple-element.35), channel_id=1, source_target_pairs={{0,4},{4,8},{8,12},{12,0},{1,5},{5,9},{9,13},{13,1},{2,6},{6,10},{... | collective-permute-start | bytes 196616 | tf_op jit(solution)/shard_map/ppermute | solution.py:280
  28.8 8.1 %collective-permute-start.11 = (bf16[2,1,128,128]{3,2,1,0:T(8,128)(2,1)S(1)}, bf16[2,1,128,128]{3,2,1,0:T(8,128)(2,1)S(1)}, u32[]{:S(2)}, u32[]{:S(2)}) collective-permute-start(bf16[2,1,128,128]{3,2,1,0:T(8,128)(2,1)S(1)} %get-tuple-element.36), channel_id=1, source_target_pairs={{0,8},{4,12},{8,0},{12,4},{1,9},{5,13},{9,1},{13,5},{2,10},{6,14},... | collective-permute-start | bytes 196616 | tf_op jit(solution)/shard_map/ppermute | solution.py:280
  30.1 6.8 %collective-permute-start.9 = (bf16[2,1,128,128]{3,2,1,0:T(8,128)(2,1)S(1)}, bf16[2,1,128,128]{3,2,1,0:T(8,128)(2,1)S(1)}, u32[]{:S(2)}, u32[]{:S(2)}) collective-permute-start(bf16[2,1,128,128]{3,2,1,0:T(8,128)(2,1)S(1)} %get-tuple-element.34), channel_id=1, source_target_pairs={{0,12},{4,0},{8,4},{12,8},{1,13},{5,1},{9,5},{13,9},{2,14},{6,2},{... | collective-permute-start | bytes 196616 | tf_op jit(solution)/shard_map/ppermute | solution.py:280

commit v12 on v10

--- a/solution.py
+++ b/solution.py
@@ -11,7 +11,7 @@
 KVH = 4
 LOG2E = 1.4426950408889634
 ROWS = 1024
-PARTS = 2
+PARTS = 1
 VMEM_LIMIT = 24 * 1024 * 1024
 
 VMEM_SPEC = pl.BlockSpec(memory_space=pltpu.VMEM)

time: 37.8 us -> 37.9 us (level); the launches traced: 37.6 us -> 37.2 us
  starting transfers between devices: 17.4 us -> 13 us
  waiting for transfers between devices: 5.5 us -> 9.6 us
    ppermute x9 -> x6, starting transfers between devices: 16.7 us -> 12.8 us  [shifted(): lax.ppermute(array, 'ctx', [(i, (i + shift) % ring) for i in range(ring)])]
    ppermute x9 -> x6, waiting for transfers between devices: 3.98 us -> 6.67 us  [shifted(): lax.ppermute(array, 'ctx', [(i, (i + shift) % ring) for i in range(ring)])]
    ppermute x3 -> x2, waiting for transfers between devices: 1.53 us -> 2.93 us  [swapped(): return lax.ppermute(array, 'sub', [(i, i ^ 1) for i in range(subs)])]
    ppermute x3 -> x2, starting transfers between devices: 0.71 us -> 0.27 us  [swapped(): return lax.ppermute(array, 'sub', [(i, i ^ 1) for i in range(subs)])]
    pallas_call x2 -> x1, Pallas kernels: 2.64 us -> 2.51 us  [body(): pl.pallas_call(functools.partial(listed_kernel, factor, rows, part * each...]
  transfers between devices with their start and end apart: 12 -> 8, of which waited for: 3 -> 4; matrix products, arithmetic and copies ran while one was open for 0% -> 0% of each run, Pallas kernels for 28% -> 24%
where the time goes in v12:
time: 37.9 us; the launch traced here: 37.2 us
  Pallas kernels  13.9 us (37%)
  starting transfers between devices  13 us (34%)
  waiting for transfers between devices  9.6 us (25%)
  between operations  0.69 us (2%)
    ppermute x6, starting transfers between devices, shifted(): lax.ppermute(array, 'ctx', [(i, (i + shift) % ring) for i in range(ring)])  12.8 us
    ppermute x6, waiting for transfers between devices, shifted(): lax.ppermute(array, 'ctx', [(i, (i + shift) % ring) for i in range(ring)])  6.67 us
    pallas_call x1, Pallas kernels, body(): pl.pallas_call(functools.partial(query_kernel, factor, rows), in_specs=[V...  3.8 us
    pallas_call x1, Pallas kernels, body(): pl.pallas_call(functools.partial(local_kernel, factor, rows), in_specs=[V...  3.77 us
    ppermute x2, waiting for transfers between devices, swapped(): return lax.ppermute(array, 'sub', [(i, i ^ 1) for i in range(subs)])  2.93 us
    pallas_call x1, Pallas kernels, body(): pl.pallas_call(functools.partial(listed_kernel, factor, rows, part * each...  2.51 us
    pallas_call x1, Pallas kernels, body(): pl.pallas_call(pack_kernel, in_specs=[HBM_SPEC] * 2, out_specs=VMEM_SPEC,...  1.24 us
    pallas_call x1, Pallas kernels, body(): pl.pallas_call(functools.partial(spread_kernel, grouped, ring, subs), in_...  1.18 us
  transfers between devices with their start and end apart: 8, of which 4 were waited for; matrix products, arithmetic and copies ran while one was open for 0% of the time, Pallas kernels for 24%

profile of v12, /device:TPU:0, one launch (start us, length us, event | category | flops | bytes accessed | tf_op | source)
XLA Modules:
  0.0 37.2 jit_solution(14476621265515415489)
XLA Ops:
  0.6 1.2 %pack.1.refs_0_ = bf16[2,2,128,128]{3,2,1,0:T(8,128)(2,1)S(1)} custom-call(bf16[128,2,128]{2,1,0:T(2,128)(2,1)} %key_ref.1, bf16[128,2,128]{2,1,0:T(2,128)(2,1)} %value_ref.1), custom_call_target="tpu_custom_call" | custom-call | tf_op jit(solution)/shard_map/pack/pallas_call | solution.py:289
  1.9 3.1 %collective-permute-start = (bf16[2,2,128,128]{3,2,1,0:T(8,128)(2,1)S(1)}, bf16[2,2,128,128]{3,2,1,0:T(8,128)(2,1)S(1)}, u32[]{:S(2)}, u32[]{:S(2)}) collective-permute-start(bf16[2,2,128,128]{3,2,1,0:T(8,128)(2,1)S(1)} %pack.1.refs_0_), channel_id=1, source_target_pairs={{0,4},{4,8},{8,12},{12,0},{1,5},{5,9},{9,13},{13,1},{2,6},{6,10},{... | collective-permute-start | bytes 393224 | tf_op jit(solution)/shard_map/ppermute | solution.py:280
  5.0 2.6 %collective-permute-start.1 = (bf16[2,2,128,128]{3,2,1,0:T(8,128)(2,1)S(1)}, bf16[2,2,128,128]{3,2,1,0:T(8,128)(2,1)S(1)}, u32[]{:S(2)}, u32[]{:S(2)}) collective-permute-start(bf16[2,2,128,128]{3,2,1,0:T(8,128)(2,1)S(1)} %pack.1.refs_0_), channel_id=1, source_target_pairs={{0,8},{4,12},{8,0},{12,4},{1,9},{5,13},{9,1},{13,5},{2,10},{6,14},... | collective-permute-start | bytes 393224 | tf_op jit(solution)/shard_map/ppermute | solution.py:280
  7.5 1.3 %collective-permute-start.2 = (bf16[2,2,128,128]{3,2,1,0:T(8,128)(2,1)S(1)}, bf16[2,2,128,128]{3,2,1,0:T(8,128)(2,1)S(1)}, u32[]{:S(2)}, u32[]{:S(2)}) collective-permute-start(bf16[2,2,128,128]{3,2,1,0:T(8,128)(2,1)S(1)} %pack.1.refs_0_), channel_id=1, source_target_pairs={{0,12},{4,0},{8,4},{12,8},{1,13},{5,1},{9,5},{13,9},{2,14},{6,2},{... | collective-permute-start | bytes 393224 | tf_op jit(solution)/shard_map/ppermute | solution.py:280
  8.9 1.2 %spread.1 = (f32[2,1,2048]{2,1,0:T(1,128)S(1)}, f32[2,1,2048]{2,1,0:T(1,128)S(1)}, f32[1,2048]{1,0:T(1,128)S(1)}, f32[128,128]{1,0:T(8,128)S(1)}, s32[8,128]{1,0:T(8,128)S(1)}) custom-call(f32[32,128]{1,0:T(8,128)} %bitcast.4, f32[32,128]{1,0:T(8,128)} %bitcast.5, s32[1,128]{1,0:T(1,128)} %bitcast.7, s32[2,8]{1,0:T(2,128)} %bitcast.6), custom_call_target="tpu_custom_call" | custom-call | tf_op jit(solution)/shard_map/spread/pallas_call | solution.py:300
  10.1 3.8 %local_block.1 = (f32[2,2,128,128]{3,2,1,0:T(8,128)S(1)}, f32[128,32,128]{2,1,0:T(8,128)S(1)}, bf16[2,2,128,16,128]{4,3,2,1,0:T(8,128)(2,1)S(1)}) custom-call(bf16[2,2,128,128]{3,2,1,0:T(8,128)(2,1)S(1)} %pack.1.refs_0_, bf16[128,32,128]{2,1,0:T(8,128)(2,1)} %refs_1_.1, bf16[128,32,128]{2,1,0:T(8,128)(2,1)} %refs_2_.1, ...), custom_call_target="tpu_custom_call" | custom-call | flops 671088640 | bytes 4194304 | tf_op jit(solution)/shard_map/local_block/pallas_call | solution.py:325
  13.8 0.0 collective-permute-done.refs_1_
  13.9 2.3 %collective-permute-done.1.refs_2_ = bf16[2,2,128,128]{3,2,1,0:T(8,128)(2,1)S(1)} collective-permute-done((bf16[2,2,128,128]{3,2,1,0:T(8,128)(2,1)S(1)}, bf16[2,2,128,128]{3,2,1,0:T(8,128)(2,1)S(1)}, u32[]{:S(2)}, u32[]{:S(2)}) %collective-permute-start.1) | collective-permute-done | bytes 131104 | tf_op jit(solution)/shard_map/ppermute | solution.py:280
  16.2 0.0 collective-permute-done.2.refs_3_
  16.2 0.1 choose.1
  16.3 0.1 collective-permute-start.3
  16.4 1.5 %collective-permute-done.3.refs_4_ = bf16[2,2,2,128,128]{4,3,2,1,0:T(8,128)(2,1)S(1)} collective-permute-done((bf16[2,2,2,128,128]{4,3,2,1,0:T(8,128)(2,1)S(1)}, bf16[2,2,2,128,128]{4,3,2,1,0:T(8,128)(2,1)S(1)}, u32[]{:S(2)}, u32[]{:S(2)}) %collective-permute-start.3) | collective-permute-done | bytes 262176 | tf_op jit(solution)/shard_map/ppermute | solution.py:283
  17.9 2.5 %listed_keys.1.mine_ref = bf16[2,2,2,128,128]{4,3,2,1,0:T(8,128)(2,1)S(1)} custom-call(s32[8,128]{1,0:T(8,128)S(1)} %get-tuple-element.17.places_ref, bf16[2,2,128,128]{3,2,1,0:T(8,128)(2,1)S(1)} %pack.1.refs_0_, bf16[2,2,128,128]{3,2,1,0:T(8,128)(2,1)S(1)} %collective-permute-done.refs_1_, bf16[2,2,128,128]{3,2,1,0:T(8,128)(2,1)S(1)} %collective-permute-done.1.refs_2_, ...), custom_call_target="tpu_custom_call" | custom-call | flops 1073741824 | bytes 2097152 | tf_op jit(solution)/shard_map/listed_keys/pallas_call | solution.py:354
  20.4 0.2 collective-permute-start.4
  20.6 1.4 %collective-permute-done.4.other_ref = bf16[2,2,2,128,128]{4,3,2,1,0:T(8,128)(2,1)S(1)} collective-permute-done((bf16[2,2,2,128,128]{4,3,2,1,0:T(8,128)(2,1)S(1)}, bf16[2,2,2,128,128]{4,3,2,1,0:T(8,128)(2,1)S(1)}, u32[]{:S(2)}, u32[]{:S(2)}) %collective-permute-start.4) | collective-permute-done | bytes 262176 | tf_op jit(solution)/shard_map/ppermute | solution.py:283
  22.0 0.4 %combine.1 = (f32[2,2,128,128]{3,2,1,0:T(8,128)S(1)}, bf16[2,2,128,128]{3,2,1,0:T(8,128)(2,1)S(1)}, bf16[2,2,128,128]{3,2,1,0:T(8,128)(2,1)S(1)}, bf16[2,2,128,128]{3,2,1,0:T(8,128)(2,1)S(1)}) custom-call(s32[8,128]{1,0:T(8,128)S(1)} %get-tuple-element.17.places_ref, bf16[2,2,2,128,128]{4,3,2,1,0:T(8,128)(2,1)S(1)} %listed_keys.1.mine_ref, ...), custom_call_target="tpu_custom_call" | custom-call | tf_op jit(solution)/shard_map/combine/pallas_call | solution.py:367
  22.4 3.3 %collective-permute-start.5 = (bf16[2,2,128,128]{3,2,1,0:T(8,128)(2,1)S(1)}, bf16[2,2,128,128]{3,2,1,0:T(8,128)(2,1)S(1)}, u32[]{:S(2)}, u32[]{:S(2)}) collective-permute-start(bf16[2,2,128,128]{3,2,1,0:T(8,128)(2,1)S(1)} %get-tuple-element.26), channel_id=1, source_target_pairs={{0,4},{4,8},{8,12},{12,0},{1,5},{5,9},{9,13},{13,1},{2,6},{6,10},{... | collective-permute-start | bytes 393224 | tf_op jit(solution)/shard_map/ppermute | solution.py:280
  25.8 1.6 %collective-permute-start.6 = (bf16[2,2,128,128]{3,2,1,0:T(8,128)(2,1)S(1)}, bf16[2,2,128,128]{3,2,1,0:T(8,128)(2,1)S(1)}, u32[]{:S(2)}, u32[]{:S(2)}) collective-permute-start(bf16[2,2,128,128]{3,2,1,0:T(8,128)(2,1)S(1)} %get-tuple-element.27), channel_id=1, source_target_pairs={{0,8},{4,12},{8,0},{12,4},{1,9},{5,13},{9,1},{13,5},{2,10},{6,14},... | collective-permute-start | bytes 393224 | tf_op jit(solution)/shard_map/ppermute | solution.py:280
  27.4 0.8 %collective-permute-start.7 = (bf16[2,2,128,128]{3,2,1,0:T(8,128)(2,1)S(1)}, bf16[2,2,128,128]{3,2,1,0:T(8,128)(2,1)S(1)}, u32[]{:S(2)}, u32[]{:S(2)}) collective-permute-start(bf16[2,2,128,128]{3,2,1,0:T(8,128)(2,1)S(1)} %get-tuple-element.28), channel_id=1, source_target_pairs={{0,12},{4,0},{8,4},{12,8},{1,13},{5,1},{9,5},{13,9},{2,14},{6,2},{... | collective-permute-start | bytes 393224 | tf_op jit(solution)/shard_map/ppermute | solution.py:280
  28.2 3.8 %listed_queries.1 = f32[128,32,128]{2,1,0:T(8,128)} custom-call(s32[8,128]{1,0:T(8,128)S(1)} %get-tuple-element.17.places_ref, bf16[2,2,128,128]{3,2,1,0:T(8,128)(2,1)S(1)} %pack.1.refs_0_, bf16[2,2,128,128]{3,2,1,0:T(8,128)(2,1)S(1)} %collective-permute-done.refs_1_, bf16[2,2,128,128]{3,2,1,0:T(8,128)(2,1)S(1)} %collective-permute-done.1.refs_2_, ...), custom_call_target="tpu_custom_call" | custom-call | flops 805306368 | bytes 6291456 | tf_op jit(solution)/shard_map/listed_queries/pallas_call | solution.py:380
  32.0 0.0 collective-permute-done.5.refs_1_
  32.0 4.3 %collective-permute-done.6.refs_2_ = bf16[2,2,128,128]{3,2,1,0:T(8,128)(2,1)S(1)} collective-permute-done((bf16[2,2,128,128]{3,2,1,0:T(8,128)(2,1)S(1)}, bf16[2,2,128,128]{3,2,1,0:T(8,128)(2,1)S(1)}, u32[]{:S(2)}, u32[]{:S(2)}) %collective-permute-start.6) | collective-permute-done | bytes 131104 | tf_op jit(solution)/shard_map/ppermute | solution.py:280
  36.4 0.0 collective-permute-done.7.refs_3_
  36.4 0.8 %total.1 = (f32[128,2,128]{2,1,0:T(2,128)}, f32[128,2,128]{2,1,0:T(2,128)}) custom-call(f32[2,2,128,128]{3,2,1,0:T(8,128)S(1)} %get-tuple-element.22.refs_4_.refs_8_.near_ref, f32[2,2,128,128]{3,2,1,0:T(8,128)S(1)} %get-tuple-element.25.refs_9_.refs_0_, bf16[2,2,128,128]{3,2,1,0:T(8,128)(2,1)S(1)} %collective-permute-done.5.refs_1_, ...), custom_call_target="tpu_custom_call" | custom-call | tf_op jit(solution)/shard_map/total/pallas_call | solution.py:390
Async XLA Ops:
  1.9 12.0 %collective-permute-start = (bf16[2,2,128,128]{3,2,1,0:T(8,128)(2,1)S(1)}, bf16[2,2,128,128]{3,2,1,0:T(8,128)(2,1)S(1)}, u32[]{:S(2)}, u32[]{:S(2)}) collective-permute-start(bf16[2,2,128,128]{3,2,1,0:T(8,128)(2,1)S(1)} %pack.1.refs_0_), channel_id=1, source_target_pairs={{0,4},{4,8},{8,12},{12,0},{1,5},{5,9},{9,13},{13,1},{2,6},{6,10},{... | collective-permute-start | bytes 393224 | tf_op jit(solution)/shard_map/ppermute | solution.py:280
  5.0 11.2 %collective-permute-start.1 = (bf16[2,2,128,128]{3,2,1,0:T(8,128)(2,1)S(1)}, bf16[2,2,128,128]{3,2,1,0:T(8,128)(2,1)S(1)}, u32[]{:S(2)}, u32[]{:S(2)}) collective-permute-start(bf16[2,2,128,128]{3,2,1,0:T(8,128)(2,1)S(1)} %pack.1.refs_0_), channel_id=1, source_target_pairs={{0,8},{4,12},{8,0},{12,4},{1,9},{5,13},{9,1},{13,5},{2,10},{6,14},... | collective-permute-start | bytes 393224 | tf_op jit(solution)/shard_map/ppermute | solution.py:280
  7.5 8.6 %collective-permute-start.2 = (bf16[2,2,128,128]{3,2,1,0:T(8,128)(2,1)S(1)}, bf16[2,2,128,128]{3,2,1,0:T(8,128)(2,1)S(1)}, u32[]{:S(2)}, u32[]{:S(2)}) collective-permute-start(bf16[2,2,128,128]{3,2,1,0:T(8,128)(2,1)S(1)} %pack.1.refs_0_), channel_id=1, source_target_pairs={{0,12},{4,0},{8,4},{12,8},{1,13},{5,1},{9,5},{13,9},{2,14},{6,2},{... | collective-permute-start | bytes 393224 | tf_op jit(solution)/shard_map/ppermute | solution.py:280
  16.3 1.6 %collective-permute-start.3 = (bf16[2,2,2,128,128]{4,3,2,1,0:T(8,128)(2,1)S(1)}, bf16[2,2,2,128,128]{4,3,2,1,0:T(8,128)(2,1)S(1)}, u32[]{:S(2)}, u32[]{:S(2)}) collective-permute-start(bf16[2,2,2,128,128]{4,3,2,1,0:T(8,128)(2,1)S(1)} %choose.1), channel_id=1, source_target_pairs={{0,1},{1,0},{2,3},{3,2},{4,5},{5,4},{6,7},{7,6},{8,9},{9,8},{10,11... | collective-permute-start | bytes 786440 | tf_op jit(solution)/shard_map/ppermute | solution.py:283
  20.4 1.6 %collective-permute-start.4 = (bf16[2,2,2,128,128]{4,3,2,1,0:T(8,128)(2,1)S(1)}, bf16[2,2,2,128,128]{4,3,2,1,0:T(8,128)(2,1)S(1)}, u32[]{:S(2)}, u32[]{:S(2)}) collective-permute-start(bf16[2,2,2,128,128]{4,3,2,1,0:T(8,128)(2,1)S(1)} %listed_keys.1.mine_ref), channel_id=1, source_target_pairs={{0,1},{1,0},{2,3},{3,2},{4,5},{5,4},{6,7},{7,6},{8,9},{9,8},{10,11... | collective-permute-start | bytes 786440 | tf_op jit(solution)/shard_map/ppermute | solution.py:283
  22.4 9.6 %collective-permute-start.5 = (bf16[2,2,128,128]{3,2,1,0:T(8,128)(2,1)S(1)}, bf16[2,2,128,128]{3,2,1,0:T(8,128)(2,1)S(1)}, u32[]{:S(2)}, u32[]{:S(2)}) collective-permute-start(bf16[2,2,128,128]{3,2,1,0:T(8,128)(2,1)S(1)} %get-tuple-element.26), channel_id=1, source_target_pairs={{0,4},{4,8},{8,12},{12,0},{1,5},{5,9},{9,13},{13,1},{2,6},{6,10},{... | collective-permute-start | bytes 393224 | tf_op jit(solution)/shard_map/ppermute | solution.py:280
  25.8 10.6 %collective-permute-start.6 = (bf16[2,2,128,128]{3,2,1,0:T(8,128)(2,1)S(1)}, bf16[2,2,128,128]{3,2,1,0:T(8,128)(2,1)S(1)}, u32[]{:S(2)}, u32[]{:S(2)}) collective-permute-start(bf16[2,2,128,128]{3,2,1,0:T(8,128)(2,1)S(1)} %get-tuple-element.27), channel_id=1, source_target_pairs={{0,8},{4,12},{8,0},{12,4},{1,9},{5,13},{9,1},{13,5},{2,10},{6,14},... | collective-permute-start | bytes 393224 | tf_op jit(solution)/shard_map/ppermute | solution.py:280
  27.4 8.9 %collective-permute-start.7 = (bf16[2,2,128,128]{3,2,1,0:T(8,128)(2,1)S(1)}, bf16[2,2,128,128]{3,2,1,0:T(8,128)(2,1)S(1)}, u32[]{:S(2)}, u32[]{:S(2)}) collective-permute-start(bf16[2,2,128,128]{3,2,1,0:T(8,128)(2,1)S(1)} %get-tuple-element.28), channel_id=1, source_target_pairs={{0,12},{4,0},{8,4},{12,8},{1,13},{5,1},{9,5},{13,9},{2,14},{6,2},{... | collective-permute-start | bytes 393224 | tf_op jit(solution)/shard_map/ppermute | solution.py:280
